TPU v7x, 32 devices: a whole 2x2x4 slice. The times are simulated.
32 devices in a mesh: depth: 2 (over core), lx: 4 (over y, x), ly: 4 (over z).
Axes of the slice: x: 2, y: 2, z: 4, core: 2. Of those that a mesh axis runs over, the one named last changes fastest.
Arguments:
- iterate: float32 [32, 4, 32, 512], P('depth', None, 'lx', 'ly'), may hold values from -3 to 3
- right_side: float32 [32, 4, 32, 512], P('depth', None, 'lx', 'ly'), may hold values from -64 to 64
- storage: float32 [32, 32, 512], P('depth', 'lx', 'ly'), may hold values from 0.02 to 0.2
- zones: int32 [32, 32, 512], P('depth', 'lx', 'ly'), may hold values from 0 to 7
- counts: int32 [32, 512], P('lx', 'ly'), may hold values from 8 to 32
- materials: float32 [2, 8, 4, 4], replicated, as said below
Outputs:
- updated: float32 [32, 4, 32, 512], P('depth', None, 'lx', 'ly')
- coarse: float32 [16, 4, 32, 512], P('depth', None, 'lx', 'ly')
Inputs may be any that keep to these rules, and one draw needn't show every extreme that they name: Nodes of column (x, y) with depth index below counts[x, y] are active. Each materials[t, k] is a symmetric matrix whose diagonal entries are positive and each larger than the sum of the magnitudes of the other entries in its row.
All inputs are finite; a program needn't handle non-finite values.
Results may differ from a plain program's by a relative error of at most 0.0003.
Values sent between devices are 32-bit elements; how exact they have to be, the bound alone decides.
No kernel may reach another device: no remote copies, remote signals or barrier semaphores. Data moves between devices by JAX's collectives and lax.ppermute only.
A program may use at most 64 MiB of HBM per device.

v0:
```python
import functools

import jax
import jax.numpy as jnp
from jax import lax
from jax.experimental import pallas as pl
from jax.experimental.pallas import tpu as pltpu
from jax.sharding import PartitionSpec as P

PAIRS = [(i, j) for i in range(4) for j in range(i, 4)]
AT = {}
for _k, (_i, _j) in enumerate(PAIRS):
    AT[_i, _j] = AT[_j, _i] = _k

ROWS, LANES = 8, 128
SUMMED = 19
LINE = 24
F32 = jnp.float32
VMEM_LIMIT = 48 * 1024 * 1024


def row_index():
    return lax.broadcasted_iota(jnp.int32, (ROWS, LANES), 0)


def lane_index():
    return lax.broadcasted_iota(jnp.int32, (ROWS, LANES), 1)


def roll_rows(x, by):
    return pltpu.roll(x, by % x.shape[0], 0)


def roll_lanes(x, by):
    return pltpu.roll(x, by % LANES if isinstance(by, int) else lax.rem(by + LANES, LANES), 1)


def activity(codes):
    return jnp.where(codes > 0, 1.0, 0.0).astype(F32)


def lookup(tables, kind, codes, act):
    rows = jnp.maximum(codes - 1, 0)
    found = []
    for i, j in PAIRS:
        table = tables[kind * 16 + 4 * i + j]
        parts = [
            jnp.take_along_axis(table, rows[at : at + ROWS], axis=0, mode="promise_in_bounds")
            for at in range(0, rows.shape[0], ROWS)
        ]
        value = parts[0] if len(parts) == 1 else jnp.concatenate(parts, axis=0)
        found.append(value * act)
    return found


def apply_sym(matrix, vector):
    out = []
    for i in range(4):
        total = matrix[AT[i, 0]] * vector[0]
        for j in range(1, 4):
            total = total + matrix[AT[i, j]] * vector[j]
        out.append(total)
    return out


def summed_fields(tables, codes, field):
    act = activity(codes)
    lateral = lookup(tables, 0, codes, act)
    return [act] + lateral + [act * v for v in field] + apply_sym(lateral, field)


def level_of(side, n, levels):
    return side * (levels - 1) + (1 - 2 * side) * n


def pack_kernel(levels, iterate, right, storage, zones, counts, met, xm, ym, dm, codes_out):
    side = lax.axis_index("depth")
    lane = lane_index()
    counts_v = counts[...]
    xm[...] = jnp.zeros(xm.shape, F32)
    acc = [jnp.zeros((ROWS, LANES), F32) for _ in range(10)]
    for n in range(levels + 2):
        if n < levels:
            z = level_of(side, n, levels)
            code = jnp.where(z + side * levels < counts_v, zones[z] + 1, 0)
            fields = [code.astype(F32)] + [iterate[z, c] for c in range(4)]
            fields += [right[z, c] for c in range(4)] + [storage[z]]
        elif n == levels:
            fields = [met[4]] + [met[c] for c in range(4)]
            code = met[4].astype(jnp.int32)
        else:
            fields = [met[5]]
            code = met[5].astype(jnp.int32)
        codes_out[n] = code
        for k, value in enumerate(fields):
            xm[k, n : n + 1, :] = value[0:1]
            if k < 5:
                xm[10 + k, n : n + 1, :] = value[1:2]
            acc[k] = jnp.where(lane // 2 == n, roll_lanes(value, 2 * n), acc[k])
    for k in range(10):
        ym[k] = acc[k]
        dm[k] = acc[k][0:2]


def own_kernel(levels, iterate, codes, met, tables, out, u):
    side = lax.axis_index("depth")
    for k in range(SUMMED):
        u[0, k] = jnp.zeros((ROWS, LANES), F32)

    def fill(n, carry):
        z = level_of(side, n, levels)
        for k, value in enumerate(summed_fields(tables, codes[n], [iterate[z, c] for c in range(4)])):
            u[n + 1, k] = value
        return carry

    lax.fori_loop(0, levels, fill, 0)
    for k, value in enumerate(summed_fields(tables, codes[levels], [met[c] for c in range(4)])):
        u[levels + 1, k] = value

    def add(n, carry):
        for k in range(SUMMED):
            out[n, k] = u[n + 1, k] + 0.5 * (u[n, k] + u[n + 2, k])
        return carry

    lax.fori_loop(0, levels, add, 0)


def invert(m):
    d = lambda i, j: m[AT[i, j]]

    def small(a, b, c):
        ia = 1.0 / a
        l = b * ia
        ic = 1.0 / (c - l * b)
        lc = l * ic
        return ia + l * lc, -lc, ic

    a00, a01, a11 = small(d(0, 0), d(0, 1), d(1, 1))
    t00 = d(2, 0) * a00 + d(2, 1) * a01
    t01 = d(2, 0) * a01 + d(2, 1) * a11
    t10 = d(3, 0) * a00 + d(3, 1) * a01
    t11 = d(3, 0) * a01 + d(3, 1) * a11
    s00 = d(2, 2) - (t00 * d(2, 0) + t01 * d(2, 1))
    s01 = d(3, 2) - (t10 * d(2, 0) + t11 * d(2, 1))
    s11 = d(3, 3) - (t10 * d(3, 0) + t11 * d(3, 1))
    i22, i32, i33 = small(s00, s01, s11)
    u00 = i22 * t00 + i32 * t10
    u01 = i22 * t01 + i32 * t11
    u10 = i32 * t00 + i33 * t10
    u11 = i32 * t01 + i33 * t11
    i00 = a00 + (t00 * u00 + t10 * u10)
    i01 = a01 + (t00 * u01 + t10 * u11)
    i11 = a11 + (t01 * u01 + t11 * u11)
    return [i00, i01, -u00, -u10, i11, -u01, -u11, i22, i32, i33]


def sym_product(left, right):
    return [
        [
            (left[AT[i, 0]] * right[AT[0, j]] + left[AT[i, 1]] * right[AT[1, j]])
            + (left[AT[i, 2]] * right[AT[2, j]] + left[AT[i, 3]] * right[AT[3, j]])
            for j in range(4)
        ]
        for i in range(4)
    ]


def line_sum(values):
    return values + 0.5 * (roll_rows(values, 1) + roll_rows(values, -1))


def lane_sum(values):
    return values + 0.5 * (roll_lanes(values, 2) + roll_lanes(values, -2))


def widen(two_rows):
    return jnp.concatenate([two_rows, jnp.zeros((ROWS - 2, LANES), F32)], axis=0)


def sweep_kernel(
    levels, own, xm, ym, dm, iterate, right, storage, codes, met, tables,
    gains, rests, message, ends, codes_s,
    xw, yv, ys, fs, rs, ss, ps, ms, qs,
):
    side = lax.axis_index("depth")
    last_x = lax.axis_index("lx") == lax.axis_size("lx") - 1
    last_y = lax.axis_index("ly") == lax.axis_size("ly") - 1
    row, lane = row_index(), lane_index()
    wl = jnp.where(last_x & (row == 7), 0.0, 0.5).astype(F32)
    wu = jnp.where(last_x & (row == 6), 0.0, 0.5).astype(F32)
    vl = jnp.where(last_y & (lane == 127), 0.0, 0.5).astype(F32)
    vu = vl
    top = row == 7
    end = lane == 127
    start = lane == 0

    for r in range(2):
        line_codes = xm[10 * r].astype(jnp.int32)
        line_field = [xm[10 * r + 1 + c] for c in range(4)]
        for k, value in enumerate(summed_fields(tables, line_codes, line_field)):
            at = (2 * k + r) * LINE
            xw[at : at + LINE, :] = line_sum(value)

    corner = [widen(dm[k]) for k in range(10)]
    side_codes = ym[0].astype(jnp.int32)
    corner_codes = corner[0].astype(jnp.int32)
    side_u = summed_fields(tables, side_codes, [ym[1 + c] for c in range(4)])
    corner_u = summed_fields(tables, corner_codes, corner[1:5])
    for k in range(SUMMED):
        w0 = lane_sum(side_u[k])
        wd = lane_sum(corner_u[k])
        w1 = roll_rows(jnp.where(row < 1, wd, w0), -1)
        w2 = roll_rows(jnp.where(row < 2, wd, w0), -2)
        g = wl * w0 + wu * w2
        b = w1 + g
        h = g + 0.5 * roll_lanes(b, -1)
        yv[k] = jnp.where(lane % 2 == 0, b, roll_lanes(h, -1))
    for k in range(10):
        ys[k] = roll_rows(jnp.where(row < 1, corner[k], ym[k]), -1)

    def shift(value, k, n):
        up = jnp.where(top, xm[k, pl.ds(n, 1), :], roll_rows(value, -1))
        return jnp.where(end, roll_lanes(ys[k], 127 - 2 * n), roll_lanes(up, -1))

    def shift_level(n, carry):
        z = level_of(side, n, levels)
        codes_s[n] = shift(codes[n].astype(F32), 0, n).astype(jnp.int32)
        for c in range(4):
            fs[n + 1, c] = shift(iterate[z, c], 1 + c, n)
            rs[n, c] = shift(right[z, c], 5 + c, n)
        ss[n] = shift(storage[z], 9, n)
        return carry

    lax.fori_loop(0, levels, shift_level, 0)
    codes_s[levels] = shift(met[4], 0, levels).astype(jnp.int32)
    codes_s[levels + 1] = shift(met[5], 0, levels + 1).astype(jnp.int32)
    for c in range(4):
        fs[0, c] = jnp.zeros((ROWS, LANES), F32)
        fs[levels + 1, c] = shift(met[c], 1 + c, levels)
    for k in range(10):
        ms[0, k] = jnp.zeros((ROWS, LANES), F32)

    def assemble(n, carry):
        sums = []
        for k in range(SUMMED):
            w = own[n, k]
            beyond = xw[pl.ds(2 * k * LINE + n, ROWS, stride=LINE), :]
            w1 = roll_rows(jnp.where(row < 1, beyond, w), -1)
            w2 = roll_rows(jnp.where(row < 2, beyond, w), -2)
            g = wl * w + wu * w2
            b = w1 + g
            v = roll_lanes(yv[k], -2 * n)
            h = g + vu * roll_lanes(jnp.where(start, v, b), -1)
            sums.append(jnp.where(end, v, roll_lanes(h, -1)) + vl * b)
        act = activity(codes_s[n])
        act_next = activity(codes_s[n + 1])
        lateral = lookup(tables, 0, codes_s[n], act)
        here = lookup(tables, 1, codes_s[n], 0.5 * act * act_next)
        there = lookup(tables, 1, codes_s[n + 1], 0.5 * act * act_next)
        half = 0.5 * act
        below = [ms[n, k] for k in range(10)]
        above = [here[k] + there[k] for k in range(10)]
        half_sum = 0.5 * sums[0]
        block = []
        for k, (i, j) in enumerate(PAIRS):
            value = (lateral[k] * half_sum + half * sums[1 + k]) + (below[k] + above[k])
            block.append(value + ss[n] if i == j else value)
        for k in range(10):
            ms[n + 1, k] = above[k]
            ps[n, k] = block[k]
        field = [fs[n + 1, c] for c in range(4)]
        before = apply_sym(below, [fs[n, c] for c in range(4)])
        after = apply_sym(above, [fs[n + 2, c] for c in range(4)])
        diagonal = apply_sym(block, field)
        flow = apply_sym(lateral, sums[11:15])
        for c in range(4):
            around = (before[c] + after[c]) + (0.5 * flow[c] + half * sums[15 + c])
            qs[n, c] = act * (rs[n, c] - (diagonal[c] - around))
        return carry

    lax.fori_loop(0, levels, assemble, 0)

    def eliminate(n, carry):
        coupled, carried = carry
        block = [ps[n, k] - coupled[k] for k in range(10)]
        value = [qs[n, c] + carried[c] for c in range(4)]
        link = [ms[n + 1, k] for k in range(10)]
        inverse = invert(block)
        gain = sym_product(inverse, link)
        rest = apply_sym(inverse, value)
        for i in range(4):
            rests[n, i] = rest[i]
            for j in range(4):
                gains[n, 4 * i + j] = gain[i][j]
        new_coupled = []
        for i, j in PAIRS:
            new_coupled.append(
                (link[AT[i, 0]] * gain[0][j] + link[AT[i, 1]] * gain[1][j])
                + (link[AT[i, 2]] * gain[2][j] + link[AT[i, 3]] * gain[3][j])
            )
        return new_coupled, apply_sym(link, rest), block, value

    zeros = [jnp.zeros((ROWS, LANES), F32) for _ in range(10)]
    coupled, carried = lax.fori_loop(
        0, levels - 1, lambda n, c: eliminate(n, c)[:2], (zeros, zeros[:4])
    )
    coupled, carried, block, value = eliminate(levels - 1, (coupled, carried))
    for k in range(10):
        message[k] = coupled[k]
        ends[k] = block[k]
    for c in range(4):
        message[10 + c] = carried[c]
        ends[10 + c] = value[c]
    for at, n in ((14, levels - 1), (34, levels - 2)):
        for k in range(16):
            message[at + k] = gains[n, k]
        for c in range(4):
            message[at + 16 + c] = rests[n, c]


def back_kernel(levels, gains, rests, ends, got, codes_s, tables, xs, kx, x3, y3, d3):
    lane = lane_index()

    def carry_on(gain, rest, x):
        out = []
        for i in range(4):
            out.append(
                rest[i] + ((gain[4 * i] * x[0] + gain[4 * i + 1] * x[1])
                           + (gain[4 * i + 2] * x[2] + gain[4 * i + 3] * x[3]))
            )
        return out

    block = [ends[k] - got[k] for k in range(10)]
    value = [ends[10 + c] + got[10 + c] for c in range(4)]
    x = apply_sym(invert(block), value)
    x_met = carry_on([got[14 + k] for k in range(16)], [got[30 + c] for c in range(4)], x)
    x_far = carry_on([got[34 + k] for k in range(16)], [got[50 + c] for c in range(4)], x_met)
    for c in range(4):
        xs[levels - 1, c] = x[c]
        xs[levels, c] = x_met[c]
        xs[levels + 1, c] = x_far[c]

    def retreat(step, x):
        n = levels - 2 - step
        x = carry_on([gains[n, k] for k in range(16)], [rests[n, c] for c in range(4)], x)
        for c in range(4):
            xs[n, c] = x[c]
        return x

    lax.fori_loop(0, levels - 1, retreat, x)

    x3[...] = jnp.zeros(x3.shape, F32)
    acc = [jnp.zeros((ROWS, LANES), F32) for _ in range(8)]
    for n in range(levels + 2):
        field = [xs[n, c] for c in range(4)]
        act = activity(codes_s[n])
        flow = apply_sym(lookup(tables, 0, codes_s[n], act), field)
        for c in range(4):
            kx[n, c] = flow[c]
        for k, value in enumerate(field + flow):
            x3[2 * k, n : n + 1, :] = value[6:7]
            x3[2 * k + 1, n : n + 1, :] = value[7:8]
            acc[k] = jnp.where(lane // 2 == n, roll_lanes(value, 2 * n + 2), acc[k])
    for k in range(8):
        y3[k] = acc[k]
        d3[k] = acc[k][6:8]


def finish_kernel(
    levels, xs, kx, x3, y3, d3, iterate, codes, tables, updated, coarse, xw, yv, ys, sm
):
    side = lax.axis_index("depth")
    first_x = lax.axis_index("lx") == 0
    first_y = lax.axis_index("ly") == 0
    last_x = lax.axis_index("lx") == lax.axis_size("lx") - 1
    last_y = lax.axis_index("ly") == lax.axis_size("ly") - 1
    row, lane = row_index(), lane_index()
    wl = jnp.where(first_x & (row == 0), 0.0, 0.5).astype(F32)
    wu = jnp.where(last_x & (row == 7), 0.0, 0.5).astype(F32)
    vu = jnp.where(last_y & (lane == 127), 0.0, 0.5).astype(F32)
    vl = jnp.where(first_y, 0.0, 0.5).astype(F32)
    end = lane == 127
    start = lane == 0

    for k in range(8):
        for r in range(2):
            at = (2 * k + r) * LINE
            xw[at : at + LINE, :] = line_sum(x3[2 * k + r])
        corner = widen(d3[k])
        w2 = lane_sum(y3[k])
        wd = lane_sum(corner)
        w0 = jnp.where(row < 2, wd, roll_rows(w2, 2))
        w1 = jnp.where(row < 1, roll_rows(wd, -1), roll_rows(w2, 1))
        g = wl * w0 + wu * w2
        b = w1 + g
        h = g + vl * roll_lanes(b, 1)
        yv[k] = jnp.where(lane % 2 == 1, b, roll_lanes(h, 1))
        if k < 4:
            ys[k] = jnp.where(row < 1, roll_rows(corner, -1), roll_rows(y3[k], 1))

    def lateral(n, k, w):
        beyond = xw[pl.ds(2 * k * LINE + n, ROWS, stride=LINE), :]
        w0 = jnp.where(row < 2, beyond, roll_rows(w, 2))
        w1 = jnp.where(row < 1, roll_rows(beyond, -1), roll_rows(w, 1))
        g = wl * w0 + wu * w
        b = w1 + g
        v = roll_lanes(yv[k], -2 * n - 2)
        h = g + 0.5 * roll_lanes(jnp.where(end, v, b), 1)
        return jnp.where(start, v, roll_lanes(h, 1)) + vu * b

    def smooth(n, first):
        sums = []
        for k in range(8):
            ref, c = (xs, k) if k < 4 else (kx, k - 4)
            outer = ref[n + 1, c] if first else ref[n - 1, c] + ref[n + 1, c]
            sums.append(lateral(n, k, ref[n, c] + 0.5 * outer))
        act = activity(codes[n])
        half = 0.5 * act
        flow = apply_sym(lookup(tables, 0, codes[n], half), sums[:4])
        for c in range(4):
            sm[n + 1, c] = flow[c] + half * sums[4 + c]

    def place(n):
        z = level_of(side, n, levels)
        for c in range(4):
            low = jnp.where(row < 1, x3[2 * c + 1, pl.ds(n, 1), :], roll_rows(xs[n, c], 1))
            x = jnp.where(start, roll_lanes(ys[c], -2 * n - 1), roll_lanes(low, 1))
            updated[z, c] = iterate[z, c] + x

    for c in range(4):
        sm[0, c] = jnp.zeros((ROWS, LANES), F32)
    smooth(0, True)
    place(0)

    def level(n, carry):
        smooth(n, False)
        place(n)
        return carry

    lax.fori_loop(1, levels, level, 0)
    smooth(levels, False)

    def restrict(k, carry):
        at = side * (levels + 1) + (1 - 2 * side) * 2 * k
        step = 1 - 2 * side
        for c in range(4):
            coarse[k, c] = sm[at + step, c] + 0.5 * (sm[at, c] + sm[at + 2 * step, c])
        return carry

    lax.fori_loop(0, levels // 2, restrict, 0)


def call(kernel, outs, *args, scratch=()):
    whole = pl.BlockSpec(memory_space=pltpu.VMEM)
    return pl.pallas_call(
        kernel,
        out_shape=[jax.ShapeDtypeStruct(s, t) for s, t in outs],
        in_specs=[whole] * len(args),
        out_specs=[whole] * len(outs),
        scratch_shapes=[pltpu.VMEM(s, F32) for s in scratch],
        compiler_params=pltpu.CompilerParams(vmem_limit_bytes=VMEM_LIMIT),
    )(*args)


def around(x, dx, dy):
    nx, ny = lax.axis_size("lx"), lax.axis_size("ly")
    pairs = [
        (i * ny + j, ((i + dx) % nx) * ny + (j + dy) % ny) for i in range(nx) for j in range(ny)
    ]
    return lax.ppermute(x, ("lx", "ly"), pairs)


def swap(x):
    return lax.ppermute(x, "depth", [(0, 1), (1, 0)])


def local(iterate, right_side, storage, zones, counts, materials):
    levels = zones.shape[0]
    tile = (ROWS, LANES)
    tables = jnp.broadcast_to(
        materials.transpose(0, 2, 3, 1).reshape(32, ROWS, 1), (32, ROWS, LANES)
    )
    side = lax.axis_index("depth")
    near = (levels - 1) * (1 - side)
    next_near = near + 2 * side - 1
    near_codes = [
        jnp.where(
            z + side * levels < counts, lax.dynamic_index_in_dim(zones, z, 0, False) + 1, 0
        ).astype(F32)[None]
        for z in (near, next_near)
    ]
    plane = lax.dynamic_index_in_dim(iterate, near, 0, False)
    met = swap(jnp.concatenate([plane] + near_codes, axis=0))

    xm, ym, dm, codes = call(
        functools.partial(pack_kernel, levels),
        [((15, LINE, LANES), F32), ((10,) + tile, F32), ((10, 2, LANES), F32),
         ((levels + 2,) + tile, jnp.int32)],
        iterate, right_side, storage, zones, counts, met,
    )
    xm_in, ym_in, dm_in = around(xm, -1, 0), around(ym, 0, -1), around(dm, -1, -1)
    own, = call(
        functools.partial(own_kernel, levels),
        [((levels, SUMMED) + tile, F32)],
        iterate, codes, met, tables,
        scratch=[(levels + 2, SUMMED) + tile],
    )
    gains, rests, message, ends, codes_s = call(
        functools.partial(sweep_kernel, levels),
        [((levels, 16) + tile, F32), ((levels, 4) + tile, F32), ((54,) + tile, F32),
         ((14,) + tile, F32), ((levels + 2,) + tile, jnp.int32)],
        own, xm_in, ym_in, dm_in, iterate, right_side, storage, codes, met, tables,
        scratch=[
            (2 * SUMMED * LINE + 6 * LINE, LANES), (SUMMED,) + tile, (10,) + tile,
            (levels + 2, 4) + tile, (levels, 4) + tile, (levels,) + tile,
            (levels, 10) + tile, (levels + 1, 10) + tile, (levels, 4) + tile,
        ],
    )
    got = swap(message)
    xs, kx, x3, y3, d3 = call(
        functools.partial(back_kernel, levels),
        [((levels + 2, 4) + tile, F32), ((levels + 2, 4) + tile, F32),
         ((16, LINE, LANES), F32), ((8,) + tile, F32), ((8, 2, LANES), F32)],
        gains, rests, ends, got, codes_s, tables,
    )
    x3_in, y3_in, d3_in = around(x3, 1, 0), around(y3, 0, 1), around(d3, 1, 1)
    updated, coarse = call(
        functools.partial(finish_kernel, levels),
        [((levels, 4) + tile, F32), ((levels // 2, 4) + tile, F32)],
        xs, kx, x3_in, y3_in, d3_in, iterate, codes, tables,
        scratch=[
            (16 * LINE + 6 * LINE, LANES), (8,) + tile, (4,) + tile, (levels + 2, 4) + tile,
        ],
    )
    return updated, coarse


def solution(mesh):
    placed = (
        P("depth", None, "lx", "ly"),
        P("depth", None, "lx", "ly"),
        P("depth", "lx", "ly"),
        P("depth", "lx", "ly"),
        P("lx", "ly"),
        P(),
    )
    return jax.shard_map(
        local,
        mesh=mesh,
        in_specs=placed,
        out_specs=(P("depth", None, "lx", "ly"), P("depth", None, "lx", "ly")),
        check_vma=False,
    )
```

profile of v0, /device:TPU:0, one launch (start us, length us, event | category | flops | bytes accessed | tf_op | source)
XLA Modules:
  0.0 42.2 jit_solution(6422112487085104795)
XLA Ops:
  0.6 0.7 %dynamic-slice_bitcast_fusion = f32[4,8,128]{2,1,0:T(8,128)S(1)} fusion(f32[16,4,8,128]{3,2,1,0:T(8,128)} %iterate.7, s32[]{:T(128)S(6)} %select_n.16), kind=kLoop, calls=%fused_computation.1 | loop fusion | bytes 32772 | tf_op jit(solution)/shard_map/jit(dynamic_index_in_dim)/squeeze | solution.py:492
  1.4 0.7 %fusion.3 = (f32[1,8,128]{2,1,0:T(8,128)S(1)}, f32[1,8,128]{2,1,0:T(8,128)S(1)}) fusion(s32[16,8,128]{2,1,0:T(8,128)} %zones.1, s32[]{:T(128)S(6)} %select_n.16, s32[8,128]{1,0:T(8,128)} %counts.1, s32[]{:T(128)S(6)} %add.34, s32[]{:T(128)S(6)} %select_n.18, s32[]{:T(128)S(6)} %add.38), kind=kLoop, calls=%fused_computation.7 | loop fusion | flops 8192 | bytes 20496 | tf_op jit(solution)/shard_map/broadcast_in_dim | solution.py:487
  2.1 0.5 %collective-permute-start = (f32[6,8,128]{2,1,0:T(8,128)S(1)}, f32[6,8,128]{2,1,0:T(8,128)S(1)}, u32[]{:S(2)}, u32[]{:S(2)}) collective-permute-start(f32[6,8,128]{2,1,0:T(8,128)S(1)} %pad_maximum_fusion), channel_id=1, source_target_pairs={{0,16},{16,0},{1,17},{17,1},{2,18},{18,2},{3,19},{19,3},{4,20},{20... | collective-permute-start | bytes 73736 | tf_op jit(solution)/shard_map/ppermute | solution.py:474
  2.6 0.8 %collective-permute-done.met = f32[6,8,128]{2,1,0:T(8,128)S(1)} collective-permute-done((f32[6,8,128]{2,1,0:T(8,128)S(1)}, f32[6,8,128]{2,1,0:T(8,128)S(1)}, u32[]{:S(2)}, u32[]{:S(2)}) %collective-permute-start) | collective-permute-done | bytes 24608 | tf_op jit(solution)/shard_map/ppermute | solution.py:474
  3.5 0.9 %copy-done = f32[16,4,8,128]{3,2,1,0:T(8,128)S(1)} copy-done((f32[16,4,8,128]{3,2,1,0:T(8,128)S(1)}, f32[16,4,8,128]{3,2,1,0:T(8,128)}, u32[]{:S(2)}) %copy-start) | copy-done | bytes 262168
  4.4 0.9 %copy-done.2 = f32[16,4,8,128]{3,2,1,0:T(8,128)S(1)} copy-done((f32[16,4,8,128]{3,2,1,0:T(8,128)S(1)}, f32[16,4,8,128]{3,2,1,0:T(8,128)}, u32[]{:S(2)}) %copy-start.2) | copy-done | bytes 262168
  5.4 0.8 %copy-done.4 = f32[16,8,128]{2,1,0:T(8,128)S(1)} copy-done((f32[16,8,128]{2,1,0:T(8,128)S(1)}, f32[16,8,128]{2,1,0:T(8,128)}, u32[]{:S(2)}) %copy-start.4) | copy-done | bytes 65560
  6.2 0.8 %copy-done.5 = s32[16,8,128]{2,1,0:T(8,128)S(1)} copy-done((s32[16,8,128]{2,1,0:T(8,128)S(1)}, s32[16,8,128]{2,1,0:T(8,128)}, u32[]{:S(2)}) %copy-start.5) | copy-done | bytes 65560
  7.0 0.7 %copy-done.6 = s32[8,128]{1,0:T(8,128)S(1)} copy-done((s32[8,128]{1,0:T(8,128)S(1)}, s32[8,128]{1,0:T(8,128)}, u32[]{:S(2)}) %copy-start.6) | copy-done | bytes 4120
  7.7 0.3 shard_map.77
  8.0 3.8 %collective-permute-start.1 = (f32[15,24,128]{2,1,0:T(8,128)S(1)}, f32[15,24,128]{2,1,0:T(8,128)S(1)}, u32[]{:S(2)}, u32[]{:S(2)}) collective-permute-start(f32[15,24,128]{2,1,0:T(8,128)S(1)} %get-tuple-element.17), channel_id=1, source_target_pairs={{0,12},{1,13},{2,14},{3,15},{4,0},{5,1},{6,2},{7,3},{8,4},{9,5},{1... | collective-permute-start | bytes 552968 | tf_op jit(solution)/shard_map/ppermute | solution.py:470
  11.8 3.6 %collective-permute-start.2 = (f32[10,8,128]{2,1,0:T(8,128)S(1)}, f32[10,8,128]{2,1,0:T(8,128)S(1)}, u32[]{:S(2)}, u32[]{:S(2)}) collective-permute-start(f32[10,8,128]{2,1,0:T(8,128)S(1)} %get-tuple-element.18), channel_id=1, source_target_pairs={{0,3},{1,0},{2,1},{3,2},{4,7},{5,4},{6,5},{7,6},{8,11},{9,8},{10,9... | collective-permute-start | bytes 122888 | tf_op jit(solution)/shard_map/ppermute | solution.py:470
  15.4 0.4 collective-permute-start.3
  15.9 0.8 %broadcast_in_dim.22.tables = f32[32,8,128]{2,1,0:T(8,128)S(1)} broadcast(f32[32,8]{1,0:T(8,128)} %bitcast.21), dimensions={0,1} | broadcast | bytes 132096 | tf_op jit(solution)/shard_map/broadcast_in_dim | solution.py:480
  16.7 0.5 %shard_map.78.own = f32[16,19,8,128]{3,2,1,0:T(8,128)S(1)} custom-call(f32[16,4,8,128]{3,2,1,0:T(8,128)S(1)} %copy-done, s32[18,8,128]{2,1,0:T(8,128)S(1)} %get-tuple-element.16.codes, f32[6,8,128]{2,1,0:T(8,128)S(1)} %collective-permute-done.met, f32[32,8,128]{2,1,0:T(8,128)S(1)} %broadcast_in_dim.22.tables), custom_call_target="tpu_custom_call" | custom-call | tf_op jit(solution)/shard_map/pallas_call | solution.py:455
  17.2 2.8 %collective-permute-done.3.dm = f32[10,2,128]{2,1,0:T(2,128)S(1)} collective-permute-done((f32[10,2,128]{2,1,0:T(2,128)S(1)}, f32[10,2,128]{2,1,0:T(2,128)S(1)}, u32[]{:S(2)}, u32[]{:S(2)}) %collective-permute-start.3) | collective-permute-done | bytes 10272 | tf_op jit(solution)/shard_map/ppermute | solution.py:470
  20.0 0.0 collective-permute-done.2.ym
  20.0 0.0 collective-permute-done.1.xm
  20.0 0.0 copy-done.3
  20.0 7.1 %shard_map.79 = (f32[16,16,8,128]{3,2,1,0:T(8,128)S(1)}, f32[16,4,8,128]{3,2,1,0:T(8,128)S(1)}, f32[54,8,128]{2,1,0:T(8,128)S(1)}, f32[14,8,128]{2,1,0:T(8,128)S(1)}, s32[18,8,128]{2,1,0:T(8,128)S(1)}) custom-call(f32[16,19,8,128]{3,2,1,0:T(8,128)S(1)} %shard_map.78.own, f32[15,24,128]{2,1,0:T(8,128)S(1)} %collective-permute-done.1.xm, ...), custom_call_target="tpu_custom_call" | custom-call | tf_op jit(solution)/shard_map/pallas_call | solution.py:455
  27.2 0.0 copy-start.1
  27.2 0.1 collective-permute-start.4
  27.3 1.5 %collective-permute-done.4.got = f32[54,8,128]{2,1,0:T(8,128)S(1)} collective-permute-done((f32[54,8,128]{2,1,0:T(8,128)S(1)}, f32[54,8,128]{2,1,0:T(8,128)S(1)}, u32[]{:S(2)}, u32[]{:S(2)}) %collective-permute-start.4) | collective-permute-done | bytes 221216 | tf_op jit(solution)/shard_map/ppermute | solution.py:474
  28.7 0.5 %shard_map.80 = (f32[18,4,8,128]{3,2,1,0:T(8,128)S(1)}, f32[18,4,8,128]{3,2,1,0:T(8,128)S(1)}, f32[16,24,128]{2,1,0:T(8,128)S(1)}, f32[8,8,128]{2,1,0:T(8,128)S(1)}, f32[8,2,128]{2,1,0:T(2,128)S(1)}) custom-call(f32[16,16,8,128]{3,2,1,0:T(8,128)S(1)} %get-tuple-element.20.gains, f32[16,4,8,128]{3,2,1,0:T(8,128)S(1)} %get-tuple-element.21.rests, ...), custom_call_target="tpu_custom_call" | custom-call | tf_op jit(solution)/shard_map/pallas_call | solution.py:455
  29.2 0.5 %collective-permute-start.5 = (f32[16,24,128]{2,1,0:T(8,128)S(1)}, f32[16,24,128]{2,1,0:T(8,128)S(1)}, u32[]{:S(2)}, u32[]{:S(2)}) collective-permute-start(f32[16,24,128]{2,1,0:T(8,128)S(1)} %get-tuple-element.27), channel_id=1, source_target_pairs={{0,4},{1,5},{2,6},{3,7},{4,8},{5,9},{6,10},{7,11},{8,12},{9,13},{1... | collective-permute-start | bytes 589832 | tf_op jit(solution)/shard_map/ppermute | solution.py:470
  29.7 0.0 collective-permute-start.6
  29.7 1.4 %collective-permute-start.7 = (f32[8,2,128]{2,1,0:T(2,128)S(1)}, f32[8,2,128]{2,1,0:T(2,128)S(1)}, u32[]{:S(2)}, u32[]{:S(2)}) collective-permute-start(f32[8,2,128]{2,1,0:T(2,128)S(1)} %get-tuple-element.29), channel_id=1, source_target_pairs={{0,5},{1,6},{2,7},{3,4},{4,9},{5,10},{6,11},{7,8},{8,13},{9,14},{1... | collective-permute-start | bytes 24584 | tf_op jit(solution)/shard_map/ppermute | solution.py:470
  31.1 6.3 %collective-permute-done.7.d3 = f32[8,2,128]{2,1,0:T(2,128)S(1)} collective-permute-done((f32[8,2,128]{2,1,0:T(2,128)S(1)}, f32[8,2,128]{2,1,0:T(2,128)S(1)}, u32[]{:S(2)}, u32[]{:S(2)}) %collective-permute-start.7) | collective-permute-done | bytes 8224 | tf_op jit(solution)/shard_map/ppermute | solution.py:470
  37.4 0.0 collective-permute-done.6.y3
  37.4 0.0 collective-permute-done.5.x3
  37.4 0.0 copy-done.1
  37.4 4.8 %shard_map.81 = (f32[16,4,8,128]{3,2,1,0:T(8,128)}, f32[8,4,8,128]{3,2,1,0:T(8,128)}) custom-call(f32[18,4,8,128]{3,2,1,0:T(8,128)S(1)} %get-tuple-element.25.xs, f32[18,4,8,128]{3,2,1,0:T(8,128)S(1)} %get-tuple-element.26.kx, f32[16,24,128]{2,1,0:T(8,128)S(1)} %collective-permute-done.5.x3, f32[8,8,128]{2,1,0:T(8,128)S(1)} %collective-permute-done.6.y3, ...), custom_call_target="tpu_custom_call" | custom-call | tf_op jit(solution)/shard_map/pallas_call | solution.py:455
  (7 shorter events, 0.0 us)
Async XLA Ops:
  2.1 1.4 %collective-permute-start = (f32[6,8,128]{2,1,0:T(8,128)S(1)}, f32[6,8,128]{2,1,0:T(8,128)S(1)}, u32[]{:S(2)}, u32[]{:S(2)}) collective-permute-start(f32[6,8,128]{2,1,0:T(8,128)S(1)} %pad_maximum_fusion), channel_id=1, source_target_pairs={{0,16},{16,0},{1,17},{17,1},{2,18},{18,2},{3,19},{19,3},{4,20},{20... | collective-permute-start | bytes 73736 | tf_op jit(solution)/shard_map/ppermute | solution.py:474
  3.5 0.9 %copy-start = (f32[16,4,8,128]{3,2,1,0:T(8,128)S(1)}, f32[16,4,8,128]{3,2,1,0:T(8,128)}, u32[]{:S(2)}) copy-start(f32[16,4,8,128]{3,2,1,0:T(8,128)} %iterate.7) | copy-start | bytes 786436
  4.4 0.9 %copy-start.2 = (f32[16,4,8,128]{3,2,1,0:T(8,128)S(1)}, f32[16,4,8,128]{3,2,1,0:T(8,128)}, u32[]{:S(2)}) copy-start(f32[16,4,8,128]{3,2,1,0:T(8,128)} %right.3) | copy-start | bytes 786436
  5.4 0.8 %copy-start.4 = (f32[16,8,128]{2,1,0:T(8,128)S(1)}, f32[16,8,128]{2,1,0:T(8,128)}, u32[]{:S(2)}) copy-start(f32[16,8,128]{2,1,0:T(8,128)} %storage.3) | copy-start | bytes 196612
  6.2 0.8 %copy-start.5 = (s32[16,8,128]{2,1,0:T(8,128)S(1)}, s32[16,8,128]{2,1,0:T(8,128)}, u32[]{:S(2)}) copy-start(s32[16,8,128]{2,1,0:T(8,128)} %zones.1) | copy-start | bytes 196612
  7.0 0.7 %copy-start.6 = (s32[8,128]{1,0:T(8,128)S(1)}, s32[8,128]{1,0:T(8,128)}, u32[]{:S(2)}) copy-start(s32[8,128]{1,0:T(8,128)} %counts.1) | copy-start | bytes 12292
  7.7 12.3 %copy-start.3 = (f32[16,4,8,128]{3,2,1,0:T(8,128)S(1)}, f32[16,4,8,128]{3,2,1,0:T(8,128)}, u32[]{:S(2)}) copy-start(f32[16,4,8,128]{3,2,1,0:T(8,128)} %right.3) | copy-start | bytes 786436
  8.0 12.0 %collective-permute-start.1 = (f32[15,24,128]{2,1,0:T(8,128)S(1)}, f32[15,24,128]{2,1,0:T(8,128)S(1)}, u32[]{:S(2)}, u32[]{:S(2)}) collective-permute-start(f32[15,24,128]{2,1,0:T(8,128)S(1)} %get-tuple-element.17), channel_id=1, source_target_pairs={{0,12},{1,13},{2,14},{3,15},{4,0},{5,1},{6,2},{7,3},{8,4},{9,5},{1... | collective-permute-start | bytes 552968 | tf_op jit(solution)/shard_map/ppermute | solution.py:470
  11.8 8.2 %collective-permute-start.2 = (f32[10,8,128]{2,1,0:T(8,128)S(1)}, f32[10,8,128]{2,1,0:T(8,128)S(1)}, u32[]{:S(2)}, u32[]{:S(2)}) collective-permute-start(f32[10,8,128]{2,1,0:T(8,128)S(1)} %get-tuple-element.18), channel_id=1, source_target_pairs={{0,3},{1,0},{2,1},{3,2},{4,7},{5,4},{6,5},{7,6},{8,11},{9,8},{10,9... | collective-permute-start | bytes 122888 | tf_op jit(solution)/shard_map/ppermute | solution.py:470
  15.4 4.6 %collective-permute-start.3 = (f32[10,2,128]{2,1,0:T(2,128)S(1)}, f32[10,2,128]{2,1,0:T(2,128)S(1)}, u32[]{:S(2)}, u32[]{:S(2)}) collective-permute-start(f32[10,2,128]{2,1,0:T(2,128)S(1)} %get-tuple-element.19), channel_id=1, source_target_pairs={{0,15},{1,12},{2,13},{3,14},{4,3},{5,0},{6,1},{7,2},{8,7},{9,4},{1... | collective-permute-start | bytes 30728 | tf_op jit(solution)/shard_map/ppermute | solution.py:470
  27.2 10.3 %copy-start.1 = (f32[16,4,8,128]{3,2,1,0:T(8,128)S(1)}, f32[16,4,8,128]{3,2,1,0:T(8,128)}, u32[]{:S(2)}) copy-start(f32[16,4,8,128]{3,2,1,0:T(8,128)} %iterate.7) | copy-start | bytes 786436
  27.2 1.5 %collective-permute-start.4 = (f32[54,8,128]{2,1,0:T(8,128)S(1)}, f32[54,8,128]{2,1,0:T(8,128)S(1)}, u32[]{:S(2)}, u32[]{:S(2)}) collective-permute-start(f32[54,8,128]{2,1,0:T(8,128)S(1)} %get-tuple-element.23), channel_id=1, source_target_pairs={{0,16},{16,0},{1,17},{17,1},{2,18},{18,2},{3,19},{19,3},{4,20},{20... | collective-permute-start | bytes 663560 | tf_op jit(solution)/shard_map/ppermute | solution.py:474
  29.2 8.2 %collective-permute-start.5 = (f32[16,24,128]{2,1,0:T(8,128)S(1)}, f32[16,24,128]{2,1,0:T(8,128)S(1)}, u32[]{:S(2)}, u32[]{:S(2)}) collective-permute-start(f32[16,24,128]{2,1,0:T(8,128)S(1)} %get-tuple-element.27), channel_id=1, source_target_pairs={{0,4},{1,5},{2,6},{3,7},{4,8},{5,9},{6,10},{7,11},{8,12},{9,13},{1... | collective-permute-start | bytes 589832 | tf_op jit(solution)/shard_map/ppermute | solution.py:470
  29.7 7.7 %collective-permute-start.6 = (f32[8,8,128]{2,1,0:T(8,128)S(1)}, f32[8,8,128]{2,1,0:T(8,128)S(1)}, u32[]{:S(2)}, u32[]{:S(2)}) collective-permute-start(f32[8,8,128]{2,1,0:T(8,128)S(1)} %get-tuple-element.28), channel_id=1, source_target_pairs={{0,1},{1,2},{2,3},{3,0},{4,5},{5,6},{6,7},{7,4},{8,9},{9,10},{10,1... | collective-permute-start | bytes 98312 | tf_op jit(solution)/shard_map/ppermute | solution.py:470
  29.7 7.7 %collective-permute-start.7 = (f32[8,2,128]{2,1,0:T(2,128)S(1)}, f32[8,2,128]{2,1,0:T(2,128)S(1)}, u32[]{:S(2)}, u32[]{:S(2)}) collective-permute-start(f32[8,2,128]{2,1,0:T(2,128)S(1)} %get-tuple-element.29), channel_id=1, source_target_pairs={{0,5},{1,6},{2,7},{3,4},{4,9},{5,10},{6,11},{7,8},{8,13},{9,14},{1... | collective-permute-start | bytes 24584 | tf_op jit(solution)/shard_map/ppermute | solution.py:470
where the time goes:
time: 42.7 us; the launch traced here: 42.2 us
  Pallas kernels  13.2 us (31%)
  waiting for transfers between devices  11.4 us (27%)
  starting transfers between devices  10.4 us (24%)
  local copies, waits for them, and re-layouts  5.8 us (14%)
  other arithmetic  0.73 us (2%)
  between operations  0.72 us (2%)
    pallas_call x5, Pallas kernels, call(): pl.pallas_call(kernel, out_shape=[jax.ShapeDtypeStruct(s, t) for s, t in...  13.2 us
    ppermute x6, starting transfers between devices, around(): return lax.ppermute(x, ('lx', 'ly'), pairs)  9.77 us
    ppermute x6, waiting for transfers between devices, around(): return lax.ppermute(x, ('lx', 'ly'), pairs)  9.11 us
    unnamed x14, local copies, waits for them, and re-layouts  4.27 us
    ppermute x2, waiting for transfers between devices, swap(): return lax.ppermute(x, 'depth', [(0, 1), (1, 0)])  2.31 us
  transfers between devices with their start and end apart: 8, of which 4 were waited for; matrix products, arithmetic and copies ran while one was open for 2% of the time, Pallas kernels for 1%

commit v1 on v0

v1 whole, which is shorter than its diff:
```python
import functools

import jax
import jax.numpy as jnp
from jax import lax
from jax.experimental import pallas as pl
from jax.experimental.pallas import tpu as pltpu
from jax.sharding import PartitionSpec as P

PAIRS = [(i, j) for i in range(4) for j in range(i, 4)]
AT = {}
for _k, (_i, _j) in enumerate(PAIRS):
    AT[_i, _j] = AT[_j, _i] = _k

ROWS, LANES = 8, 128
SUMMED = 19
PAD = 8
MESSAGE = 60
F32 = jnp.float32
VMEM_LIMIT = 48 * 1024 * 1024


def row_index():
    return lax.broadcasted_iota(jnp.int32, (ROWS, LANES), 0)


def lane_index():
    return lax.broadcasted_iota(jnp.int32, (ROWS, LANES), 1)


def roll_rows(x, by):
    return pltpu.roll(x, by % x.shape[0], 0)


def roll_lanes(x, by):
    return pltpu.roll(x, by % LANES if isinstance(by, int) else lax.rem(by + LANES, LANES), 1)


def activity(codes):
    return jnp.where(codes > 0, 1.0, 0.0).astype(F32)


def lookup(tables, kind, codes, act):
    rows = jnp.maximum(codes - 1, 0)
    found = []
    for i, j in PAIRS:
        table = tables[kind * 16 + 4 * i + j]
        parts = [
            jnp.take_along_axis(table, rows[at : at + ROWS], axis=0, mode="promise_in_bounds")
            for at in range(0, rows.shape[0], ROWS)
        ]
        value = parts[0] if len(parts) == 1 else jnp.concatenate(parts, axis=0)
        found.append(value * act)
    return found


def apply_sym(matrix, vector):
    out = []
    for i in range(4):
        total = matrix[AT[i, 0]] * vector[0]
        for j in range(1, 4):
            total = total + matrix[AT[i, j]] * vector[j]
        out.append(total)
    return out


def summed_fields(tables, codes, field):
    act = activity(codes)
    lateral = lookup(tables, 0, codes, act)
    return [act] + lateral + [act * v for v in field] + apply_sym(lateral, field)


def level_of(side, n, levels):
    return side * (levels - 1) + (1 - 2 * side) * n


def steps(first, last, body, width=1):
    passes = (last - first) // width

    def one(i, carry):
        for j in range(width):
            body(first + i * width + j)
        return carry

    lax.fori_loop(0, passes, one, 0)
    for n in range(first + passes * width, last):
        body(n)


def zero():
    return jnp.zeros((ROWS, LANES), F32)


def pack_kernel(
    levels, iterate, right, storage, zones, counts,
    it, rt, st, codes_out, xm, ym, dm, zones_v, counts_v, sems,
):
    side = lax.axis_index("depth")
    lane = lane_index()
    copies = [
        pltpu.make_async_copy(source, target, sems.at[k])
        for k, (source, target) in enumerate(
            [(zones, zones_v), (counts, counts_v), (iterate, it), (right, rt), (storage, st)]
        )
    ]
    for copy in copies:
        copy.start()
    for copy in copies:
        copy.wait()
    limit = counts_v[...] - side * levels
    acc = [zero() for _ in range(10)]
    for n in range(levels):
        z = level_of(side, n, levels)
        code = jnp.where(z < limit, zones_v[z] + 1, 0)
        codes_out[n] = code
        fields = [code.astype(F32)] + [it[z, c] for c in range(4)]
        fields += [rt[z, c] for c in range(4)] + [st[z]]
        for k, value in enumerate(fields):
            xm[k, n : n + 1, :] = value[0:1]
            if k < 5:
                xm[10 + k, n : n + 1, :] = value[1:2]
            acc[k] = jnp.where(lane // 2 == n, roll_lanes(value, 2 * n), acc[k])
    for k in range(10):
        ym[k] = acc[k]
        dm[k] = acc[k][0:2]


def own_kernel(levels, it, rt, st, codes, tables, sown, pre, u):
    side = lax.axis_index("depth")
    last_x = lax.axis_index("lx") == lax.axis_size("lx") - 1
    last_y = lax.axis_index("ly") == lax.axis_size("ly") - 1
    row, lane = row_index(), lane_index()
    wl = jnp.where(last_x & (row == 7), 0.0, 0.5).astype(F32)
    wu = jnp.where(row < 6, 0.5, 0.0).astype(F32)
    vl = jnp.where(last_y & (lane == 127), 0.0, 0.5).astype(F32)
    vu = jnp.where(lane < 127, 0.5, 0.0).astype(F32)
    for k in range(SUMMED):
        u[0, k] = zero()
        u[levels + 1, k] = zero()
        u[levels + 2, k] = zero()

    def fill(n):
        z = level_of(side, n, levels)
        field = [it[z, c] for c in range(4)]
        for k, value in enumerate(summed_fields(tables, codes[n], field)):
            u[n + 1, k] = value

    steps(0, levels, fill)

    def shift(n):
        z = level_of(side, n, levels)
        fields = [codes[n].astype(F32)] + [it[z, c] for c in range(4)]
        fields += [rt[z, c] for c in range(4)] + [st[z]]
        for k, value in enumerate(fields):
            pre[n, k] = roll_lanes(roll_rows(value, -1), -1)

    steps(0, levels, shift, 2)

    def gather(n):
        for k in range(SUMMED):
            w = u[n + 1, k] + 0.5 * (u[n, k] + u[n + 2, k])
            g = wl * w + wu * roll_rows(w, -2)
            b = jnp.where(row < 7, roll_rows(w, -1), 0.0) + g
            h = g + vu * roll_lanes(b, -1)
            sown[n, k] = jnp.where(lane < 127, roll_lanes(h, -1), 0.0) + vl * b

    steps(0, levels + 1, gather, 2)


def invert(m):
    d = lambda i, j: m[AT[i, j]]

    def small(a, b, c):
        ia = 1.0 / a
        l = b * ia
        ic = 1.0 / (c - l * b)
        lc = l * ic
        return ia + l * lc, -lc, ic

    a00, a01, a11 = small(d(0, 0), d(0, 1), d(1, 1))
    t00 = d(2, 0) * a00 + d(2, 1) * a01
    t01 = d(2, 0) * a01 + d(2, 1) * a11
    t10 = d(3, 0) * a00 + d(3, 1) * a01
    t11 = d(3, 0) * a01 + d(3, 1) * a11
    s00 = d(2, 2) - (t00 * d(2, 0) + t01 * d(2, 1))
    s01 = d(3, 2) - (t10 * d(2, 0) + t11 * d(2, 1))
    s11 = d(3, 3) - (t10 * d(3, 0) + t11 * d(3, 1))
    i22, i32, i33 = small(s00, s01, s11)
    u00 = i22 * t00 + i32 * t10
    u01 = i22 * t01 + i32 * t11
    u10 = i32 * t00 + i33 * t10
    u11 = i32 * t01 + i33 * t11
    i00 = a00 + (t00 * u00 + t10 * u10)
    i01 = a01 + (t00 * u01 + t10 * u11)
    i11 = a11 + (t01 * u01 + t11 * u11)
    return [i00, i01, -u00, -u10, i11, -u01, -u11, i22, i32, i33]


def sym_product(left, right):
    return [
        [
            (left[AT[i, 0]] * right[AT[0, j]] + left[AT[i, 1]] * right[AT[1, j]])
            + (left[AT[i, 2]] * right[AT[2, j]] + left[AT[i, 3]] * right[AT[3, j]])
            for j in range(4)
        ]
        for i in range(4)
    ]


def back_product(link, gain):
    return [
        (link[AT[i, 0]] * gain[0][j] + link[AT[i, 1]] * gain[1][j])
        + (link[AT[i, 2]] * gain[2][j] + link[AT[i, 3]] * gain[3][j])
        for i, j in PAIRS
    ]


def line_sum(values):
    return values + 0.5 * (roll_rows(values, 1) + roll_rows(values, -1))


def lane_sum(values):
    return values + 0.5 * (roll_lanes(values, 2) + roll_lanes(values, -2))


def lengthen(values, rows):
    return jnp.concatenate([values, jnp.zeros((rows - values.shape[0], LANES), F32)], axis=0)


def sweep_kernel(
    levels, sown, pre, xm, ym, dm, codes, tables,
    gains, rests, message, codes_s,
    xw, xl, yv, ys, fs, rs, ss, ps, ms, qs,
):
    line = levels + PAD
    last_x = lax.axis_index("lx") == lax.axis_size("lx") - 1
    last_y = lax.axis_index("ly") == lax.axis_size("ly") - 1
    row, lane = row_index(), lane_index()
    wl = jnp.where(last_x & (row == 7), 0.0, 0.5).astype(F32)
    wu = jnp.where(last_x & (row == 6), 0.0, 0.5).astype(F32)
    wu6 = jnp.where(last_x, 0.0, 0.5).astype(F32)
    vu127 = jnp.where(last_y, 0.0, 0.5).astype(F32)
    top = row == 7
    end = lane == 127

    line_lane = lax.broadcasted_iota(jnp.int32, (line, LANES), 1)
    line_vl = jnp.where(last_y & (line_lane == 127), 0.0, 0.5).astype(F32)
    line_vu = jnp.where(line_lane < 127, 0.5, 0.0).astype(F32)
    lines = []
    for r in range(2):
        line_codes = lengthen(xm[10 * r], line).astype(jnp.int32)
        line_field = [lengthen(xm[10 * r + 1 + c], line) for c in range(4)]
        lines.append(summed_fields(tables, line_codes, line_field))
    for k in range(SUMMED):
        x8, x9 = line_sum(lines[0][k]), line_sum(lines[1][k])
        g6, g7 = wu6 * x8, 0.5 * x9
        for r, (g, b) in enumerate(((g6, g6), (g7, x8 + g7))):
            h = g + line_vu * roll_lanes(b, -1)
            at = (2 * k + r + 6) * line
            xw[at : at + line, :] = jnp.where(line_lane < 127, roll_lanes(h, -1), 0.0) + line_vl * b
    for k in range(10):
        xl[k] = roll_lanes(xm[k], -1)

    corner = [lengthen(dm[k], ROWS) for k in range(10)]
    side_u = summed_fields(tables, ym[0].astype(jnp.int32), [ym[1 + c] for c in range(4)])
    corner_u = summed_fields(tables, corner[0].astype(jnp.int32), corner[1:5])
    for k in range(SUMMED):
        w0 = lane_sum(side_u[k])
        wd = lane_sum(corner_u[k])
        w1 = roll_rows(jnp.where(row < 1, wd, w0), -1)
        w2 = roll_rows(jnp.where(row < 2, wd, w0), -2)
        g = wl * w0 + wu * w2
        b = w1 + g
        h = g + 0.5 * roll_lanes(b, -1)
        yv[k] = jnp.where(lane % 2 == 0, vu127 * b, roll_lanes(h, 1))
    for k in range(10):
        ys[k] = roll_rows(jnp.where(row < 1, corner[k], ym[k]), -1)

    def shift_level(n):
        moved = []
        for k in range(10):
            value = jnp.where(top, xl[k, pl.ds(n, 1), :], pre[n, k])
            moved.append(jnp.where(end, roll_lanes(ys[k], 127 - 2 * n), value))
        codes_s[n] = moved[0].astype(jnp.int32)
        for c in range(4):
            fs[n + 1, c] = moved[1 + c]
            rs[n, c] = moved[5 + c]
        ss[n] = moved[9]

    steps(0, levels, shift_level, 2)
    for c in range(4):
        fs[0, c] = zero()
        fs[levels + 1, c] = zero()
    for k in range(10):
        ms[0, k] = zero()

    def lateral_sums(n):
        sums = []
        for k in range(SUMMED):
            beyond = xw[pl.ds(2 * k * line + n, ROWS, stride=line), :]
            value = sown[n, k] + jnp.where(row >= 6, beyond, 0.0)
            sums.append(value + jnp.where(lane >= 126, roll_lanes(yv[k], 126 - 2 * n), 0.0))
        return sums

    def assemble(n, last=False):
        sums = lateral_sums(n)
        act = activity(codes_s[n])
        half = 0.5 * act
        lateral = lookup(tables, 0, codes_s[n], half)
        below = [ms[n, k] for k in range(10)]
        if last:
            above = [zero() for _ in range(10)]
        else:
            both = half * activity(codes_s[n + 1])
            here = lookup(tables, 1, codes_s[n], both)
            there = lookup(tables, 1, codes_s[n + 1], both)
            above = [here[k] + there[k] for k in range(10)]
        block = []
        for k, (i, j) in enumerate(PAIRS):
            value = (lateral[k] * sums[0] + half * sums[1 + k]) + (below[k] + above[k])
            block.append(value + ss[n] if i == j else value)
        for k in range(10):
            ms[n + 1, k] = above[k]
            ps[n, k] = block[k]
        field = [fs[n + 1, c] for c in range(4)]
        before = apply_sym(below, [fs[n, c] for c in range(4)])
        after = apply_sym(above, [fs[n + 2, c] for c in range(4)])
        diagonal = apply_sym(block, field)
        flow = apply_sym(lateral, sums[11:15])
        for c in range(4):
            near = (before[c] + after[c]) + (flow[c] + half * sums[15 + c])
            qs[n, c] = act * (rs[n, c] - (diagonal[c] - near))

    steps(0, levels - 1, assemble, 2)
    assemble(levels - 1, True)

    def eliminate(n, carry):
        coupled, carried = carry
        inverse = invert([ps[n, k] - coupled[k] for k in range(10)])
        value = [qs[n, c] + carried[c] for c in range(4)]
        link = [ms[n + 1, k] for k in range(10)]
        gain = sym_product(inverse, link)
        rest = apply_sym(inverse, value)
        for i in range(4):
            rests[n, i] = rest[i]
            for j in range(4):
                gains[n, 4 * i + j] = gain[i][j]
        return back_product(link, gain), apply_sym(link, rest)

    zeros = [zero() for _ in range(10)]
    coupled, carried = lax.fori_loop(0, levels - 1, eliminate, (zeros, zeros[:4]))
    end_n = levels - 1
    for k in range(10):
        message[k] = ps[end_n, k] - coupled[k]
    for c in range(4):
        message[10 + c] = qs[end_n, c] + carried[c]
        message[33 + c] = fs[levels, c]
        message[56 + c] = rests[end_n - 1, c]
    for k, value in enumerate(lateral_sums(levels)):
        message[14 + k] = value
    message[37] = codes_s[end_n].astype(F32)
    message[38] = codes_s[end_n - 1].astype(F32)
    message[39] = codes[end_n].astype(F32)
    for k in range(16):
        message[40 + k] = gains[end_n - 1, k]


def back_kernel(levels, gains, rests, message, got, codes_s, tables, xs, kx, x3, y3, d3):
    lane = lane_index()
    planes = levels + 2

    def carry_on(gain, rest, x):
        out = []
        for i in range(4):
            out.append(
                rest[i] + ((gain[4 * i] * x[0] + gain[4 * i + 1] * x[1])
                           + (gain[4 * i + 2] * x[2] + gain[4 * i + 3] * x[3]))
            )
        return out

    def end_of(ref):
        code = ref[37].astype(jnp.int32)
        act = activity(code)
        part = lambda at, count: [ref[at + k] for k in range(count)]
        return code, act, part(0, 10), part(10, 4), part(14, SUMMED), part(33, 4)

    here, there = end_of(message), end_of(got)
    both = 0.5 * here[1] * there[1]
    link_here = lookup(tables, 1, here[0], both)
    link_there = lookup(tables, 1, there[0], both)
    link = [link_here[k] + link_there[k] for k in range(10)]

    def complete(one, other):
        code, act, block, value, _, field = one
        _, _, _, _, sums, field_there = other
        half = 0.5 * act
        lateral = lookup(tables, 0, code, half)
        added = [lateral[k] * sums[0] + half * sums[1 + k] + link[k] for k in range(10)]
        across = apply_sym(link, field_there)
        flow = apply_sym(lateral, sums[11:15])
        diagonal = apply_sym(added, field)
        full = [
            value[c] + act * ((across[c] + flow[c] + half * sums[15 + c]) - diagonal[c])
            for c in range(4)
        ]
        return [block[k] + added[k] for k in range(10)], full

    block, value = complete(here, there)
    block_there, value_there = complete(there, here)
    inverse = invert(block_there)
    gain = sym_product(inverse, link)
    rest = apply_sym(inverse, value_there)
    coupled, carried = back_product(link, gain), apply_sym(link, rest)
    x = apply_sym(
        invert([block[k] - coupled[k] for k in range(10)]),
        [value[c] + carried[c] for c in range(4)],
    )
    x_met = carry_on([gain[i][j] for i in range(4) for j in range(4)], rest, x)
    x_far = carry_on([got[40 + k] for k in range(16)], [got[56 + c] for c in range(4)], x_met)
    for c in range(4):
        xs[levels - 1, c] = x[c]
        xs[levels, c] = x_met[c]
        xs[levels + 1, c] = x_far[c]

    def retreat(step, x):
        n = levels - 2 - step
        x = carry_on([gains[n, k] for k in range(16)], [rests[n, c] for c in range(4)], x)
        for c in range(4):
            xs[n, c] = x[c]
        return x

    lax.fori_loop(0, levels - 1, retreat, x)

    acc = [zero() for _ in range(8)]
    for n in range(planes):
        field = [xs[n, c] for c in range(4)]
        code = codes_s[n] if n < levels else got[37 + n - levels].astype(jnp.int32)
        flow = apply_sym(lookup(tables, 0, code, activity(code)), field)
        for c in range(4):
            kx[n, c] = flow[c]
        for k, value in enumerate(field + flow):
            for r in range(2):
                at = (2 * k + r) * planes + n
                x3[at : at + 1, :] = value[6 + r : 7 + r]
            acc[k] = jnp.where(lane // 2 == n, roll_lanes(value, 2 * n + 2), acc[k])
    for k in range(8):
        y3[k] = acc[k]
        d3[k] = acc[k][6:8]


def own_back_kernel(levels, xs, kx, sown, pre):
    last_x = lax.axis_index("lx") == lax.axis_size("lx") - 1
    last_y = lax.axis_index("ly") == lax.axis_size("ly") - 1
    row, lane = row_index(), lane_index()
    wl = jnp.where(row >= 2, 0.5, 0.0).astype(F32)
    wu = jnp.where(last_x & (row == 7), 0.0, 0.5).astype(F32)
    vl = jnp.where(lane >= 1, 0.5, 0.0).astype(F32)
    vu = jnp.where(last_y & (lane == 127), 0.0, 0.5).astype(F32)

    def gather(n, first=False):
        for k in range(8):
            ref, c = (xs, k) if k < 4 else (kx, k - 4)
            outer = ref[n + 1, c] if first else ref[n - 1, c] + ref[n + 1, c]
            w = ref[n, c] + 0.5 * outer
            g = wl * roll_rows(w, 2) + wu * w
            b = jnp.where(row >= 1, roll_rows(w, 1), 0.0) + g
            h = g + vl * roll_lanes(b, 1)
            sown[n, k] = jnp.where(lane >= 1, roll_lanes(h, 1), 0.0) + vu * b

    gather(0, True)
    steps(1, levels + 1, gather, 2)

    def shift(n):
        for c in range(4):
            pre[n, c] = roll_lanes(roll_rows(xs[n, c], 1), 1)

    steps(0, levels, shift, 4)


def finish_kernel(
    levels, sown, pre, x3, y3, d3, it, codes, got, tables,
    updated, coarse, xw, xl, yv, ys, sm, up, co, sems,
):
    line = levels + PAD
    planes = levels + 2
    side = lax.axis_index("depth")
    first_x = lax.axis_index("lx") == 0
    first_y = lax.axis_index("ly") == 0
    last_x = lax.axis_index("lx") == lax.axis_size("lx") - 1
    last_y = lax.axis_index("ly") == lax.axis_size("ly") - 1
    row, lane = row_index(), lane_index()
    wl = jnp.where(first_x & (row == 0), 0.0, 0.5).astype(F32)
    wu = jnp.where(last_x & (row == 7), 0.0, 0.5).astype(F32)
    wl0 = jnp.where(first_x, 0.0, 0.5).astype(F32)
    vl0 = jnp.where(first_y, 0.0, 0.5).astype(F32)
    line_lane = lax.broadcasted_iota(jnp.int32, (line, LANES), 1)
    line_vu = jnp.where(last_y & (line_lane == 127), 0.0, 0.5).astype(F32)
    line_vl = jnp.where(line_lane >= 1, 0.5, 0.0).astype(F32)

    corner = [lengthen(d3[k], ROWS) for k in range(8)]
    for c in range(4):
        last_row = lengthen(x3[(2 * c + 1) * planes : (2 * c + 2) * planes, :], line)
        xl[c] = roll_lanes(last_row, 1)
        ys[c] = jnp.where(row < 1, roll_rows(corner[c], -1), roll_rows(y3[c], 1))

    def place(n):
        z = level_of(side, n, levels)
        for c in range(4):
            x = jnp.where(row < 1, xl[c, pl.ds(n, 1), :], pre[n, c])
            x = jnp.where(lane < 1, roll_lanes(ys[c], -2 * n - 1), x)
            up[z, c] = it[z, c] + x

    steps(0, levels, place, 4)
    send_updated = pltpu.make_async_copy(up, updated, sems.at[0])
    send_updated.start()

    for k in range(8):
        far, near = [
            line_sum(lengthen(x3[(2 * k + r) * planes : (2 * k + r + 1) * planes, :], line))
            for r in range(2)
        ]
        g0, g1 = wl0 * far, 0.5 * near
        for r, (g, b) in enumerate(((g0, near + g0), (g1, g1))):
            h = g + line_vl * roll_lanes(b, 1)
            at = (2 * k + r) * line
            xw[at : at + line, :] = jnp.where(line_lane >= 1, roll_lanes(h, 1), 0.0) + line_vu * b
        w2 = lane_sum(y3[k])
        wd = lane_sum(corner[k])
        w0 = jnp.where(row < 2, wd, roll_rows(w2, 2))
        w1 = jnp.where(row < 1, roll_rows(wd, -1), roll_rows(w2, 1))
        g = wl * w0 + wu * w2
        b = w1 + g
        h = g + vl0 * roll_lanes(b, 1)
        yv[k] = jnp.where(lane % 2 == 0, roll_lanes(h, -1), 0.5 * b)

    def smooth(n, code):
        sums = []
        for k in range(8):
            beyond = xw[pl.ds(2 * k * line + n, ROWS, stride=line), :]
            value = sown[n, k] + jnp.where(row < 2, beyond, 0.0)
            sums.append(value + jnp.where(lane < 2, roll_lanes(yv[k], -2 * n), 0.0))
        half = 0.5 * activity(code)
        flow = apply_sym(lookup(tables, 0, code, half), sums[:4])
        for c in range(4):
            sm[n + 1, c] = flow[c] + half * sums[4 + c]

    for c in range(4):
        sm[0, c] = zero()
    steps(0, levels, lambda n: smooth(n, codes[n]), 4)
    smooth(levels, got[39].astype(jnp.int32))

    step = 1 - 2 * side
    for k in range(levels // 2):
        at = side * (levels + 1) + step * 2 * k
        for c in range(4):
            co[k, c] = sm[at + step, c] + 0.5 * (sm[at, c] + sm[at + 2 * step, c])
    send_coarse = pltpu.make_async_copy(co, coarse, sems.at[1])
    send_coarse.start()
    send_updated.wait()
    send_coarse.wait()


def call(kernel, outs, *args, scratch=(), far_in=False, far_out=False):
    vmem = pl.BlockSpec(memory_space=pltpu.VMEM)
    if far_in:
        args = [pltpu.with_memory_space_constraint(x, pltpu.HBM) for x in args]
    far = pl.BlockSpec(memory_space=pltpu.HBM)
    return pl.pallas_call(
        kernel,
        out_shape=[jax.ShapeDtypeStruct(s, t) for s, t in outs],
        in_specs=[far if far_in else vmem] * len(args),
        out_specs=[far if far_out else vmem] * len(outs),
        scratch_shapes=list(scratch),
        compiler_params=pltpu.CompilerParams(vmem_limit_bytes=VMEM_LIMIT),
    )(*args)


def around(x, dx, dy):
    nx, ny = lax.axis_size("lx"), lax.axis_size("ly")
    pairs = [
        (i * ny + j, ((i + dx) % nx) * ny + (j + dy) % ny) for i in range(nx) for j in range(ny)
    ]
    return lax.ppermute(x, ("lx", "ly"), pairs)


def swap(x):
    return lax.ppermute(x, "depth", [(0, 1), (1, 0)])


def local(iterate, right_side, storage, zones, counts, materials):
    levels = zones.shape[0]
    line, planes = levels + PAD, levels + 2
    tile = (ROWS, LANES)
    vmem = lambda *shape: pltpu.VMEM(shape, F32)
    tables = jnp.broadcast_to(
        materials.transpose(0, 2, 3, 1).reshape(32, ROWS, 1), (32, ROWS, LANES)
    )
    it, rt, st, codes, xm, ym, dm = call(
        functools.partial(pack_kernel, levels),
        [((levels, 4) + tile, F32), ((levels, 4) + tile, F32), ((levels,) + tile, F32),
         ((levels,) + tile, jnp.int32),
         ((15, levels, LANES), F32), ((10,) + tile, F32), ((10, 2, LANES), F32)],
        iterate, right_side, storage, zones, counts,
        scratch=[
            pltpu.VMEM((levels,) + tile, jnp.int32), pltpu.VMEM(tile, jnp.int32),
            pltpu.SemaphoreType.DMA((5,)),
        ],
        far_in=True,
    )
    xm_in, ym_in, dm_in = around(xm, -1, 0), around(ym, 0, -1), around(dm, -1, -1)
    sown, pre = call(
        functools.partial(own_kernel, levels),
        [((levels + 1, SUMMED) + tile, F32), ((levels, 10) + tile, F32)],
        it, rt, st, codes, tables,
        scratch=[vmem(levels + 3, SUMMED, *tile)],
    )
    gains, rests, message, codes_s = call(
        functools.partial(sweep_kernel, levels),
        [((levels - 1, 16) + tile, F32), ((levels - 1, 4) + tile, F32), ((MESSAGE,) + tile, F32),
         ((levels,) + tile, jnp.int32)],
        sown, pre, xm_in, ym_in, dm_in, codes, tables,
        scratch=[
            vmem((2 * SUMMED + 12) * line, LANES), vmem(10, levels, LANES),
            vmem(SUMMED, *tile), vmem(10, *tile),
            vmem(planes, 4, *tile), vmem(levels, 4, *tile), vmem(levels, *tile),
            vmem(levels, 10, *tile), vmem(levels + 1, 10, *tile), vmem(levels, 4, *tile),
        ],
    )
    got = swap(message)
    xs, kx, x3, y3, d3 = call(
        functools.partial(back_kernel, levels),
        [((planes, 4) + tile, F32), ((planes, 4) + tile, F32),
         ((16 * planes, LANES), F32), ((8,) + tile, F32), ((8, 2, LANES), F32)],
        gains, rests, message, got, codes_s, tables,
    )
    x3_in, y3_in, d3_in = around(x3, 1, 0), around(y3, 0, 1), around(d3, 1, 1)
    sown3, pre3 = call(
        functools.partial(own_back_kernel, levels),
        [((levels + 1, 8) + tile, F32), ((levels, 4) + tile, F32)],
        xs, kx,
    )
    updated, coarse = call(
        functools.partial(finish_kernel, levels),
        [((levels, 4) + tile, F32), ((levels // 2, 4) + tile, F32)],
        sown3, pre3, x3_in, y3_in, d3_in, it, codes, got, tables,
        scratch=[
            vmem((16 + 6) * line, LANES), vmem(4, line, LANES), vmem(8, *tile), vmem(4, *tile),
            vmem(levels + 2, 4, *tile), vmem(levels, 4, *tile), vmem(levels // 2, 4, *tile),
            pltpu.SemaphoreType.DMA((2,)),
        ],
        far_out=True,
    )
    return updated, coarse


def solution(mesh):
    placed = (
        P("depth", None, "lx", "ly"),
        P("depth", None, "lx", "ly"),
        P("depth", "lx", "ly"),
        P("depth", "lx", "ly"),
        P("lx", "ly"),
        P(),
    )
    return jax.shard_map(
        local,
        mesh=mesh,
        in_specs=placed,
        out_specs=(P("depth", None, "lx", "ly"), P("depth", None, "lx", "ly")),
        check_vma=False,
    )
```

time: 42.7 us -> 33.9 us (0.79)
  local copies, waits for them, and re-layouts: 5.8 us -> 0.8 us
  waiting for transfers between devices: 11.4 us -> 7.51 us
  Pallas kernels: 13.2 us -> 14 us
  other arithmetic: 0.73 us -> 0 us
    unnamed x14 -> x0, local copies, waits for them, and re-layouts: 4.27 us -> none
    ppermute x6, waiting for transfers between devices: 9.11 us -> 6.01 us  [around(): return lax.ppermute(x, ('lx', 'ly'), pairs)]
    pallas_call x5 -> x6, Pallas kernels: 13.2 us -> 14 us  [call(): pl.pallas_call(kernel, out_shape=[jax.ShapeDtypeStruct(s, t) for s, t in...]
    ppermute x2 -> x1, waiting for transfers between devices: 2.31 us -> 1.5 us  [swap(): return lax.ppermute(x, 'depth', [(0, 1), (1, 0)])]
    ppermute x6, starting transfers between devices: 9.77 us -> 10.5 us  [around(): return lax.ppermute(x, ('lx', 'ly'), pairs)]
    squeeze x1 -> x0, local copies, waits for them, and re-layouts: 0.73 us -> none  [local(): plane = lax.dynamic_index_in_dim(iterate, near, 0, False)]
    broadcast_in_dim x1 -> x0, other arithmetic: 0.72 us -> none  [local(): jnp.where(z + side * levels < counts, lax.dynamic_index_in_dim(zones, z,...]
    ppermute x2 -> x1, starting transfers between devices: 0.58 us -> 0.07 us  [swap(): return lax.ppermute(x, 'depth', [(0, 1), (1, 0)])]
  transfers between devices with their start and end apart: 8 -> 7, of which waited for: 4 -> 3; matrix products, arithmetic and copies ran while one was open for 2% -> 2% of each run, Pallas kernels for 1% -> 14%
where the time goes in v1:
time: 33.9 us; the launch traced here: 33.6 us
  Pallas kernels  14 us (41%)
  starting transfers between devices  10.6 us (31%)
  waiting for transfers between devices  7.51 us (22%)
  local copies, waits for them, and re-layouts  0.8 us (2%)
  between operations  0.68 us (2%)
    pallas_call x6, Pallas kernels, call(): pl.pallas_call(kernel, out_shape=[jax.ShapeDtypeStruct(s, t) for s, t in...  14 us
    ppermute x6, starting transfers between devices, around(): return lax.ppermute(x, ('lx', 'ly'), pairs)  10.5 us
    ppermute x6, waiting for transfers between devices, around(): return lax.ppermute(x, ('lx', 'ly'), pairs)  6.01 us
    ppermute x1, waiting for transfers between devices, swap(): return lax.ppermute(x, 'depth', [(0, 1), (1, 0)])  1.5 us
    broadcast_in_dim x1, local copies, waits for them, and re-layouts, local(): jnp.broadcast_to(materials.transpose(0, 2, 3, 1).reshape(32, ROWS, 1), (3...  0.8 us
  transfers between devices with their start and end apart: 7, of which 3 were waited for; matrix products, arithmetic and copies ran while one was open for 2% of the time, Pallas kernels for 14%

profile of v1, /device:TPU:0, one launch (start us, length us, event | category | flops | bytes accessed | tf_op | source)
XLA Modules:
  0.0 33.6 jit_solution(398637006063934619)
XLA Ops:
  0.6 1.4 %shard_map.77 = (f32[16,4,8,128]{3,2,1,0:T(8,128)S(1)}, f32[16,4,8,128]{3,2,1,0:T(8,128)S(1)}, f32[16,8,128]{2,1,0:T(8,128)S(1)}, s32[16,8,128]{2,1,0:T(8,128)S(...) custom-call(f32[16,4,8,128]{3,2,1,0:T(8,128)} %iterate.1, ...), custom_call_target="tpu_custom_call" | custom-call | tf_op jit(solution)/shard_map/pallas_call | solution.py:568
  2.0 3.9 %collective-permute-start = (f32[15,16,128]{2,1,0:T(8,128)S(1)}, f32[15,16,128]{2,1,0:T(8,128)S(1)}, u32[]{:S(2)}, u32[]{:S(2)}) collective-permute-start(f32[15,16,128]{2,1,0:T(8,128)S(1)} %get-tuple-element.28), channel_id=1, source_target_pairs={{0,12},{1,13},{2,14},{3,15},{4,0},{5,1},{6,2},{7,3},{8,4},{9,5},{1... | collective-permute-start | bytes 368648 | tf_op jit(solution)/shard_map/ppermute | solution.py:583
  6.0 3.6 %collective-permute-start.1 = (f32[10,8,128]{2,1,0:T(8,128)S(1)}, f32[10,8,128]{2,1,0:T(8,128)S(1)}, u32[]{:S(2)}, u32[]{:S(2)}) collective-permute-start(f32[10,8,128]{2,1,0:T(8,128)S(1)} %get-tuple-element.29), channel_id=1, source_target_pairs={{0,3},{1,0},{2,1},{3,2},{4,7},{5,4},{6,5},{7,6},{8,11},{9,8},{10,9... | collective-permute-start | bytes 122888 | tf_op jit(solution)/shard_map/ppermute | solution.py:583
  9.6 0.4 %collective-permute-start.2 = (f32[10,2,128]{2,1,0:T(2,128)S(1)}, f32[10,2,128]{2,1,0:T(2,128)S(1)}, u32[]{:S(2)}, u32[]{:S(2)}) collective-permute-start(f32[10,2,128]{2,1,0:T(2,128)S(1)} %get-tuple-element.30), channel_id=1, source_target_pairs={{0,15},{1,12},{2,13},{3,14},{4,3},{5,0},{6,1},{7,2},{8,7},{9,4},{1... | collective-permute-start | bytes 30728 | tf_op jit(solution)/shard_map/ppermute | solution.py:583
  10.0 0.8 %broadcast_in_dim.8.tables = f32[32,8,128]{2,1,0:T(8,128)S(1)} broadcast(f32[32,8]{1,0:T(8,128)} %bitcast.3), dimensions={0,1} | broadcast | bytes 132096 | tf_op jit(solution)/shard_map/broadcast_in_dim | solution.py:595
  10.8 2.8 %shard_map.78 = (f32[17,19,8,128]{3,2,1,0:T(8,128)S(1)}, f32[16,10,8,128]{3,2,1,0:T(8,128)S(1)}) custom-call(f32[16,4,8,128]{3,2,1,0:T(8,128)S(1)} %get-tuple-element.22.it, f32[16,4,8,128]{3,2,1,0:T(8,128)S(1)} %get-tuple-element.23.rt, f32[16,8,128]{2,1,0:T(8,128)S(1)} %get-tuple-element.24.st, s32[16,8,128]{2,1,0:T(8,128)S(1)} %get-tuple-element.25.codes, ...), custom_call_target="tpu_custom_call" | custom-call | tf_op jit(solution)/shard_map/pallas_call | solution.py:568
  13.6 0.6 %collective-permute-done.2.dm = f32[10,2,128]{2,1,0:T(2,128)S(1)} collective-permute-done((f32[10,2,128]{2,1,0:T(2,128)S(1)}, f32[10,2,128]{2,1,0:T(2,128)S(1)}, u32[]{:S(2)}, u32[]{:S(2)}) %collective-permute-start.2) | collective-permute-done | bytes 10272 | tf_op jit(solution)/shard_map/ppermute | solution.py:583
  14.1 0.0 collective-permute-done.1.ym
  14.1 0.0 collective-permute-done.xm
  14.1 5.5 %shard_map.79 = (f32[15,16,8,128]{3,2,1,0:T(8,128)S(1)}, f32[15,4,8,128]{3,2,1,0:T(8,128)S(1)}, f32[60,8,128]{2,1,0:T(8,128)S(1)}, s32[16,8,128]{2,1,0:T(8,128)S(1)}) custom-call(f32[17,19,8,128]{3,2,1,0:T(8,128)S(1)} %get-tuple-element.26.sown, f32[16,10,8,128]{3,2,1,0:T(8,128)S(1)} %get-tuple-element.27.pre, f32[15,16,128]{2,1,0:T(8,128)S(1)} %collective-permute-done.xm, ...), custom_call_target="tpu_custom_call" | custom-call | tf_op jit(solution)/shard_map/pallas_call | solution.py:568
  19.7 0.1 collective-permute-start.3
  19.8 1.5 %collective-permute-done.3.got = f32[60,8,128]{2,1,0:T(8,128)S(1)} collective-permute-done((f32[60,8,128]{2,1,0:T(8,128)S(1)}, f32[60,8,128]{2,1,0:T(8,128)S(1)}, u32[]{:S(2)}, u32[]{:S(2)}) %collective-permute-start.3) | collective-permute-done | bytes 245792 | tf_op jit(solution)/shard_map/ppermute | solution.py:587
  21.2 0.6 %shard_map.80 = (f32[18,4,8,128]{3,2,1,0:T(8,128)S(1)}, f32[18,4,8,128]{3,2,1,0:T(8,128)S(1)}, f32[288,128]{1,0:T(8,128)S(1)}, f32[8,8,128]{2,1,0:T(8,128)S(1)}, f32[8,2,128]{2,1,0:T(2,128)S(1)}) custom-call(f32[15,16,8,128]{3,2,1,0:T(8,128)S(1)} %get-tuple-element.31.gains, f32[15,4,8,128]{3,2,1,0:T(8,128)S(1)} %get-tuple-element.32.rests, ...), custom_call_target="tpu_custom_call" | custom-call | tf_op jit(solution)/shard_map/pallas_call | solution.py:568
  21.8 1.0 %collective-permute-start.4 = (f32[288,128]{1,0:T(8,128)S(1)}, f32[288,128]{1,0:T(8,128)S(1)}, u32[]{:S(2)}, u32[]{:S(2)}) collective-permute-start(f32[288,128]{1,0:T(8,128)S(1)} %get-tuple-element.39), channel_id=1, source_target_pairs={{0,4},{1,5},{2,6},{3,7},{4,8},{5,9},{6,10},{7,11},{8,12},{9,13},{1... | collective-permute-start | bytes 442376 | tf_op jit(solution)/shard_map/ppermute | solution.py:583
  22.8 1.6 %collective-permute-start.5 = (f32[8,8,128]{2,1,0:T(8,128)S(1)}, f32[8,8,128]{2,1,0:T(8,128)S(1)}, u32[]{:S(2)}, u32[]{:S(2)}) collective-permute-start(f32[8,8,128]{2,1,0:T(8,128)S(1)} %get-tuple-element.40), channel_id=1, source_target_pairs={{0,1},{1,2},{2,3},{3,0},{4,5},{5,6},{6,7},{7,4},{8,9},{9,10},{10,1... | collective-permute-start | bytes 98312 | tf_op jit(solution)/shard_map/ppermute | solution.py:583
  24.4 0.0 collective-permute-start.6
  24.4 1.8 %shard_map.81 = (f32[17,8,8,128]{3,2,1,0:T(8,128)S(1)}, f32[16,4,8,128]{3,2,1,0:T(8,128)S(1)}) custom-call(f32[18,4,8,128]{3,2,1,0:T(8,128)S(1)} %get-tuple-element.35.xs, f32[18,4,8,128]{3,2,1,0:T(8,128)S(1)} %get-tuple-element.36.kx), custom_call_target="tpu_custom_call" | custom-call | tf_op jit(solution)/shard_map/pallas_call | solution.py:568
  26.2 5.4 %collective-permute-done.6.d3 = f32[8,2,128]{2,1,0:T(2,128)S(1)} collective-permute-done((f32[8,2,128]{2,1,0:T(2,128)S(1)}, f32[8,2,128]{2,1,0:T(2,128)S(1)}, u32[]{:S(2)}, u32[]{:S(2)}) %collective-permute-start.6) | collective-permute-done | bytes 8224 | tf_op jit(solution)/shard_map/ppermute | solution.py:583
  31.7 0.0 collective-permute-done.5.y3
  31.7 0.0 collective-permute-done.4.x3
  31.7 2.0 %shard_map.82 = (f32[16,4,8,128]{3,2,1,0:T(8,128)}, f32[8,4,8,128]{3,2,1,0:T(8,128)}) custom-call(f32[17,8,8,128]{3,2,1,0:T(8,128)S(1)} %get-tuple-element.37.sown, f32[16,4,8,128]{3,2,1,0:T(8,128)S(1)} %get-tuple-element.38.pre, f32[288,128]{1,0:T(8,128)S(1)} %collective-permute-done.4.x3, f32[8,8,128]{2,1,0:T(8,128)S(1)} %collective-permute-done.5.y3, ...), custom_call_target="tpu_custom_call" | custom-call | tf_op jit(solution)/shard_map/pallas_call | solution.py:568
Async XLA Ops:
  2.0 12.1 %collective-permute-start = (f32[15,16,128]{2,1,0:T(8,128)S(1)}, f32[15,16,128]{2,1,0:T(8,128)S(1)}, u32[]{:S(2)}, u32[]{:S(2)}) collective-permute-start(f32[15,16,128]{2,1,0:T(8,128)S(1)} %get-tuple-element.28), channel_id=1, source_target_pairs={{0,12},{1,13},{2,14},{3,15},{4,0},{5,1},{6,2},{7,3},{8,4},{9,5},{1... | collective-permute-start | bytes 368648 | tf_op jit(solution)/shard_map/ppermute | solution.py:583
  6.0 8.2 %collective-permute-start.1 = (f32[10,8,128]{2,1,0:T(8,128)S(1)}, f32[10,8,128]{2,1,0:T(8,128)S(1)}, u32[]{:S(2)}, u32[]{:S(2)}) collective-permute-start(f32[10,8,128]{2,1,0:T(8,128)S(1)} %get-tuple-element.29), channel_id=1, source_target_pairs={{0,3},{1,0},{2,1},{3,2},{4,7},{5,4},{6,5},{7,6},{8,11},{9,8},{10,9... | collective-permute-start | bytes 122888 | tf_op jit(solution)/shard_map/ppermute | solution.py:583
  9.6 4.6 %collective-permute-start.2 = (f32[10,2,128]{2,1,0:T(2,128)S(1)}, f32[10,2,128]{2,1,0:T(2,128)S(1)}, u32[]{:S(2)}, u32[]{:S(2)}) collective-permute-start(f32[10,2,128]{2,1,0:T(2,128)S(1)} %get-tuple-element.30), channel_id=1, source_target_pairs={{0,15},{1,12},{2,13},{3,14},{4,3},{5,0},{6,1},{7,2},{8,7},{9,4},{1... | collective-permute-start | bytes 30728 | tf_op jit(solution)/shard_map/ppermute | solution.py:583
  19.7 1.6 %collective-permute-start.3 = (f32[60,8,128]{2,1,0:T(8,128)S(1)}, f32[60,8,128]{2,1,0:T(8,128)S(1)}, u32[]{:S(2)}, u32[]{:S(2)}) collective-permute-start(f32[60,8,128]{2,1,0:T(8,128)S(1)} %get-tuple-element.33.message), channel_id=1, source_target_pairs={{0,16},{16,0},{1,17},{17,1},{2,18},{18,2},{3,19},{19,3},{4,20},{20... | collective-permute-start | bytes 737288 | tf_op jit(solution)/shard_map/ppermute | solution.py:587
  21.8 9.8 %collective-permute-start.4 = (f32[288,128]{1,0:T(8,128)S(1)}, f32[288,128]{1,0:T(8,128)S(1)}, u32[]{:S(2)}, u32[]{:S(2)}) collective-permute-start(f32[288,128]{1,0:T(8,128)S(1)} %get-tuple-element.39), channel_id=1, source_target_pairs={{0,4},{1,5},{2,6},{3,7},{4,8},{5,9},{6,10},{7,11},{8,12},{9,13},{1... | collective-permute-start | bytes 442376 | tf_op jit(solution)/shard_map/ppermute | solution.py:583
  22.8 8.8 %collective-permute-start.5 = (f32[8,8,128]{2,1,0:T(8,128)S(1)}, f32[8,8,128]{2,1,0:T(8,128)S(1)}, u32[]{:S(2)}, u32[]{:S(2)}) collective-permute-start(f32[8,8,128]{2,1,0:T(8,128)S(1)} %get-tuple-element.40), channel_id=1, source_target_pairs={{0,1},{1,2},{2,3},{3,0},{4,5},{5,6},{6,7},{7,4},{8,9},{9,10},{10,1... | collective-permute-start | bytes 98312 | tf_op jit(solution)/shard_map/ppermute | solution.py:583
  24.4 7.2 %collective-permute-start.6 = (f32[8,2,128]{2,1,0:T(2,128)S(1)}, f32[8,2,128]{2,1,0:T(2,128)S(1)}, u32[]{:S(2)}, u32[]{:S(2)}) collective-permute-start(f32[8,2,128]{2,1,0:T(2,128)S(1)} %get-tuple-element.41), channel_id=1, source_target_pairs={{0,5},{1,6},{2,7},{3,4},{4,9},{5,10},{6,11},{7,8},{8,13},{9,14},{1... | collective-permute-start | bytes 24584 | tf_op jit(solution)/shard_map/ppermute | solution.py:583

commit v2 on v1

--- a/solution.py
+++ b/solution.py
@@ -40,7 +40,7 @@
     return jnp.where(codes > 0, 1.0, 0.0).astype(F32)
 
 
-def lookup(tables, kind, codes, act):
+def lookup(tables, kind, codes):
     rows = jnp.maximum(codes - 1, 0)
     found = []
     for i, j in PAIRS:
@@ -49,8 +49,7 @@
             jnp.take_along_axis(table, rows[at : at + ROWS], axis=0, mode="promise_in_bounds")
             for at in range(0, rows.shape[0], ROWS)
         ]
-        value = parts[0] if len(parts) == 1 else jnp.concatenate(parts, axis=0)
-        found.append(value * act)
+        found.append(parts[0] if len(parts) == 1 else jnp.concatenate(parts, axis=0))
     return found
 
 
@@ -66,7 +65,7 @@
 
 def summed_fields(tables, codes, field):
     act = activity(codes)
-    lateral = lookup(tables, 0, codes, act)
+    lateral = [act * value for value in lookup(tables, 0, codes)]
     return [act] + lateral + [act * v for v in field] + apply_sym(lateral, field)
 
 
@@ -133,7 +132,7 @@
     wl = jnp.where(last_x & (row == 7), 0.0, 0.5).astype(F32)
     wu = jnp.where(row < 6, 0.5, 0.0).astype(F32)
     vl = jnp.where(last_y & (lane == 127), 0.0, 0.5).astype(F32)
-    vu = jnp.where(lane < 127, 0.5, 0.0).astype(F32)
+    vu = jnp.where(lane < 126, 0.5, 0.0).astype(F32)
     for k in range(SUMMED):
         u[0, k] = zero()
         u[levels + 1, k] = zero()
@@ -161,8 +160,7 @@
             w = u[n + 1, k] + 0.5 * (u[n, k] + u[n + 2, k])
             g = wl * w + wu * roll_rows(w, -2)
             b = jnp.where(row < 7, roll_rows(w, -1), 0.0) + g
-            h = g + vu * roll_lanes(b, -1)
-            sown[n, k] = jnp.where(lane < 127, roll_lanes(h, -1), 0.0) + vl * b
+            sown[n, k] = jnp.where(lane < 127, roll_lanes(g, -1), 0.0) + (vu * roll_lanes(b, -2) + vl * b)
 
     steps(0, levels + 1, gather, 2)
 
@@ -227,67 +225,77 @@
     return jnp.concatenate([values, jnp.zeros((rows - values.shape[0], LANES), F32)], axis=0)
 
 
+def line_kernel(levels, sown, pre, xm, tables, sums, moved, xw, xl):
+    line = levels + PAD
+    last_x = lax.axis_index("lx") == lax.axis_size("lx") - 1
+    last_y = lax.axis_index("ly") == lax.axis_size("ly") - 1
+    row = row_index()
+    wu6 = jnp.where(last_x, 0.0, 0.5).astype(F32)
+    lane = lax.broadcasted_iota(jnp.int32, (line, LANES), 1)
+    vl = jnp.where(last_y & (lane == 127), 0.0, 0.5).astype(F32)
+    vu = jnp.where(lane < 126, 0.5, 0.0).astype(F32)
+    lines = []
+    for r in range(2):
+        codes = lengthen(xm[10 * r], line).astype(jnp.int32)
+        lines.append(summed_fields(tables, codes, [lengthen(xm[10 * r + 1 + c], line) for c in range(4)]))
+    for k in range(SUMMED):
+        x8, x9 = line_sum(lines[0][k]), line_sum(lines[1][k])
+        g6, g7 = wu6 * x8, 0.5 * x9
+        for r, (g, b) in enumerate(((g6, g6), (g7, x8 + g7))):
+            at = (2 * k + r + 6) * line
+            xw[at : at + line, :] = jnp.where(lane < 127, roll_lanes(g, -1), 0.0) + (
+                vu * roll_lanes(b, -2) + vl * b
+            )
+    for k in range(10):
+        xl[k] = roll_lanes(xm[k], -1)
+
+    def add(n):
+        for k in range(SUMMED):
+            beyond = xw[pl.ds(2 * k * line + n, ROWS, stride=line), :]
+            sums[n, k] = sown[n, k] + jnp.where(row >= 6, beyond, 0.0)
+
+    def fill(n):
+        for k in range(10):
+            moved[n, k] = jnp.where(row == 7, xl[k, pl.ds(n, 1), :], pre[n, k])
+
+    steps(0, levels + 1, add, 2)
+    steps(0, levels, fill, 2)
+
+
 def sweep_kernel(
-    levels, sown, pre, xm, ym, dm, codes, tables,
+    levels, sown, pre, ym, dm, codes, tables,
     gains, rests, message, codes_s,
-    xw, xl, yv, ys, fs, rs, ss, ps, ms, qs,
+    yv, ys, fs, rs, ss, ps, ms, qs,
 ):
-    line = levels + PAD
     last_x = lax.axis_index("lx") == lax.axis_size("lx") - 1
     last_y = lax.axis_index("ly") == lax.axis_size("ly") - 1
     row, lane = row_index(), lane_index()
     wl = jnp.where(last_x & (row == 7), 0.0, 0.5).astype(F32)
     wu = jnp.where(last_x & (row == 6), 0.0, 0.5).astype(F32)
-    wu6 = jnp.where(last_x, 0.0, 0.5).astype(F32)
     vu127 = jnp.where(last_y, 0.0, 0.5).astype(F32)
-    top = row == 7
+    even = lane % 2 == 0
     end = lane == 127
 
-    line_lane = lax.broadcasted_iota(jnp.int32, (line, LANES), 1)
-    line_vl = jnp.where(last_y & (line_lane == 127), 0.0, 0.5).astype(F32)
-    line_vu = jnp.where(line_lane < 127, 0.5, 0.0).astype(F32)
-    lines = []
-    for r in range(2):
-        line_codes = lengthen(xm[10 * r], line).astype(jnp.int32)
-        line_field = [lengthen(xm[10 * r + 1 + c], line) for c in range(4)]
-        lines.append(summed_fields(tables, line_codes, line_field))
-    for k in range(SUMMED):
-        x8, x9 = line_sum(lines[0][k]), line_sum(lines[1][k])
-        g6, g7 = wu6 * x8, 0.5 * x9
-        for r, (g, b) in enumerate(((g6, g6), (g7, x8 + g7))):
-            h = g + line_vu * roll_lanes(b, -1)
-            at = (2 * k + r + 6) * line
-            xw[at : at + line, :] = jnp.where(line_lane < 127, roll_lanes(h, -1), 0.0) + line_vl * b
+    corner = [lengthen(dm[k], ROWS) for k in range(10)]
     for k in range(10):
-        xl[k] = roll_lanes(xm[k], -1)
-
-    corner = [lengthen(dm[k], ROWS) for k in range(10)]
+        ys[k] = roll_rows(jnp.where(row < 1, corner[k], ym[k]), -1)
     side_u = summed_fields(tables, ym[0].astype(jnp.int32), [ym[1 + c] for c in range(4)])
     corner_u = summed_fields(tables, corner[0].astype(jnp.int32), corner[1:5])
     for k in range(SUMMED):
-        w0 = lane_sum(side_u[k])
-        wd = lane_sum(corner_u[k])
-        w1 = roll_rows(jnp.where(row < 1, wd, w0), -1)
-        w2 = roll_rows(jnp.where(row < 2, wd, w0), -2)
-        g = wl * w0 + wu * w2
-        b = w1 + g
-        h = g + 0.5 * roll_lanes(b, -1)
-        yv[k] = jnp.where(lane % 2 == 0, vu127 * b, roll_lanes(h, 1))
-    for k in range(10):
-        ys[k] = roll_rows(jnp.where(row < 1, corner[k], ym[k]), -1)
-
-    def shift_level(n):
-        moved = []
-        for k in range(10):
-            value = jnp.where(top, xl[k, pl.ds(n, 1), :], pre[n, k])
-            moved.append(jnp.where(end, roll_lanes(ys[k], 127 - 2 * n), value))
+        one = roll_rows(jnp.where(row < 1, corner_u[k], side_u[k]), -1)
+        two = roll_rows(jnp.where(row < 2, corner_u[k], side_u[k]), -2)
+        g = wl * side_u[k] + wu * two
+        b = one + g
+        yv[k] = lane_sum(jnp.where(even, vu127 * b, roll_lanes(g, 1) + 0.5 * b))
+
+    def shift(n):
+        moved = [jnp.where(end, roll_lanes(ys[k], 127 - 2 * n), pre[n, k]) for k in range(10)]
         codes_s[n] = moved[0].astype(jnp.int32)
         for c in range(4):
             fs[n + 1, c] = moved[1 + c]
             rs[n, c] = moved[5 + c]
         ss[n] = moved[9]
 
-    steps(0, levels, shift_level, 2)
     for c in range(4):
         fs[0, c] = zero()
         fs[levels + 1, c] = zero()
@@ -295,50 +303,46 @@
         ms[0, k] = zero()
 
     def lateral_sums(n):
-        sums = []
-        for k in range(SUMMED):
-            beyond = xw[pl.ds(2 * k * line + n, ROWS, stride=line), :]
-            value = sown[n, k] + jnp.where(row >= 6, beyond, 0.0)
-            sums.append(value + jnp.where(lane >= 126, roll_lanes(yv[k], 126 - 2 * n), 0.0))
-        return sums
+        return [
+            sown[n, k] + jnp.where(lane >= 126, roll_lanes(yv[k], 126 - 2 * n), 0.0)
+            for k in range(SUMMED)
+        ]
 
     def assemble(n, last=False):
         sums = lateral_sums(n)
         act = activity(codes_s[n])
         half = 0.5 * act
-        lateral = lookup(tables, 0, codes_s[n], half)
+        lateral = lookup(tables, 0, codes_s[n])
         below = [ms[n, k] for k in range(10)]
         if last:
             above = [zero() for _ in range(10)]
         else:
             both = half * activity(codes_s[n + 1])
-            here = lookup(tables, 1, codes_s[n], both)
-            there = lookup(tables, 1, codes_s[n + 1], both)
-            above = [here[k] + there[k] for k in range(10)]
+            here = lookup(tables, 1, codes_s[n])
+            there = lookup(tables, 1, codes_s[n + 1])
+            above = [both * (here[k] + there[k]) for k in range(10)]
         block = []
         for k, (i, j) in enumerate(PAIRS):
-            value = (lateral[k] * sums[0] + half * sums[1 + k]) + (below[k] + above[k])
+            value = half * (lateral[k] * sums[0] + sums[1 + k]) + (below[k] + above[k])
             block.append(value + ss[n] if i == j else value)
-        for k in range(10):
-            ms[n + 1, k] = above[k]
-            ps[n, k] = block[k]
         field = [fs[n + 1, c] for c in range(4)]
         before = apply_sym(below, [fs[n, c] for c in range(4)])
         after = apply_sym(above, [fs[n + 2, c] for c in range(4)])
         diagonal = apply_sym(block, field)
         flow = apply_sym(lateral, sums[11:15])
-        for c in range(4):
-            near = (before[c] + after[c]) + (flow[c] + half * sums[15 + c])
+        for k in range(10):
+            ms[n + 1, k] = above[k]
+            ps[n, k] = block[k]
+        for c in range(4):
+            near = (before[c] + after[c]) + half * (flow[c] + sums[15 + c])
             qs[n, c] = act * (rs[n, c] - (diagonal[c] - near))
-
-    steps(0, levels - 1, assemble, 2)
-    assemble(levels - 1, True)
 
     def eliminate(n, carry):
         coupled, carried = carry
-        inverse = invert([ps[n, k] - coupled[k] for k in range(10)])
+        block = [ps[n, k] for k in range(10)]
+        link = [ms[n + 1, k] for k in range(10)]
         value = [qs[n, c] + carried[c] for c in range(4)]
-        link = [ms[n + 1, k] for k in range(10)]
+        inverse = invert([block[k] - coupled[k] for k in range(10)])
         gain = sym_product(inverse, link)
         rest = apply_sym(inverse, value)
         for i in range(4):
@@ -347,8 +351,24 @@
                 gains[n, 4 * i + j] = gain[i][j]
         return back_product(link, gain), apply_sym(link, rest)
 
+    shift(0)
+    shift(1)
+    shift(2)
+    assemble(0)
+
+    def advance(n, carry):
+        carry = eliminate(n, carry)
+        assemble(n + 1)
+        shift(n + 3)
+        return carry
+
     zeros = [zero() for _ in range(10)]
-    coupled, carried = lax.fori_loop(0, levels - 1, eliminate, (zeros, zeros[:4]))
+    carry = lax.fori_loop(0, levels - 3, advance, (zeros, zeros[:4]))
+    carry = eliminate(levels - 3, carry)
+    assemble(levels - 2)
+    carry = eliminate(levels - 2, carry)
+    assemble(levels - 1, True)
+    coupled, carried = carry
     end_n = levels - 1
     for k in range(10):
         message[k] = ps[end_n, k] - coupled[k]
@@ -386,21 +406,21 @@
 
     here, there = end_of(message), end_of(got)
     both = 0.5 * here[1] * there[1]
-    link_here = lookup(tables, 1, here[0], both)
-    link_there = lookup(tables, 1, there[0], both)
-    link = [link_here[k] + link_there[k] for k in range(10)]
+    link_here = lookup(tables, 1, here[0])
+    link_there = lookup(tables, 1, there[0])
+    link = [both * (link_here[k] + link_there[k]) for k in range(10)]
 
     def complete(one, other):
         code, act, block, value, _, field = one
         _, _, _, _, sums, field_there = other
         half = 0.5 * act
-        lateral = lookup(tables, 0, code, half)
-        added = [lateral[k] * sums[0] + half * sums[1 + k] + link[k] for k in range(10)]
+        lateral = lookup(tables, 0, code)
+        added = [half * (lateral[k] * sums[0] + sums[1 + k]) + link[k] for k in range(10)]
         across = apply_sym(link, field_there)
         flow = apply_sym(lateral, sums[11:15])
         diagonal = apply_sym(added, field)
         full = [
-            value[c] + act * ((across[c] + flow[c] + half * sums[15 + c]) - diagonal[c])
+            value[c] + act * ((across[c] + half * (flow[c] + sums[15 + c])) - diagonal[c])
             for c in range(4)
         ]
         return [block[k] + added[k] for k in range(10)], full
@@ -435,7 +455,8 @@
     for n in range(planes):
         field = [xs[n, c] for c in range(4)]
         code = codes_s[n] if n < levels else got[37 + n - levels].astype(jnp.int32)
-        flow = apply_sym(lookup(tables, 0, code, activity(code)), field)
+        act = activity(code)
+        flow = [act * value for value in apply_sym(lookup(tables, 0, code), field)]
         for c in range(4):
             kx[n, c] = flow[c]
         for k, value in enumerate(field + flow):
@@ -454,7 +475,7 @@
     row, lane = row_index(), lane_index()
     wl = jnp.where(row >= 2, 0.5, 0.0).astype(F32)
     wu = jnp.where(last_x & (row == 7), 0.0, 0.5).astype(F32)
-    vl = jnp.where(lane >= 1, 0.5, 0.0).astype(F32)
+    vl = jnp.where(lane >= 2, 0.5, 0.0).astype(F32)
     vu = jnp.where(last_y & (lane == 127), 0.0, 0.5).astype(F32)
 
     def gather(n, first=False):
@@ -464,8 +485,7 @@
             w = ref[n, c] + 0.5 * outer
             g = wl * roll_rows(w, 2) + wu * w
             b = jnp.where(row >= 1, roll_rows(w, 1), 0.0) + g
-            h = g + vl * roll_lanes(b, 1)
-            sown[n, k] = jnp.where(lane >= 1, roll_lanes(h, 1), 0.0) + vu * b
+            sown[n, k] = jnp.where(lane >= 1, roll_lanes(g, 1), 0.0) + (vl * roll_lanes(b, 2) + vu * b)
 
     gather(0, True)
     steps(1, levels + 1, gather, 2)
@@ -477,37 +497,65 @@
     steps(0, levels, shift, 4)
 
 
-def finish_kernel(
-    levels, sown, pre, x3, y3, d3, it, codes, got, tables,
-    updated, coarse, xw, xl, yv, ys, sm, up, co, sems,
-):
+def line_back_kernel(levels, sown, pre, x3, sums, moved, xw, xl):
     line = levels + PAD
     planes = levels + 2
+    first_x = lax.axis_index("lx") == 0
+    last_y = lax.axis_index("ly") == lax.axis_size("ly") - 1
+    row = row_index()
+    wl0 = jnp.where(first_x, 0.0, 0.5).astype(F32)
+    lane = lax.broadcasted_iota(jnp.int32, (line, LANES), 1)
+    vu = jnp.where(last_y & (lane == 127), 0.0, 0.5).astype(F32)
+    vl = jnp.where(lane >= 2, 0.5, 0.0).astype(F32)
+    for k in range(8):
+        far, near = [
+            lengthen(x3[(2 * k + r) * planes : (2 * k + r + 1) * planes, :], line) for r in range(2)
+        ]
+        if k < 4:
+            xl[k] = roll_lanes(near, 1)
+        far, near = line_sum(far), line_sum(near)
+        g0, g1 = wl0 * far, 0.5 * near
+        for r, (g, b) in enumerate(((g0, near + g0), (g1, g1))):
+            at = (2 * k + r) * line
+            xw[at : at + line, :] = jnp.where(lane >= 1, roll_lanes(g, 1), 0.0) + (
+                vl * roll_lanes(b, 2) + vu * b
+            )
+
+    def add(n):
+        for k in range(8):
+            beyond = xw[pl.ds(2 * k * line + n, ROWS, stride=line), :]
+            sums[n, k] = sown[n, k] + jnp.where(row < 2, beyond, 0.0)
+
+    def fill(n):
+        for c in range(4):
+            moved[n, c] = jnp.where(row < 1, xl[c, pl.ds(n, 1), :], pre[n, c])
+
+    steps(0, levels + 1, add, 4)
+    steps(0, levels, fill, 4)
+
+
+def finish_kernel(
+    levels, sown, pre, y3, d3, it, codes, got, tables,
+    updated, coarse, yv, ys, sm, up, co, sems,
+):
     side = lax.axis_index("depth")
     first_x = lax.axis_index("lx") == 0
     first_y = lax.axis_index("ly") == 0
     last_x = lax.axis_index("lx") == lax.axis_size("lx") - 1
-    last_y = lax.axis_index("ly") == lax.axis_size("ly") - 1
     row, lane = row_index(), lane_index()
     wl = jnp.where(first_x & (row == 0), 0.0, 0.5).astype(F32)
     wu = jnp.where(last_x & (row == 7), 0.0, 0.5).astype(F32)
-    wl0 = jnp.where(first_x, 0.0, 0.5).astype(F32)
     vl0 = jnp.where(first_y, 0.0, 0.5).astype(F32)
-    line_lane = lax.broadcasted_iota(jnp.int32, (line, LANES), 1)
-    line_vu = jnp.where(last_y & (line_lane == 127), 0.0, 0.5).astype(F32)
-    line_vl = jnp.where(line_lane >= 1, 0.5, 0.0).astype(F32)
+    even = lane % 2 == 0
 
     corner = [lengthen(d3[k], ROWS) for k in range(8)]
     for c in range(4):
-        last_row = lengthen(x3[(2 * c + 1) * planes : (2 * c + 2) * planes, :], line)
-        xl[c] = roll_lanes(last_row, 1)
         ys[c] = jnp.where(row < 1, roll_rows(corner[c], -1), roll_rows(y3[c], 1))
 
     def place(n):
         z = level_of(side, n, levels)
         for c in range(4):
-            x = jnp.where(row < 1, xl[c, pl.ds(n, 1), :], pre[n, c])
-            x = jnp.where(lane < 1, roll_lanes(ys[c], -2 * n - 1), x)
+            x = jnp.where(lane < 1, roll_lanes(ys[c], -2 * n - 1), pre[n, c])
             up[z, c] = it[z, c] + x
 
     steps(0, levels, place, 4)
@@ -515,34 +563,20 @@
     send_updated.start()
 
     for k in range(8):
-        far, near = [
-            line_sum(lengthen(x3[(2 * k + r) * planes : (2 * k + r + 1) * planes, :], line))
-            for r in range(2)
+        two = jnp.where(row < 2, corner[k], roll_rows(y3[k], 2))
+        one = jnp.where(row < 1, roll_rows(corner[k], -1), roll_rows(y3[k], 1))
+        g = wl * two + wu * y3[k]
+        b = one + g
+        yv[k] = lane_sum(jnp.where(even, roll_lanes(g, -1) + vl0 * b, 0.5 * b))
+
+    def smooth(n, code):
+        sums = [
+            sown[n, k] + jnp.where(lane < 2, roll_lanes(yv[k], -2 * n), 0.0) for k in range(8)
         ]
-        g0, g1 = wl0 * far, 0.5 * near
-        for r, (g, b) in enumerate(((g0, near + g0), (g1, g1))):
-            h = g + line_vl * roll_lanes(b, 1)
-            at = (2 * k + r) * line
-            xw[at : at + line, :] = jnp.where(line_lane >= 1, roll_lanes(h, 1), 0.0) + line_vu * b
-        w2 = lane_sum(y3[k])
-        wd = lane_sum(corner[k])
-        w0 = jnp.where(row < 2, wd, roll_rows(w2, 2))
-        w1 = jnp.where(row < 1, roll_rows(wd, -1), roll_rows(w2, 1))
-        g = wl * w0 + wu * w2
-        b = w1 + g
-        h = g + vl0 * roll_lanes(b, 1)
-        yv[k] = jnp.where(lane % 2 == 0, roll_lanes(h, -1), 0.5 * b)
-
-    def smooth(n, code):
-        sums = []
-        for k in range(8):
-            beyond = xw[pl.ds(2 * k * line + n, ROWS, stride=line), :]
-            value = sown[n, k] + jnp.where(row < 2, beyond, 0.0)
-            sums.append(value + jnp.where(lane < 2, roll_lanes(yv[k], -2 * n), 0.0))
         half = 0.5 * activity(code)
-        flow = apply_sym(lookup(tables, 0, code, half), sums[:4])
-        for c in range(4):
-            sm[n + 1, c] = flow[c] + half * sums[4 + c]
+        flow = apply_sym(lookup(tables, 0, code), sums[:4])
+        for c in range(4):
+            sm[n + 1, c] = half * (flow[c] + sums[4 + c])
 
     for c in range(4):
         sm[0, c] = zero()
@@ -614,13 +648,18 @@
         it, rt, st, codes, tables,
         scratch=[vmem(levels + 3, SUMMED, *tile)],
     )
+    sums, moved = call(
+        functools.partial(line_kernel, levels),
+        [((levels + 1, SUMMED) + tile, F32), ((levels, 10) + tile, F32)],
+        sown, pre, xm_in, tables,
+        scratch=[vmem((2 * SUMMED + 12) * line, LANES), vmem(10, levels, LANES)],
+    )
     gains, rests, message, codes_s = call(
         functools.partial(sweep_kernel, levels),
         [((levels - 1, 16) + tile, F32), ((levels - 1, 4) + tile, F32), ((MESSAGE,) + tile, F32),
          ((levels,) + tile, jnp.int32)],
-        sown, pre, xm_in, ym_in, dm_in, codes, tables,
+        sums, moved, ym_in, dm_in, codes, tables,
         scratch=[
-            vmem((2 * SUMMED + 12) * line, LANES), vmem(10, levels, LANES),
             vmem(SUMMED, *tile), vmem(10, *tile),
             vmem(planes, 4, *tile), vmem(levels, 4, *tile), vmem(levels, *tile),
             vmem(levels, 10, *tile), vmem(levels + 1, 10, *tile), vmem(levels, 4, *tile),
@@ -639,12 +678,18 @@
         [((levels + 1, 8) + tile, F32), ((levels, 4) + tile, F32)],
         xs, kx,
     )
+    sums3, moved3 = call(
+        functools.partial(line_back_kernel, levels),
+        [((levels + 1, 8) + tile, F32), ((levels, 4) + tile, F32)],
+        sown3, pre3, x3_in,
+        scratch=[vmem((16 + 6) * line, LANES), vmem(4, line, LANES)],
+    )
     updated, coarse = call(
         functools.partial(finish_kernel, levels),
         [((levels, 4) + tile, F32), ((levels // 2, 4) + tile, F32)],
-        sown3, pre3, x3_in, y3_in, d3_in, it, codes, got, tables,
+        sums3, moved3, y3_in, d3_in, it, codes, got, tables,
         scratch=[
-            vmem((16 + 6) * line, LANES), vmem(4, line, LANES), vmem(8, *tile), vmem(4, *tile),
+            vmem(8, *tile), vmem(4, *tile),
             vmem(levels + 2, 4, *tile), vmem(levels, 4, *tile), vmem(levels // 2, 4, *tile),
             pltpu.SemaphoreType.DMA((2,)),
         ],

time: 33.9 us -> 30.7 us (0.906)
  Pallas kernels: 14 us -> 10.8 us
  starting transfers between devices: 10.6 us -> 11.1 us
  waiting for transfers between devices: 7.51 us -> 7.14 us
    pallas_call x6 -> x8, Pallas kernels: 14 us -> 10.8 us  [call(): pl.pallas_call(kernel, out_shape=[jax.ShapeDtypeStruct(s, t) for s, t in...]
    ppermute x6, starting transfers between devices: 10.5 us -> 11 us  [around(): return lax.ppermute(x, ('lx', 'ly'), pairs)]
    ppermute x6, waiting for transfers between devices: 6.01 us -> 5.64 us  [around(): return lax.ppermute(x, ('lx', 'ly'), pairs)]
  transfers between devices with their start and end apart: 7 -> 7, of which waited for: 3 -> 4; matrix products, arithmetic and copies ran while one was open for 2% -> 3% of each run, Pallas kernels for 14% -> 16%
where the time goes in v2:
time: 30.7 us; the launch traced here: 30.5 us
  starting transfers between devices  11.1 us (36%)
  Pallas kernels  10.8 us (35%)
  waiting for transfers between devices  7.14 us (23%)
  local copies, waits for them, and re-layouts  0.8 us (3%)
  between operations  0.7 us (2%)
    ppermute x6, starting transfers between devices, around(): return lax.ppermute(x, ('lx', 'ly'), pairs)  11 us
    pallas_call x8, Pallas kernels, call(): pl.pallas_call(kernel, out_shape=[jax.ShapeDtypeStruct(s, t) for s, t in...  10.8 us
    ppermute x6, waiting for transfers between devices, around(): return lax.ppermute(x, ('lx', 'ly'), pairs)  5.64 us
    ppermute x1, waiting for transfers between devices, swap(): return lax.ppermute(x, 'depth', [(0, 1), (1, 0)])  1.5 us
    broadcast_in_dim x1, local copies, waits for them, and re-layouts, local(): jnp.broadcast_to(materials.transpose(0, 2, 3, 1).reshape(32, ROWS, 1), (3...  0.8 us
  transfers between devices with their start and end apart: 7, of which 4 were waited for; matrix products, arithmetic and copies ran while one was open for 3% of the time, Pallas kernels for 16%

profile of v2, /device:TPU:0, one launch (start us, length us, event | category | flops | bytes accessed | tf_op | source)
XLA Modules:
  0.0 30.5 jit_solution(15291732371831703545)
XLA Ops:
  0.6 1.4 %shard_map.77 = (f32[16,4,8,128]{3,2,1,0:T(8,128)S(1)}, f32[16,4,8,128]{3,2,1,0:T(8,128)S(1)}, f32[16,8,128]{2,1,0:T(8,128)S(1)}, s32[16,8,128]{2,1,0:T(8,128)S(...) custom-call(f32[16,4,8,128]{3,2,1,0:T(8,128)} %iterate.1, ...), custom_call_target="tpu_custom_call" | custom-call | tf_op jit(solution)/shard_map/pallas_call | solution.py:602
  2.0 3.9 %collective-permute-start = (f32[15,16,128]{2,1,0:T(8,128)S(1)}, f32[15,16,128]{2,1,0:T(8,128)S(1)}, u32[]{:S(2)}, u32[]{:S(2)}) collective-permute-start(f32[15,16,128]{2,1,0:T(8,128)S(1)} %get-tuple-element.32), channel_id=1, source_target_pairs={{0,12},{1,13},{2,14},{3,15},{4,0},{5,1},{6,2},{7,3},{8,4},{9,5},{1... | collective-permute-start | bytes 368648 | tf_op jit(solution)/shard_map/ppermute | solution.py:617
  6.0 3.6 %collective-permute-start.1 = (f32[10,8,128]{2,1,0:T(8,128)S(1)}, f32[10,8,128]{2,1,0:T(8,128)S(1)}, u32[]{:S(2)}, u32[]{:S(2)}) collective-permute-start(f32[10,8,128]{2,1,0:T(8,128)S(1)} %get-tuple-element.35), channel_id=1, source_target_pairs={{0,3},{1,0},{2,1},{3,2},{4,7},{5,4},{6,5},{7,6},{8,11},{9,8},{10,9... | collective-permute-start | bytes 122888 | tf_op jit(solution)/shard_map/ppermute | solution.py:617
  9.6 0.4 %collective-permute-start.2 = (f32[10,2,128]{2,1,0:T(2,128)S(1)}, f32[10,2,128]{2,1,0:T(2,128)S(1)}, u32[]{:S(2)}, u32[]{:S(2)}) collective-permute-start(f32[10,2,128]{2,1,0:T(2,128)S(1)} %get-tuple-element.36), channel_id=1, source_target_pairs={{0,15},{1,12},{2,13},{3,14},{4,3},{5,0},{6,1},{7,2},{8,7},{9,4},{1... | collective-permute-start | bytes 30728 | tf_op jit(solution)/shard_map/ppermute | solution.py:617
  10.0 0.8 %broadcast_in_dim.8.tables = f32[32,8,128]{2,1,0:T(8,128)S(1)} broadcast(f32[32,8]{1,0:T(8,128)} %bitcast.3), dimensions={0,1} | broadcast | bytes 132096 | tf_op jit(solution)/shard_map/broadcast_in_dim | solution.py:629
  10.8 2.4 %shard_map.78 = (f32[17,19,8,128]{3,2,1,0:T(8,128)S(1)}, f32[16,10,8,128]{3,2,1,0:T(8,128)S(1)}) custom-call(f32[16,4,8,128]{3,2,1,0:T(8,128)S(1)} %get-tuple-element.26.it, f32[16,4,8,128]{3,2,1,0:T(8,128)S(1)} %get-tuple-element.27.rt, f32[16,8,128]{2,1,0:T(8,128)S(1)} %get-tuple-element.28.st, s32[16,8,128]{2,1,0:T(8,128)S(1)} %get-tuple-element.29.codes, ...), custom_call_target="tpu_custom_call" | custom-call | tf_op jit(solution)/shard_map/pallas_call | solution.py:602
  13.2 0.0 collective-permute-done.xm
  13.2 0.8 %shard_map.79 = (f32[17,19,8,128]{3,2,1,0:T(8,128)S(1)}, f32[16,10,8,128]{3,2,1,0:T(8,128)S(1)}) custom-call(f32[17,19,8,128]{3,2,1,0:T(8,128)S(1)} %get-tuple-element.30.sown, f32[16,10,8,128]{3,2,1,0:T(8,128)S(1)} %get-tuple-element.31.pre, f32[15,16,128]{2,1,0:T(8,128)S(1)} %collective-permute-done.xm, f32[32,8,128]{2,1,0:T(8,128)S(1)} %broadcast_in_dim.8.tables), custom_call_target="tpu_custom_call" | custom-call | tf_op jit(solution)/shard_map/pallas_call | solution.py:602
  14.0 0.1 collective-permute-done.2.dm
  14.1 0.0 collective-permute-done.1.ym
  14.1 2.2 %shard_map.80 = (f32[15,16,8,128]{3,2,1,0:T(8,128)S(1)}, f32[15,4,8,128]{3,2,1,0:T(8,128)S(1)}, f32[60,8,128]{2,1,0:T(8,128)S(1)}, s32[16,8,128]{2,1,0:T(8,128)S(1)}) custom-call(f32[17,19,8,128]{3,2,1,0:T(8,128)S(1)} %get-tuple-element.33.sown, f32[16,10,8,128]{3,2,1,0:T(8,128)S(1)} %get-tuple-element.34.pre, f32[10,8,128]{2,1,0:T(8,128)S(1)} %collective-permute-done.1.ym, ...), custom_call_target="tpu_custom_call" | custom-call | tf_op jit(solution)/shard_map/pallas_call | solution.py:602
  16.3 0.1 collective-permute-start.3
  16.4 1.5 %collective-permute-done.3.got = f32[60,8,128]{2,1,0:T(8,128)S(1)} collective-permute-done((f32[60,8,128]{2,1,0:T(8,128)S(1)}, f32[60,8,128]{2,1,0:T(8,128)S(1)}, u32[]{:S(2)}, u32[]{:S(2)}) %collective-permute-start.3) | collective-permute-done | bytes 245792 | tf_op jit(solution)/shard_map/ppermute | solution.py:621
  17.9 0.6 %shard_map.81 = (f32[18,4,8,128]{3,2,1,0:T(8,128)S(1)}, f32[18,4,8,128]{3,2,1,0:T(8,128)S(1)}, f32[288,128]{1,0:T(8,128)S(1)}, f32[8,8,128]{2,1,0:T(8,128)S(1)}, f32[8,2,128]{2,1,0:T(2,128)S(1)}) custom-call(f32[15,16,8,128]{3,2,1,0:T(8,128)S(1)} %get-tuple-element.37.gains, f32[15,4,8,128]{3,2,1,0:T(8,128)S(1)} %get-tuple-element.38.rests, ...), custom_call_target="tpu_custom_call" | custom-call | tf_op jit(solution)/shard_map/pallas_call | solution.py:602
  18.5 1.5 %collective-permute-start.4 = (f32[288,128]{1,0:T(8,128)S(1)}, f32[288,128]{1,0:T(8,128)S(1)}, u32[]{:S(2)}, u32[]{:S(2)}) collective-permute-start(f32[288,128]{1,0:T(8,128)S(1)} %get-tuple-element.45), channel_id=1, source_target_pairs={{0,4},{1,5},{2,6},{3,7},{4,8},{5,9},{6,10},{7,11},{8,12},{9,13},{1... | collective-permute-start | bytes 442376 | tf_op jit(solution)/shard_map/ppermute | solution.py:617
  20.0 1.6 %collective-permute-start.5 = (f32[8,8,128]{2,1,0:T(8,128)S(1)}, f32[8,8,128]{2,1,0:T(8,128)S(1)}, u32[]{:S(2)}, u32[]{:S(2)}) collective-permute-start(f32[8,8,128]{2,1,0:T(8,128)S(1)} %get-tuple-element.48), channel_id=1, source_target_pairs={{0,1},{1,2},{2,3},{3,0},{4,5},{5,6},{6,7},{7,4},{8,9},{9,10},{10,1... | collective-permute-start | bytes 98312 | tf_op jit(solution)/shard_map/ppermute | solution.py:617
  21.5 0.0 collective-permute-start.6
  21.5 1.3 %shard_map.82 = (f32[17,8,8,128]{3,2,1,0:T(8,128)S(1)}, f32[16,4,8,128]{3,2,1,0:T(8,128)S(1)}) custom-call(f32[18,4,8,128]{3,2,1,0:T(8,128)S(1)} %get-tuple-element.41.xs, f32[18,4,8,128]{3,2,1,0:T(8,128)S(1)} %get-tuple-element.42.kx), custom_call_target="tpu_custom_call" | custom-call | tf_op jit(solution)/shard_map/pallas_call | solution.py:602
  22.9 2.5 %collective-permute-done.4.x3 = f32[288,128]{1,0:T(8,128)S(1)} collective-permute-done((f32[288,128]{1,0:T(8,128)S(1)}, f32[288,128]{1,0:T(8,128)S(1)}, u32[]{:S(2)}, u32[]{:S(2)}) %collective-permute-start.4) | collective-permute-done | bytes 147488 | tf_op jit(solution)/shard_map/ppermute | solution.py:617
  25.3 0.4 %shard_map.83 = (f32[17,8,8,128]{3,2,1,0:T(8,128)S(1)}, f32[16,4,8,128]{3,2,1,0:T(8,128)S(1)}) custom-call(f32[17,8,8,128]{3,2,1,0:T(8,128)S(1)} %get-tuple-element.43.sown, f32[16,4,8,128]{3,2,1,0:T(8,128)S(1)} %get-tuple-element.44.pre, f32[288,128]{1,0:T(8,128)S(1)} %collective-permute-done.4.x3), custom_call_target="tpu_custom_call" | custom-call | tf_op jit(solution)/shard_map/pallas_call | solution.py:602
  25.7 3.1 %collective-permute-done.6.d3 = f32[8,2,128]{2,1,0:T(2,128)S(1)} collective-permute-done((f32[8,2,128]{2,1,0:T(2,128)S(1)}, f32[8,2,128]{2,1,0:T(2,128)S(1)}, u32[]{:S(2)}, u32[]{:S(2)}) %collective-permute-start.6) | collective-permute-done | bytes 8224 | tf_op jit(solution)/shard_map/ppermute | solution.py:617
  28.8 0.0 collective-permute-done.5.y3
  28.8 1.7 %shard_map.84 = (f32[16,4,8,128]{3,2,1,0:T(8,128)}, f32[8,4,8,128]{3,2,1,0:T(8,128)}) custom-call(f32[17,8,8,128]{3,2,1,0:T(8,128)S(1)} %get-tuple-element.46.sown, f32[16,4,8,128]{3,2,1,0:T(8,128)S(1)} %get-tuple-element.47.pre, f32[8,8,128]{2,1,0:T(8,128)S(1)} %collective-permute-done.5.y3, f32[8,2,128]{2,1,0:T(2,128)S(1)} %collective-permute-done.6.d3, ...), custom_call_target="tpu_custom_call" | custom-call | tf_op jit(solution)/shard_map/pallas_call | solution.py:602
Async XLA Ops:
  2.0 11.2 %collective-permute-start = (f32[15,16,128]{2,1,0:T(8,128)S(1)}, f32[15,16,128]{2,1,0:T(8,128)S(1)}, u32[]{:S(2)}, u32[]{:S(2)}) collective-permute-start(f32[15,16,128]{2,1,0:T(8,128)S(1)} %get-tuple-element.32), channel_id=1, source_target_pairs={{0,12},{1,13},{2,14},{3,15},{4,0},{5,1},{6,2},{7,3},{8,4},{9,5},{1... | collective-permute-start | bytes 368648 | tf_op jit(solution)/shard_map/ppermute | solution.py:617
  6.0 8.2 %collective-permute-start.1 = (f32[10,8,128]{2,1,0:T(8,128)S(1)}, f32[10,8,128]{2,1,0:T(8,128)S(1)}, u32[]{:S(2)}, u32[]{:S(2)}) collective-permute-start(f32[10,8,128]{2,1,0:T(8,128)S(1)} %get-tuple-element.35), channel_id=1, source_target_pairs={{0,3},{1,0},{2,1},{3,2},{4,7},{5,4},{6,5},{7,6},{8,11},{9,8},{10,9... | collective-permute-start | bytes 122888 | tf_op jit(solution)/shard_map/ppermute | solution.py:617
  9.6 4.6 %collective-permute-start.2 = (f32[10,2,128]{2,1,0:T(2,128)S(1)}, f32[10,2,128]{2,1,0:T(2,128)S(1)}, u32[]{:S(2)}, u32[]{:S(2)}) collective-permute-start(f32[10,2,128]{2,1,0:T(2,128)S(1)} %get-tuple-element.36), channel_id=1, source_target_pairs={{0,15},{1,12},{2,13},{3,14},{4,3},{5,0},{6,1},{7,2},{8,7},{9,4},{1... | collective-permute-start | bytes 30728 | tf_op jit(solution)/shard_map/ppermute | solution.py:617
  16.3 1.6 %collective-permute-start.3 = (f32[60,8,128]{2,1,0:T(8,128)S(1)}, f32[60,8,128]{2,1,0:T(8,128)S(1)}, u32[]{:S(2)}, u32[]{:S(2)}) collective-permute-start(f32[60,8,128]{2,1,0:T(8,128)S(1)} %get-tuple-element.39.message), channel_id=1, source_target_pairs={{0,16},{16,0},{1,17},{17,1},{2,18},{18,2},{3,19},{19,3},{4,20},{20... | collective-permute-start | bytes 737288 | tf_op jit(solution)/shard_map/ppermute | solution.py:621
  18.5 6.8 %collective-permute-start.4 = (f32[288,128]{1,0:T(8,128)S(1)}, f32[288,128]{1,0:T(8,128)S(1)}, u32[]{:S(2)}, u32[]{:S(2)}) collective-permute-start(f32[288,128]{1,0:T(8,128)S(1)} %get-tuple-element.45), channel_id=1, source_target_pairs={{0,4},{1,5},{2,6},{3,7},{4,8},{5,9},{6,10},{7,11},{8,12},{9,13},{1... | collective-permute-start | bytes 442376 | tf_op jit(solution)/shard_map/ppermute | solution.py:617
  20.0 8.8 %collective-permute-start.5 = (f32[8,8,128]{2,1,0:T(8,128)S(1)}, f32[8,8,128]{2,1,0:T(8,128)S(1)}, u32[]{:S(2)}, u32[]{:S(2)}) collective-permute-start(f32[8,8,128]{2,1,0:T(8,128)S(1)} %get-tuple-element.48), channel_id=1, source_target_pairs={{0,1},{1,2},{2,3},{3,0},{4,5},{5,6},{6,7},{7,4},{8,9},{9,10},{10,1... | collective-permute-start | bytes 98312 | tf_op jit(solution)/shard_map/ppermute | solution.py:617
  21.5 7.2 %collective-permute-start.6 = (f32[8,2,128]{2,1,0:T(2,128)S(1)}, f32[8,2,128]{2,1,0:T(2,128)S(1)}, u32[]{:S(2)}, u32[]{:S(2)}) collective-permute-start(f32[8,2,128]{2,1,0:T(2,128)S(1)} %get-tuple-element.49), channel_id=1, source_target_pairs={{0,5},{1,6},{2,7},{3,4},{4,9},{5,10},{6,11},{7,8},{8,13},{9,14},{1... | collective-permute-start | bytes 24584 | tf_op jit(solution)/shard_map/ppermute | solution.py:617

commit v3 on v2

--- a/solution.py
+++ b/solution.py
@@ -92,7 +92,7 @@
 
 def pack_kernel(
     levels, iterate, right, storage, zones, counts,
-    it, rt, st, codes_out, xm, ym, dm, zones_v, counts_v, sems,
+    it, rt, st, codes_out, ym, dm, zones_v, counts_v, sems,
 ):
     side = lax.axis_index("depth")
     lane = lane_index()
@@ -115,13 +115,22 @@
         fields = [code.astype(F32)] + [it[z, c] for c in range(4)]
         fields += [rt[z, c] for c in range(4)] + [st[z]]
         for k, value in enumerate(fields):
-            xm[k, n : n + 1, :] = value[0:1]
-            if k < 5:
-                xm[10 + k, n : n + 1, :] = value[1:2]
             acc[k] = jnp.where(lane // 2 == n, roll_lanes(value, 2 * n), acc[k])
     for k in range(10):
         ym[k] = acc[k]
         dm[k] = acc[k][0:2]
+
+
+def pack_rows_kernel(levels, it, rt, st, codes, xm):
+    side = lax.axis_index("depth")
+    for n in range(levels):
+        z = level_of(side, n, levels)
+        fields = [codes[n].astype(F32)] + [it[z, c] for c in range(4)]
+        fields += [rt[z, c] for c in range(4)] + [st[z]]
+        for k, value in enumerate(fields):
+            xm[k, n : n + 1, :] = value[0:1]
+            if k < 5:
+                xm[10 + k, n : n + 1, :] = value[1:2]
 
 
 def own_kernel(levels, it, rt, st, codes, tables, sown, pre, u):
@@ -459,10 +468,11 @@
         flow = [act * value for value in apply_sym(lookup(tables, 0, code), field)]
         for c in range(4):
             kx[n, c] = flow[c]
-        for k, value in enumerate(field + flow):
+        for k, value in enumerate(field + [code.astype(F32)]):
             for r in range(2):
                 at = (2 * k + r) * planes + n
                 x3[at : at + 1, :] = value[6 + r : 7 + r]
+        for k, value in enumerate(field + flow):
             acc[k] = jnp.where(lane // 2 == n, roll_lanes(value, 2 * n + 2), acc[k])
     for k in range(8):
         y3[k] = acc[k]
@@ -497,7 +507,7 @@
     steps(0, levels, shift, 4)
 
 
-def line_back_kernel(levels, sown, pre, x3, sums, moved, xw, xl):
+def line_back_kernel(levels, sown, pre, x3, tables, sums, moved, xw, xl):
     line = levels + PAD
     planes = levels + 2
     first_x = lax.axis_index("lx") == 0
@@ -507,10 +517,17 @@
     lane = lax.broadcasted_iota(jnp.int32, (line, LANES), 1)
     vu = jnp.where(last_y & (lane == 127), 0.0, 0.5).astype(F32)
     vl = jnp.where(lane >= 2, 0.5, 0.0).astype(F32)
+    lines = []
+    for r in range(2):
+        parts = [
+            lengthen(x3[(2 * k + r) * planes : (2 * k + r + 1) * planes, :], line) for k in range(5)
+        ]
+        codes = parts[4].astype(jnp.int32)
+        act = activity(codes)
+        flow = apply_sym(lookup(tables, 0, codes), parts[:4])
+        lines.append(parts[:4] + [act * value for value in flow])
     for k in range(8):
-        far, near = [
-            lengthen(x3[(2 * k + r) * planes : (2 * k + r + 1) * planes, :], line) for r in range(2)
-        ]
+        far, near = lines[0][k], lines[1][k]
         if k < 4:
             xl[k] = roll_lanes(near, 1)
         far, near = line_sum(far), line_sum(near)
@@ -629,17 +646,20 @@
     tables = jnp.broadcast_to(
         materials.transpose(0, 2, 3, 1).reshape(32, ROWS, 1), (32, ROWS, LANES)
     )
-    it, rt, st, codes, xm, ym, dm = call(
+    it, rt, st, codes, ym, dm = call(
         functools.partial(pack_kernel, levels),
         [((levels, 4) + tile, F32), ((levels, 4) + tile, F32), ((levels,) + tile, F32),
          ((levels,) + tile, jnp.int32),
-         ((15, levels, LANES), F32), ((10,) + tile, F32), ((10, 2, LANES), F32)],
+         ((10,) + tile, F32), ((10, 2, LANES), F32)],
         iterate, right_side, storage, zones, counts,
         scratch=[
             pltpu.VMEM((levels,) + tile, jnp.int32), pltpu.VMEM(tile, jnp.int32),
             pltpu.SemaphoreType.DMA((5,)),
         ],
         far_in=True,
+    )
+    xm, = call(
+        functools.partial(pack_rows_kernel, levels), [((15, levels, LANES), F32)], it, rt, st, codes
     )
     xm_in, ym_in, dm_in = around(xm, -1, 0), around(ym, 0, -1), around(dm, -1, -1)
     sown, pre = call(
@@ -669,7 +689,7 @@
     xs, kx, x3, y3, d3 = call(
         functools.partial(back_kernel, levels),
         [((planes, 4) + tile, F32), ((planes, 4) + tile, F32),
-         ((16 * planes, LANES), F32), ((8,) + tile, F32), ((8, 2, LANES), F32)],
+         ((10 * planes, LANES), F32), ((8,) + tile, F32), ((8, 2, LANES), F32)],
         gains, rests, message, got, codes_s, tables,
     )
     x3_in, y3_in, d3_in = around(x3, 1, 0), around(y3, 0, 1), around(d3, 1, 1)
@@ -681,7 +701,7 @@
     sums3, moved3 = call(
         functools.partial(line_back_kernel, levels),
         [((levels + 1, 8) + tile, F32), ((levels, 4) + tile, F32)],
-        sown3, pre3, x3_in,
+        sown3, pre3, x3_in, tables,
         scratch=[vmem((16 + 6) * line, LANES), vmem(4, line, LANES)],
     )
     updated, coarse = call(

time: 30.7 us -> 30 us (0.977)
  local copies, waits for them, and re-layouts: 0.8 us -> 0.09 us
  waiting for transfers between devices: 7.14 us -> 7.85 us
  starting transfers between devices: 11.1 us -> 10.4 us
    ppermute x6, starting transfers between devices: 11 us -> 10.3 us  [around(): return lax.ppermute(x, ('lx', 'ly'), pairs)]
    broadcast_in_dim x1, local copies, waits for them, and re-layouts: 0.8 us -> 0.09 us  [local(): jnp.broadcast_to(materials.transpose(0, 2, 3, 1).reshape(32, ROWS, 1), (3...]
    ppermute x6, waiting for transfers between devices: 5.64 us -> 6.35 us  [around(): return lax.ppermute(x, ('lx', 'ly'), pairs)]
    pallas_call x8 -> x9, Pallas kernels: 10.8 us -> 10.8 us  [call(): pl.pallas_call(kernel, out_shape=[jax.ShapeDtypeStruct(s, t) for s, t in...]
  transfers between devices with their start and end apart: 7 -> 7, of which waited for: 4 -> 4; matrix products, arithmetic and copies ran while one was open for 3% -> 0% of each run, Pallas kernels for 16% -> 16%
where the time goes in v3:
time: 30 us; the launch traced here: 29.9 us
  Pallas kernels  10.8 us (36%)
  starting transfers between devices  10.4 us (35%)
  waiting for transfers between devices  7.85 us (26%)
  between operations  0.72 us (2%)
    pallas_call x9, Pallas kernels, call(): pl.pallas_call(kernel, out_shape=[jax.ShapeDtypeStruct(s, t) for s, t in...  10.8 us
    ppermute x6, starting transfers between devices, around(): return lax.ppermute(x, ('lx', 'ly'), pairs)  10.3 us
    ppermute x6, waiting for transfers between devices, around(): return lax.ppermute(x, ('lx', 'ly'), pairs)  6.35 us
    ppermute x1, waiting for transfers between devices, swap(): return lax.ppermute(x, 'depth', [(0, 1), (1, 0)])  1.5 us
  transfers between devices with their start and end apart: 7, of which 4 were waited for; matrix products, arithmetic and copies ran while one was open for 0% of the time, Pallas kernels for 16%

profile of v3, /device:TPU:0, one launch (start us, length us, event | category | flops | bytes accessed | tf_op | source)
XLA Modules:
  0.0 29.9 jit_solution(9778256709945321907)
XLA Ops:
  0.6 0.0 copy-start
  0.6 1.4 %shard_map.77 = (f32[16,4,8,128]{3,2,1,0:T(8,128)S(1)}, f32[16,4,8,128]{3,2,1,0:T(8,128)S(1)}, f32[16,8,128]{2,1,0:T(8,128)S(1)}, s32[16,8,128]{2,1,0:T(8,128)S(...) custom-call(f32[16,4,8,128]{3,2,1,0:T(8,128)} %iterate.1, f32[16,4,8,128]{3,2,1,0:T(8,128)} %right.1, ...), custom_call_target="tpu_custom_call" | custom-call | tf_op jit(solution)/shard_map/pallas_call | solution.py:619
  2.0 0.1 shard_map.79
  2.1 3.9 %collective-permute-start = (f32[15,16,128]{2,1,0:T(8,128)S(1)}, f32[15,16,128]{2,1,0:T(8,128)S(1)}, u32[]{:S(2)}, u32[]{:S(2)}) collective-permute-start(f32[15,16,128]{2,1,0:T(8,128)S(1)} %shard_map.79), channel_id=1, source_target_pairs={{0,12},{1,13},{2,14},{3,15},{4,0},{5,1},{6,2},{7,3},{8,4},{9,5},{1... | collective-permute-start | bytes 368648 | tf_op jit(solution)/shard_map/ppermute | solution.py:634
  6.0 3.6 %collective-permute-start.1 = (f32[10,8,128]{2,1,0:T(8,128)S(1)}, f32[10,8,128]{2,1,0:T(8,128)S(1)}, u32[]{:S(2)}, u32[]{:S(2)}) collective-permute-start(f32[10,8,128]{2,1,0:T(8,128)S(1)} %get-tuple-element.33), channel_id=1, source_target_pairs={{0,3},{1,0},{2,1},{3,2},{4,7},{5,4},{6,5},{7,6},{8,11},{9,8},{10,9... | collective-permute-start | bytes 122888 | tf_op jit(solution)/shard_map/ppermute | solution.py:634
  9.6 0.4 %collective-permute-start.2 = (f32[10,2,128]{2,1,0:T(2,128)S(1)}, f32[10,2,128]{2,1,0:T(2,128)S(1)}, u32[]{:S(2)}, u32[]{:S(2)}) collective-permute-start(f32[10,2,128]{2,1,0:T(2,128)S(1)} %get-tuple-element.34), channel_id=1, source_target_pairs={{0,15},{1,12},{2,13},{3,14},{4,3},{5,0},{6,1},{7,2},{8,7},{9,4},{1... | collective-permute-start | bytes 30728 | tf_op jit(solution)/shard_map/ppermute | solution.py:634
  10.1 0.0 copy-done
  10.1 0.1 broadcast_in_dim.8.tables
  10.2 2.4 %shard_map.78 = (f32[17,19,8,128]{3,2,1,0:T(8,128)S(1)}, f32[16,10,8,128]{3,2,1,0:T(8,128)S(1)}) custom-call(f32[16,4,8,128]{3,2,1,0:T(8,128)S(1)} %get-tuple-element.25.it, f32[16,4,8,128]{3,2,1,0:T(8,128)S(1)} %get-tuple-element.26.rt, f32[16,8,128]{2,1,0:T(8,128)S(1)} %get-tuple-element.27.st, s32[16,8,128]{2,1,0:T(8,128)S(1)} %get-tuple-element.28.codes, ...), custom_call_target="tpu_custom_call" | custom-call | tf_op jit(solution)/shard_map/pallas_call | solution.py:619
  12.5 0.0 collective-permute-done.xm
  12.5 0.8 %shard_map.80 = (f32[17,19,8,128]{3,2,1,0:T(8,128)S(1)}, f32[16,10,8,128]{3,2,1,0:T(8,128)S(1)}) custom-call(f32[17,19,8,128]{3,2,1,0:T(8,128)S(1)} %get-tuple-element.29.sown, f32[16,10,8,128]{3,2,1,0:T(8,128)S(1)} %get-tuple-element.30.pre, f32[15,16,128]{2,1,0:T(8,128)S(1)} %collective-permute-done.xm, f32[32,8,128]{2,1,0:T(8,128)S(1)} %broadcast_in_dim.8.tables), custom_call_target="tpu_custom_call" | custom-call | tf_op jit(solution)/shard_map/pallas_call | solution.py:619
  13.4 0.8 %collective-permute-done.2.dm = f32[10,2,128]{2,1,0:T(2,128)S(1)} collective-permute-done((f32[10,2,128]{2,1,0:T(2,128)S(1)}, f32[10,2,128]{2,1,0:T(2,128)S(1)}, u32[]{:S(2)}, u32[]{:S(2)}) %collective-permute-start.2) | collective-permute-done | bytes 10272 | tf_op jit(solution)/shard_map/ppermute | solution.py:634
  14.2 0.0 collective-permute-done.1.ym
  14.2 2.2 %shard_map.81 = (f32[15,16,8,128]{3,2,1,0:T(8,128)S(1)}, f32[15,4,8,128]{3,2,1,0:T(8,128)S(1)}, f32[60,8,128]{2,1,0:T(8,128)S(1)}, s32[16,8,128]{2,1,0:T(8,128)S(1)}) custom-call(f32[17,19,8,128]{3,2,1,0:T(8,128)S(1)} %get-tuple-element.31.sown, f32[16,10,8,128]{3,2,1,0:T(8,128)S(1)} %get-tuple-element.32.pre, f32[10,8,128]{2,1,0:T(8,128)S(1)} %collective-permute-done.1.ym, ...), custom_call_target="tpu_custom_call" | custom-call | tf_op jit(solution)/shard_map/pallas_call | solution.py:619
  16.4 0.1 collective-permute-start.3
  16.5 1.5 %collective-permute-done.3.got = f32[60,8,128]{2,1,0:T(8,128)S(1)} collective-permute-done((f32[60,8,128]{2,1,0:T(8,128)S(1)}, f32[60,8,128]{2,1,0:T(8,128)S(1)}, u32[]{:S(2)}, u32[]{:S(2)}) %collective-permute-start.3) | collective-permute-done | bytes 245792 | tf_op jit(solution)/shard_map/ppermute | solution.py:638
  18.0 0.6 %shard_map.82 = (f32[18,4,8,128]{3,2,1,0:T(8,128)S(1)}, f32[18,4,8,128]{3,2,1,0:T(8,128)S(1)}, f32[180,128]{1,0:T(8,128)S(1)}, f32[8,8,128]{2,1,0:T(8,128)S(1)}, f32[8,2,128]{2,1,0:T(2,128)S(1)}) custom-call(f32[15,16,8,128]{3,2,1,0:T(8,128)S(1)} %get-tuple-element.35.gains, f32[15,4,8,128]{3,2,1,0:T(8,128)S(1)} %get-tuple-element.36.rests, ...), custom_call_target="tpu_custom_call" | custom-call | tf_op jit(solution)/shard_map/pallas_call | solution.py:619
  18.6 0.7 %collective-permute-start.4 = (f32[180,128]{1,0:T(8,128)S(1)}, f32[180,128]{1,0:T(8,128)S(1)}, u32[]{:S(2)}, u32[]{:S(2)}) collective-permute-start(f32[180,128]{1,0:T(8,128)S(1)} %get-tuple-element.43), channel_id=1, source_target_pairs={{0,4},{1,5},{2,6},{3,7},{4,8},{5,9},{6,10},{7,11},{8,12},{9,13},{1... | collective-permute-start | bytes 276488 | tf_op jit(solution)/shard_map/ppermute | solution.py:634
  19.3 1.6 %collective-permute-start.5 = (f32[8,8,128]{2,1,0:T(8,128)S(1)}, f32[8,8,128]{2,1,0:T(8,128)S(1)}, u32[]{:S(2)}, u32[]{:S(2)}) collective-permute-start(f32[8,8,128]{2,1,0:T(8,128)S(1)} %get-tuple-element.46), channel_id=1, source_target_pairs={{0,1},{1,2},{2,3},{3,0},{4,5},{5,6},{6,7},{7,4},{8,9},{9,10},{10,1... | collective-permute-start | bytes 98312 | tf_op jit(solution)/shard_map/ppermute | solution.py:634
  20.9 0.0 collective-permute-start.6
  20.9 1.3 %shard_map.83 = (f32[17,8,8,128]{3,2,1,0:T(8,128)S(1)}, f32[16,4,8,128]{3,2,1,0:T(8,128)S(1)}) custom-call(f32[18,4,8,128]{3,2,1,0:T(8,128)S(1)} %get-tuple-element.39.xs, f32[18,4,8,128]{3,2,1,0:T(8,128)S(1)} %get-tuple-element.40.kx), custom_call_target="tpu_custom_call" | custom-call | tf_op jit(solution)/shard_map/pallas_call | solution.py:619
  22.2 2.1 %collective-permute-done.4.x3 = f32[180,128]{1,0:T(8,128)S(1)} collective-permute-done((f32[180,128]{1,0:T(8,128)S(1)}, f32[180,128]{1,0:T(8,128)S(1)}, u32[]{:S(2)}, u32[]{:S(2)}) %collective-permute-start.4) | collective-permute-done | bytes 92192 | tf_op jit(solution)/shard_map/ppermute | solution.py:634
  24.3 0.4 %shard_map.84 = (f32[17,8,8,128]{3,2,1,0:T(8,128)S(1)}, f32[16,4,8,128]{3,2,1,0:T(8,128)S(1)}) custom-call(f32[17,8,8,128]{3,2,1,0:T(8,128)S(1)} %get-tuple-element.41.sown, f32[16,4,8,128]{3,2,1,0:T(8,128)S(1)} %get-tuple-element.42.pre, f32[180,128]{1,0:T(8,128)S(1)} %collective-permute-done.4.x3, f32[32,8,128]{2,1,0:T(8,128)S(1)} %broadcast_in_dim.8.tables), custom_call_target="tpu_custom_call" | custom-call | tf_op jit(solution)/shard_map/pallas_call | solution.py:619
  24.7 3.5 %collective-permute-done.6.d3 = f32[8,2,128]{2,1,0:T(2,128)S(1)} collective-permute-done((f32[8,2,128]{2,1,0:T(2,128)S(1)}, f32[8,2,128]{2,1,0:T(2,128)S(1)}, u32[]{:S(2)}, u32[]{:S(2)}) %collective-permute-start.6) | collective-permute-done | bytes 8224 | tf_op jit(solution)/shard_map/ppermute | solution.py:634
  28.1 0.0 collective-permute-done.5.y3
  28.1 1.7 %shard_map.85 = (f32[16,4,8,128]{3,2,1,0:T(8,128)}, f32[8,4,8,128]{3,2,1,0:T(8,128)}) custom-call(f32[17,8,8,128]{3,2,1,0:T(8,128)S(1)} %get-tuple-element.44.sown, f32[16,4,8,128]{3,2,1,0:T(8,128)S(1)} %get-tuple-element.45.pre, f32[8,8,128]{2,1,0:T(8,128)S(1)} %collective-permute-done.5.y3, f32[8,2,128]{2,1,0:T(2,128)S(1)} %collective-permute-done.6.d3, ...), custom_call_target="tpu_custom_call" | custom-call | tf_op jit(solution)/shard_map/pallas_call | solution.py:619
Async XLA Ops:
  0.6 9.4 %copy-start = (f32[2,8,4,4]{1,3,2,0:T(4,128)S(1)}, f32[2,8,4,4]{1,3,2,0:T(4,128)}, u32[]{:S(2)}) copy-start(f32[2,8,4,4]{1,3,2,0:T(4,128)} %param.11) | copy-start | bytes 3076
  2.1 10.4 %collective-permute-start = (f32[15,16,128]{2,1,0:T(8,128)S(1)}, f32[15,16,128]{2,1,0:T(8,128)S(1)}, u32[]{:S(2)}, u32[]{:S(2)}) collective-permute-start(f32[15,16,128]{2,1,0:T(8,128)S(1)} %shard_map.79), channel_id=1, source_target_pairs={{0,12},{1,13},{2,14},{3,15},{4,0},{5,1},{6,2},{7,3},{8,4},{9,5},{1... | collective-permute-start | bytes 368648 | tf_op jit(solution)/shard_map/ppermute | solution.py:634
  6.0 8.2 %collective-permute-start.1 = (f32[10,8,128]{2,1,0:T(8,128)S(1)}, f32[10,8,128]{2,1,0:T(8,128)S(1)}, u32[]{:S(2)}, u32[]{:S(2)}) collective-permute-start(f32[10,8,128]{2,1,0:T(8,128)S(1)} %get-tuple-element.33), channel_id=1, source_target_pairs={{0,3},{1,0},{2,1},{3,2},{4,7},{5,4},{6,5},{7,6},{8,11},{9,8},{10,9... | collective-permute-start | bytes 122888 | tf_op jit(solution)/shard_map/ppermute | solution.py:634
  9.6 4.6 %collective-permute-start.2 = (f32[10,2,128]{2,1,0:T(2,128)S(1)}, f32[10,2,128]{2,1,0:T(2,128)S(1)}, u32[]{:S(2)}, u32[]{:S(2)}) collective-permute-start(f32[10,2,128]{2,1,0:T(2,128)S(1)} %get-tuple-element.34), channel_id=1, source_target_pairs={{0,15},{1,12},{2,13},{3,14},{4,3},{5,0},{6,1},{7,2},{8,7},{9,4},{1... | collective-permute-start | bytes 30728 | tf_op jit(solution)/shard_map/ppermute | solution.py:634
  16.4 1.6 %collective-permute-start.3 = (f32[60,8,128]{2,1,0:T(8,128)S(1)}, f32[60,8,128]{2,1,0:T(8,128)S(1)}, u32[]{:S(2)}, u32[]{:S(2)}) collective-permute-start(f32[60,8,128]{2,1,0:T(8,128)S(1)} %get-tuple-element.37.message), channel_id=1, source_target_pairs={{0,16},{16,0},{1,17},{17,1},{2,18},{18,2},{3,19},{19,3},{4,20},{20... | collective-permute-start | bytes 737288 | tf_op jit(solution)/shard_map/ppermute | solution.py:638
  18.6 5.7 %collective-permute-start.4 = (f32[180,128]{1,0:T(8,128)S(1)}, f32[180,128]{1,0:T(8,128)S(1)}, u32[]{:S(2)}, u32[]{:S(2)}) collective-permute-start(f32[180,128]{1,0:T(8,128)S(1)} %get-tuple-element.43), channel_id=1, source_target_pairs={{0,4},{1,5},{2,6},{3,7},{4,8},{5,9},{6,10},{7,11},{8,12},{9,13},{1... | collective-permute-start | bytes 276488 | tf_op jit(solution)/shard_map/ppermute | solution.py:634
  19.3 8.8 %collective-permute-start.5 = (f32[8,8,128]{2,1,0:T(8,128)S(1)}, f32[8,8,128]{2,1,0:T(8,128)S(1)}, u32[]{:S(2)}, u32[]{:S(2)}) collective-permute-start(f32[8,8,128]{2,1,0:T(8,128)S(1)} %get-tuple-element.46), channel_id=1, source_target_pairs={{0,1},{1,2},{2,3},{3,0},{4,5},{5,6},{6,7},{7,4},{8,9},{9,10},{10,1... | collective-permute-start | bytes 98312 | tf_op jit(solution)/shard_map/ppermute | solution.py:634
  20.9 7.2 %collective-permute-start.6 = (f32[8,2,128]{2,1,0:T(2,128)S(1)}, f32[8,2,128]{2,1,0:T(2,128)S(1)}, u32[]{:S(2)}, u32[]{:S(2)}) collective-permute-start(f32[8,2,128]{2,1,0:T(2,128)S(1)} %get-tuple-element.47), channel_id=1, source_target_pairs={{0,5},{1,6},{2,7},{3,4},{4,9},{5,10},{6,11},{7,8},{8,13},{9,14},{1... | collective-permute-start | bytes 24584 | tf_op jit(solution)/shard_map/ppermute | solution.py:634

commit v4 on v3

--- a/solution.py
+++ b/solution.py
@@ -115,10 +115,10 @@
         fields = [code.astype(F32)] + [it[z, c] for c in range(4)]
         fields += [rt[z, c] for c in range(4)] + [st[z]]
         for k, value in enumerate(fields):
-            acc[k] = jnp.where(lane // 2 == n, roll_lanes(value, 2 * n), acc[k])
+            acc[k] = jnp.where(lane // 2 == n, roll_lanes(value, 2 * n + 2), acc[k])
     for k in range(10):
         ym[k] = acc[k]
-        dm[k] = acc[k][0:2]
+        dm[k] = acc[k][6:8]
 
 
 def pack_rows_kernel(levels, it, rt, st, codes, xm):
@@ -128,20 +128,20 @@
         fields = [codes[n].astype(F32)] + [it[z, c] for c in range(4)]
         fields += [rt[z, c] for c in range(4)] + [st[z]]
         for k, value in enumerate(fields):
-            xm[k, n : n + 1, :] = value[0:1]
+            xm[k, n : n + 1, :] = value[7:8]
             if k < 5:
-                xm[10 + k, n : n + 1, :] = value[1:2]
+                xm[10 + k, n : n + 1, :] = value[6:7]
 
 
 def own_kernel(levels, it, rt, st, codes, tables, sown, pre, u):
     side = lax.axis_index("depth")
-    last_x = lax.axis_index("lx") == lax.axis_size("lx") - 1
-    last_y = lax.axis_index("ly") == lax.axis_size("ly") - 1
+    first_x = lax.axis_index("lx") == 0
+    first_y = lax.axis_index("ly") == 0
     row, lane = row_index(), lane_index()
-    wl = jnp.where(last_x & (row == 7), 0.0, 0.5).astype(F32)
-    wu = jnp.where(row < 6, 0.5, 0.0).astype(F32)
-    vl = jnp.where(last_y & (lane == 127), 0.0, 0.5).astype(F32)
-    vu = jnp.where(lane < 126, 0.5, 0.0).astype(F32)
+    wl = jnp.where(row >= 2, 0.5, 0.0).astype(F32)
+    wu = jnp.where(first_x & (row == 0), 0.0, 0.5).astype(F32)
+    vl = jnp.where(lane >= 2, 0.5, 0.0).astype(F32)
+    vu = jnp.where(first_y & (lane == 0), 0.0, 0.5).astype(F32)
     for k in range(SUMMED):
         u[0, k] = zero()
         u[levels + 1, k] = zero()
@@ -160,16 +160,16 @@
         fields = [codes[n].astype(F32)] + [it[z, c] for c in range(4)]
         fields += [rt[z, c] for c in range(4)] + [st[z]]
         for k, value in enumerate(fields):
-            pre[n, k] = roll_lanes(roll_rows(value, -1), -1)
+            pre[n, k] = roll_lanes(roll_rows(value, 1), 1)
 
     steps(0, levels, shift, 2)
 
     def gather(n):
         for k in range(SUMMED):
             w = u[n + 1, k] + 0.5 * (u[n, k] + u[n + 2, k])
-            g = wl * w + wu * roll_rows(w, -2)
-            b = jnp.where(row < 7, roll_rows(w, -1), 0.0) + g
-            sown[n, k] = jnp.where(lane < 127, roll_lanes(g, -1), 0.0) + (vu * roll_lanes(b, -2) + vl * b)
+            g = wl * roll_rows(w, 2) + wu * w
+            b = jnp.where(row >= 1, roll_rows(w, 1), 0.0) + g
+            sown[n, k] = jnp.where(lane >= 1, roll_lanes(g, 1), 0.0) + (vl * roll_lanes(b, 2) + vu * b)
 
     steps(0, levels + 1, gather, 2)
 
@@ -236,36 +236,36 @@
 
 def line_kernel(levels, sown, pre, xm, tables, sums, moved, xw, xl):
     line = levels + PAD
-    last_x = lax.axis_index("lx") == lax.axis_size("lx") - 1
-    last_y = lax.axis_index("ly") == lax.axis_size("ly") - 1
+    first_x = lax.axis_index("lx") == 0
+    first_y = lax.axis_index("ly") == 0
     row = row_index()
-    wu6 = jnp.where(last_x, 0.0, 0.5).astype(F32)
+    wl1 = jnp.where(first_x, 0.0, 0.5).astype(F32)
     lane = lax.broadcasted_iota(jnp.int32, (line, LANES), 1)
-    vl = jnp.where(last_y & (lane == 127), 0.0, 0.5).astype(F32)
-    vu = jnp.where(lane < 126, 0.5, 0.0).astype(F32)
+    vl = jnp.where(lane >= 2, 0.5, 0.0).astype(F32)
+    vu = jnp.where(first_y & (lane == 0), 0.0, 0.5).astype(F32)
     lines = []
     for r in range(2):
         codes = lengthen(xm[10 * r], line).astype(jnp.int32)
         lines.append(summed_fields(tables, codes, [lengthen(xm[10 * r + 1 + c], line) for c in range(4)]))
     for k in range(SUMMED):
-        x8, x9 = line_sum(lines[0][k]), line_sum(lines[1][k])
-        g6, g7 = wu6 * x8, 0.5 * x9
-        for r, (g, b) in enumerate(((g6, g6), (g7, x8 + g7))):
-            at = (2 * k + r + 6) * line
-            xw[at : at + line, :] = jnp.where(lane < 127, roll_lanes(g, -1), 0.0) + (
-                vu * roll_lanes(b, -2) + vl * b
+        near, far = line_sum(lines[0][k]), line_sum(lines[1][k])
+        g0, g1 = 0.5 * far, wl1 * near
+        for r, (g, b) in enumerate(((g0, near + g0), (g1, g1))):
+            at = (2 * k + r) * line
+            xw[at : at + line, :] = jnp.where(lane >= 1, roll_lanes(g, 1), 0.0) + (
+                vl * roll_lanes(b, 2) + vu * b
             )
     for k in range(10):
-        xl[k] = roll_lanes(xm[k], -1)
+        xl[k] = roll_lanes(xm[k], 1)
 
     def add(n):
         for k in range(SUMMED):
             beyond = xw[pl.ds(2 * k * line + n, ROWS, stride=line), :]
-            sums[n, k] = sown[n, k] + jnp.where(row >= 6, beyond, 0.0)
+            sums[n, k] = sown[n, k] + jnp.where(row < 2, beyond, 0.0)
 
     def fill(n):
         for k in range(10):
-            moved[n, k] = jnp.where(row == 7, xl[k, pl.ds(n, 1), :], pre[n, k])
+            moved[n, k] = jnp.where(row < 1, xl[k, pl.ds(n, 1), :], pre[n, k])
 
     steps(0, levels + 1, add, 2)
     steps(0, levels, fill, 2)
@@ -276,29 +276,28 @@
     gains, rests, message, codes_s,
     yv, ys, fs, rs, ss, ps, ms, qs,
 ):
-    last_x = lax.axis_index("lx") == lax.axis_size("lx") - 1
-    last_y = lax.axis_index("ly") == lax.axis_size("ly") - 1
+    first_x = lax.axis_index("lx") == 0
+    first_y = lax.axis_index("ly") == 0
     row, lane = row_index(), lane_index()
-    wl = jnp.where(last_x & (row == 7), 0.0, 0.5).astype(F32)
-    wu = jnp.where(last_x & (row == 6), 0.0, 0.5).astype(F32)
-    vu127 = jnp.where(last_y, 0.0, 0.5).astype(F32)
+    wl = jnp.where(first_x & (row == 1), 0.0, 0.5).astype(F32)
+    wu = jnp.where(first_x & (row == 0), 0.0, 0.5).astype(F32)
+    vl1 = jnp.where(first_y, 0.0, 0.5).astype(F32)
     even = lane % 2 == 0
-    end = lane == 127
 
     corner = [lengthen(dm[k], ROWS) for k in range(10)]
     for k in range(10):
-        ys[k] = roll_rows(jnp.where(row < 1, corner[k], ym[k]), -1)
+        ys[k] = jnp.where(row < 1, roll_rows(corner[k], -1), roll_rows(ym[k], 1))
     side_u = summed_fields(tables, ym[0].astype(jnp.int32), [ym[1 + c] for c in range(4)])
     corner_u = summed_fields(tables, corner[0].astype(jnp.int32), corner[1:5])
     for k in range(SUMMED):
-        one = roll_rows(jnp.where(row < 1, corner_u[k], side_u[k]), -1)
-        two = roll_rows(jnp.where(row < 2, corner_u[k], side_u[k]), -2)
-        g = wl * side_u[k] + wu * two
+        one = jnp.where(row < 1, roll_rows(corner_u[k], -1), roll_rows(side_u[k], 1))
+        two = jnp.where(row < 2, corner_u[k], roll_rows(side_u[k], 2))
+        g = wl * two + wu * side_u[k]
         b = one + g
-        yv[k] = lane_sum(jnp.where(even, vu127 * b, roll_lanes(g, 1) + 0.5 * b))
+        yv[k] = lane_sum(jnp.where(even, roll_lanes(g, -1) + 0.5 * b, vl1 * b))
 
     def shift(n):
-        moved = [jnp.where(end, roll_lanes(ys[k], 127 - 2 * n), pre[n, k]) for k in range(10)]
+        moved = [jnp.where(lane < 1, roll_lanes(ys[k], -2 * n - 1), pre[n, k]) for k in range(10)]
         codes_s[n] = moved[0].astype(jnp.int32)
         for c in range(4):
             fs[n + 1, c] = moved[1 + c]
@@ -313,7 +312,7 @@
 
     def lateral_sums(n):
         return [
-            sown[n, k] + jnp.where(lane >= 126, roll_lanes(yv[k], 126 - 2 * n), 0.0)
+            sown[n, k] + jnp.where(lane < 2, roll_lanes(yv[k], -2 * n), 0.0)
             for k in range(SUMMED)
         ]
 
@@ -471,38 +470,38 @@
         for k, value in enumerate(field + [code.astype(F32)]):
             for r in range(2):
                 at = (2 * k + r) * planes + n
-                x3[at : at + 1, :] = value[6 + r : 7 + r]
+                x3[at : at + 1, :] = value[r : r + 1]
         for k, value in enumerate(field + flow):
-            acc[k] = jnp.where(lane // 2 == n, roll_lanes(value, 2 * n + 2), acc[k])
+            acc[k] = jnp.where(lane // 2 == n, roll_lanes(value, 2 * n), acc[k])
     for k in range(8):
         y3[k] = acc[k]
-        d3[k] = acc[k][6:8]
+        d3[k] = acc[k][0:2]
 
 
 def own_back_kernel(levels, xs, kx, sown, pre):
-    last_x = lax.axis_index("lx") == lax.axis_size("lx") - 1
-    last_y = lax.axis_index("ly") == lax.axis_size("ly") - 1
+    first_x = lax.axis_index("lx") == 0
+    first_y = lax.axis_index("ly") == 0
     row, lane = row_index(), lane_index()
-    wl = jnp.where(row >= 2, 0.5, 0.0).astype(F32)
-    wu = jnp.where(last_x & (row == 7), 0.0, 0.5).astype(F32)
-    vl = jnp.where(lane >= 2, 0.5, 0.0).astype(F32)
-    vu = jnp.where(last_y & (lane == 127), 0.0, 0.5).astype(F32)
+    wl = jnp.where(first_x & (row == 0), 0.0, 0.5).astype(F32)
+    wu = jnp.where(row < 6, 0.5, 0.0).astype(F32)
+    vl = jnp.where(first_y & (lane == 0), 0.0, 0.5).astype(F32)
+    vu = jnp.where(lane < 126, 0.5, 0.0).astype(F32)
 
     def gather(n, first=False):
         for k in range(8):
             ref, c = (xs, k) if k < 4 else (kx, k - 4)
             outer = ref[n + 1, c] if first else ref[n - 1, c] + ref[n + 1, c]
             w = ref[n, c] + 0.5 * outer
-            g = wl * roll_rows(w, 2) + wu * w
-            b = jnp.where(row >= 1, roll_rows(w, 1), 0.0) + g
-            sown[n, k] = jnp.where(lane >= 1, roll_lanes(g, 1), 0.0) + (vl * roll_lanes(b, 2) + vu * b)
+            g = wl * w + wu * roll_rows(w, -2)
+            b = jnp.where(row < 7, roll_rows(w, -1), 0.0) + g
+            sown[n, k] = jnp.where(lane < 127, roll_lanes(g, -1), 0.0) + (vu * roll_lanes(b, -2) + vl * b)
 
     gather(0, True)
     steps(1, levels + 1, gather, 2)
 
     def shift(n):
         for c in range(4):
-            pre[n, c] = roll_lanes(roll_rows(xs[n, c], 1), 1)
+            pre[n, c] = roll_lanes(roll_rows(xs[n, c], -1), -1)
 
     steps(0, levels, shift, 4)
 
@@ -510,13 +509,13 @@
 def line_back_kernel(levels, sown, pre, x3, tables, sums, moved, xw, xl):
     line = levels + PAD
     planes = levels + 2
-    first_x = lax.axis_index("lx") == 0
-    last_y = lax.axis_index("ly") == lax.axis_size("ly") - 1
+    last_x = lax.axis_index("lx") == lax.axis_size("lx") - 1
+    first_y = lax.axis_index("ly") == 0
     row = row_index()
-    wl0 = jnp.where(first_x, 0.0, 0.5).astype(F32)
+    wu7 = jnp.where(last_x, 0.0, 0.5).astype(F32)
     lane = lax.broadcasted_iota(jnp.int32, (line, LANES), 1)
-    vu = jnp.where(last_y & (lane == 127), 0.0, 0.5).astype(F32)
-    vl = jnp.where(lane >= 2, 0.5, 0.0).astype(F32)
+    vl = jnp.where(first_y & (lane == 0), 0.0, 0.5).astype(F32)
+    vu = jnp.where(lane < 126, 0.5, 0.0).astype(F32)
     lines = []
     for r in range(2):
         parts = [
@@ -527,25 +526,25 @@
         flow = apply_sym(lookup(tables, 0, codes), parts[:4])
         lines.append(parts[:4] + [act * value for value in flow])
     for k in range(8):
-        far, near = lines[0][k], lines[1][k]
+        near, far = lines[0][k], lines[1][k]
         if k < 4:
-            xl[k] = roll_lanes(near, 1)
-        far, near = line_sum(far), line_sum(near)
-        g0, g1 = wl0 * far, 0.5 * near
-        for r, (g, b) in enumerate(((g0, near + g0), (g1, g1))):
-            at = (2 * k + r) * line
-            xw[at : at + line, :] = jnp.where(lane >= 1, roll_lanes(g, 1), 0.0) + (
-                vl * roll_lanes(b, 2) + vu * b
+            xl[k] = roll_lanes(near, -1)
+        near, far = line_sum(near), line_sum(far)
+        g6, g7 = 0.5 * near, wu7 * far
+        for r, (g, b) in enumerate(((g6, g6), (g7, near + g7))):
+            at = (2 * k + r + 6) * line
+            xw[at : at + line, :] = jnp.where(lane < 127, roll_lanes(g, -1), 0.0) + (
+                vu * roll_lanes(b, -2) + vl * b
             )
 
     def add(n):
         for k in range(8):
             beyond = xw[pl.ds(2 * k * line + n, ROWS, stride=line), :]
-            sums[n, k] = sown[n, k] + jnp.where(row < 2, beyond, 0.0)
+            sums[n, k] = sown[n, k] + jnp.where(row >= 6, beyond, 0.0)
 
     def fill(n):
         for c in range(4):
-            moved[n, c] = jnp.where(row < 1, xl[c, pl.ds(n, 1), :], pre[n, c])
+            moved[n, c] = jnp.where(row == 7, xl[c, pl.ds(n, 1), :], pre[n, c])
 
     steps(0, levels + 1, add, 4)
     steps(0, levels, fill, 4)
@@ -557,22 +556,22 @@
 ):
     side = lax.axis_index("depth")
     first_x = lax.axis_index("lx") == 0
-    first_y = lax.axis_index("ly") == 0
+    last_y = lax.axis_index("ly") == lax.axis_size("ly") - 1
     last_x = lax.axis_index("lx") == lax.axis_size("lx") - 1
     row, lane = row_index(), lane_index()
     wl = jnp.where(first_x & (row == 0), 0.0, 0.5).astype(F32)
     wu = jnp.where(last_x & (row == 7), 0.0, 0.5).astype(F32)
-    vl0 = jnp.where(first_y, 0.0, 0.5).astype(F32)
+    vu127 = jnp.where(last_y, 0.0, 0.5).astype(F32)
     even = lane % 2 == 0
 
     corner = [lengthen(d3[k], ROWS) for k in range(8)]
     for c in range(4):
-        ys[c] = jnp.where(row < 1, roll_rows(corner[c], -1), roll_rows(y3[c], 1))
+        ys[c] = roll_rows(jnp.where(row < 1, corner[c], y3[c]), -1)
 
     def place(n):
         z = level_of(side, n, levels)
         for c in range(4):
-            x = jnp.where(lane < 1, roll_lanes(ys[c], -2 * n - 1), pre[n, c])
+            x = jnp.where(lane == 127, roll_lanes(ys[c], 127 - 2 * n), pre[n, c])
             up[z, c] = it[z, c] + x
 
     steps(0, levels, place, 4)
@@ -580,15 +579,15 @@
     send_updated.start()
 
     for k in range(8):
-        two = jnp.where(row < 2, corner[k], roll_rows(y3[k], 2))
-        one = jnp.where(row < 1, roll_rows(corner[k], -1), roll_rows(y3[k], 1))
-        g = wl * two + wu * y3[k]
+        two = roll_rows(jnp.where(row < 2, corner[k], y3[k]), -2)
+        one = roll_rows(jnp.where(row < 1, corner[k], y3[k]), -1)
+        g = wl * y3[k] + wu * two
         b = one + g
-        yv[k] = lane_sum(jnp.where(even, roll_lanes(g, -1) + vl0 * b, 0.5 * b))
+        yv[k] = lane_sum(jnp.where(even, 0.5 * b, roll_lanes(g, 1) + vu127 * b))
 
     def smooth(n, code):
         sums = [
-            sown[n, k] + jnp.where(lane < 2, roll_lanes(yv[k], -2 * n), 0.0) for k in range(8)
+            sown[n, k] + jnp.where(lane >= 126, roll_lanes(yv[k], 126 - 2 * n), 0.0) for k in range(8)
         ]
         half = 0.5 * activity(code)
         flow = apply_sym(lookup(tables, 0, code), sums[:4])
@@ -661,7 +660,7 @@
     xm, = call(
         functools.partial(pack_rows_kernel, levels), [((15, levels, LANES), F32)], it, rt, st, codes
     )
-    xm_in, ym_in, dm_in = around(xm, -1, 0), around(ym, 0, -1), around(dm, -1, -1)
+    xm_in, ym_in, dm_in = around(xm, 1, 0), around(ym, 0, 1), around(dm, 1, 1)
     sown, pre = call(
         functools.partial(own_kernel, levels),
         [((levels + 1, SUMMED) + tile, F32), ((levels, 10) + tile, F32)],
@@ -692,7 +691,7 @@
          ((10 * planes, LANES), F32), ((8,) + tile, F32), ((8, 2, LANES), F32)],
         gains, rests, message, got, codes_s, tables,
     )
-    x3_in, y3_in, d3_in = around(x3, 1, 0), around(y3, 0, 1), around(d3, 1, 1)
+    x3_in, y3_in, d3_in = around(x3, -1, 0), around(y3, 0, -1), around(d3, -1, -1)
     sown3, pre3 = call(
         functools.partial(own_back_kernel, levels),
         [((levels + 1, 8) + tile, F32), ((levels, 4) + tile, F32)],

time: 30 us -> 26.9 us (0.90)
  waiting for transfers between devices: 7.85 us -> 3.35 us
  starting transfers between devices: 10.4 us -> 11.9 us
    ppermute x6, waiting for transfers between devices: 6.35 us -> 1.85 us  [around(): return lax.ppermute(x, ('lx', 'ly'), pairs)]
    ppermute x6, starting transfers between devices: 10.3 us -> 11.8 us  [around(): return lax.ppermute(x, ('lx', 'ly'), pairs)]
  transfers between devices with their start and end apart: 7 -> 7, of which waited for: 4 -> 3; matrix products, arithmetic and copies ran while one was open for 0% -> 0% of each run, Pallas kernels for 16% -> 18%
where the time goes in v4:
time: 26.9 us; the launch traced here: 26.8 us
  starting transfers between devices  11.9 us (44%)
  Pallas kernels  10.7 us (40%)
  waiting for transfers between devices  3.35 us (12%)
  between operations  0.73 us (3%)
    ppermute x6, starting transfers between devices, around(): return lax.ppermute(x, ('lx', 'ly'), pairs)  11.8 us
    pallas_call x9, Pallas kernels, call(): pl.pallas_call(kernel, out_shape=[jax.ShapeDtypeStruct(s, t) for s, t in...  10.7 us
    ppermute x6, waiting for transfers between devices, around(): return lax.ppermute(x, ('lx', 'ly'), pairs)  1.85 us
    ppermute x1, waiting for transfers between devices, swap(): return lax.ppermute(x, 'depth', [(0, 1), (1, 0)])  1.5 us
  transfers between devices with their start and end apart: 7, of which 3 were waited for; matrix products, arithmetic and copies ran while one was open for 0% of the time, Pallas kernels for 18%

profile of v4, /device:TPU:0, one launch (start us, length us, event | category | flops | bytes accessed | tf_op | source)
XLA Modules:
  0.0 26.8 jit_solution(18417191340638395992)
XLA Ops:
  0.6 0.0 copy-start
  0.6 1.4 %shard_map.77 = (f32[16,4,8,128]{3,2,1,0:T(8,128)S(1)}, f32[16,4,8,128]{3,2,1,0:T(8,128)S(1)}, f32[16,8,128]{2,1,0:T(8,128)S(1)}, s32[16,8,128]{2,1,0:T(8,128)S(...) custom-call(f32[16,4,8,128]{3,2,1,0:T(8,128)} %iterate.1, f32[16,4,8,128]{3,2,1,0:T(8,128)} %right.1, ...), custom_call_target="tpu_custom_call" | custom-call | tf_op jit(solution)/shard_map/pallas_call | solution.py:618
  2.0 0.1 shard_map.79
  2.1 3.0 %collective-permute-start = (f32[15,16,128]{2,1,0:T(8,128)S(1)}, f32[15,16,128]{2,1,0:T(8,128)S(1)}, u32[]{:S(2)}, u32[]{:S(2)}) collective-permute-start(f32[15,16,128]{2,1,0:T(8,128)S(1)} %shard_map.79), channel_id=1, source_target_pairs={{0,4},{1,5},{2,6},{3,7},{4,8},{5,9},{6,10},{7,11},{8,12},{9,13},{1... | collective-permute-start | bytes 368648 | tf_op jit(solution)/shard_map/ppermute | solution.py:633
  5.1 1.6 %collective-permute-start.1 = (f32[10,8,128]{2,1,0:T(8,128)S(1)}, f32[10,8,128]{2,1,0:T(8,128)S(1)}, u32[]{:S(2)}, u32[]{:S(2)}) collective-permute-start(f32[10,8,128]{2,1,0:T(8,128)S(1)} %get-tuple-element.33), channel_id=1, source_target_pairs={{0,1},{1,2},{2,3},{3,0},{4,5},{5,6},{6,7},{7,4},{8,9},{9,10},{10,1... | collective-permute-start | bytes 122888 | tf_op jit(solution)/shard_map/ppermute | solution.py:633
  6.7 2.5 %collective-permute-start.2 = (f32[10,2,128]{2,1,0:T(2,128)S(1)}, f32[10,2,128]{2,1,0:T(2,128)S(1)}, u32[]{:S(2)}, u32[]{:S(2)}) collective-permute-start(f32[10,2,128]{2,1,0:T(2,128)S(1)} %get-tuple-element.34), channel_id=1, source_target_pairs={{0,5},{1,6},{2,7},{3,4},{4,9},{5,10},{6,11},{7,8},{8,13},{9,14},{1... | collective-permute-start | bytes 30728 | tf_op jit(solution)/shard_map/ppermute | solution.py:633
  9.2 0.0 copy-done
  9.2 0.1 broadcast_in_dim.8.tables
  9.3 2.4 %shard_map.78 = (f32[17,19,8,128]{3,2,1,0:T(8,128)S(1)}, f32[16,10,8,128]{3,2,1,0:T(8,128)S(1)}) custom-call(f32[16,4,8,128]{3,2,1,0:T(8,128)S(1)} %get-tuple-element.25.it, f32[16,4,8,128]{3,2,1,0:T(8,128)S(1)} %get-tuple-element.26.rt, f32[16,8,128]{2,1,0:T(8,128)S(1)} %get-tuple-element.27.st, s32[16,8,128]{2,1,0:T(8,128)S(1)} %get-tuple-element.28.codes, ...), custom_call_target="tpu_custom_call" | custom-call | tf_op jit(solution)/shard_map/pallas_call | solution.py:618
  11.6 0.0 collective-permute-done.xm
  11.7 0.8 %shard_map.80 = (f32[17,19,8,128]{3,2,1,0:T(8,128)S(1)}, f32[16,10,8,128]{3,2,1,0:T(8,128)S(1)}) custom-call(f32[17,19,8,128]{3,2,1,0:T(8,128)S(1)} %get-tuple-element.29.sown, f32[16,10,8,128]{3,2,1,0:T(8,128)S(1)} %get-tuple-element.30.pre, f32[15,16,128]{2,1,0:T(8,128)S(1)} %collective-permute-done.xm, f32[32,8,128]{2,1,0:T(8,128)S(1)} %broadcast_in_dim.8.tables), custom_call_target="tpu_custom_call" | custom-call | tf_op jit(solution)/shard_map/pallas_call | solution.py:618
  12.5 1.4 %collective-permute-done.2.dm = f32[10,2,128]{2,1,0:T(2,128)S(1)} collective-permute-done((f32[10,2,128]{2,1,0:T(2,128)S(1)}, f32[10,2,128]{2,1,0:T(2,128)S(1)}, u32[]{:S(2)}, u32[]{:S(2)}) %collective-permute-start.2) | collective-permute-done | bytes 10272 | tf_op jit(solution)/shard_map/ppermute | solution.py:633
  13.9 0.0 collective-permute-done.1.ym
  13.9 2.1 %shard_map.81 = (f32[15,16,8,128]{3,2,1,0:T(8,128)S(1)}, f32[15,4,8,128]{3,2,1,0:T(8,128)S(1)}, f32[60,8,128]{2,1,0:T(8,128)S(1)}, s32[16,8,128]{2,1,0:T(8,128)S(1)}) custom-call(f32[17,19,8,128]{3,2,1,0:T(8,128)S(1)} %get-tuple-element.31.sown, f32[16,10,8,128]{3,2,1,0:T(8,128)S(1)} %get-tuple-element.32.pre, f32[10,8,128]{2,1,0:T(8,128)S(1)} %collective-permute-done.1.ym, ...), custom_call_target="tpu_custom_call" | custom-call | tf_op jit(solution)/shard_map/pallas_call | solution.py:618
  16.0 0.1 collective-permute-start.3
  16.1 1.5 %collective-permute-done.3.got = f32[60,8,128]{2,1,0:T(8,128)S(1)} collective-permute-done((f32[60,8,128]{2,1,0:T(8,128)S(1)}, f32[60,8,128]{2,1,0:T(8,128)S(1)}, u32[]{:S(2)}, u32[]{:S(2)}) %collective-permute-start.3) | collective-permute-done | bytes 245792 | tf_op jit(solution)/shard_map/ppermute | solution.py:637
  17.6 0.6 %shard_map.82 = (f32[18,4,8,128]{3,2,1,0:T(8,128)S(1)}, f32[18,4,8,128]{3,2,1,0:T(8,128)S(1)}, f32[180,128]{1,0:T(8,128)S(1)}, f32[8,8,128]{2,1,0:T(8,128)S(1)}, f32[8,2,128]{2,1,0:T(2,128)S(1)}) custom-call(f32[15,16,8,128]{3,2,1,0:T(8,128)S(1)} %get-tuple-element.35.gains, f32[15,4,8,128]{3,2,1,0:T(8,128)S(1)} %get-tuple-element.36.rests, ...), custom_call_target="tpu_custom_call" | custom-call | tf_op jit(solution)/shard_map/pallas_call | solution.py:618
  18.2 0.6 %collective-permute-start.4 = (f32[180,128]{1,0:T(8,128)S(1)}, f32[180,128]{1,0:T(8,128)S(1)}, u32[]{:S(2)}, u32[]{:S(2)}) collective-permute-start(f32[180,128]{1,0:T(8,128)S(1)} %get-tuple-element.43), channel_id=1, source_target_pairs={{0,12},{1,13},{2,14},{3,15},{4,0},{5,1},{6,2},{7,3},{8,4},{9,5},{1... | collective-permute-start | bytes 276488 | tf_op jit(solution)/shard_map/ppermute | solution.py:633
  18.8 1.7 %collective-permute-start.5 = (f32[8,8,128]{2,1,0:T(8,128)S(1)}, f32[8,8,128]{2,1,0:T(8,128)S(1)}, u32[]{:S(2)}, u32[]{:S(2)}) collective-permute-start(f32[8,8,128]{2,1,0:T(8,128)S(1)} %get-tuple-element.46), channel_id=1, source_target_pairs={{0,3},{1,0},{2,1},{3,2},{4,7},{5,4},{6,5},{7,6},{8,11},{9,8},{10,9... | collective-permute-start | bytes 98312 | tf_op jit(solution)/shard_map/ppermute | solution.py:633
  20.5 2.4 %collective-permute-start.6 = (f32[8,2,128]{2,1,0:T(2,128)S(1)}, f32[8,2,128]{2,1,0:T(2,128)S(1)}, u32[]{:S(2)}, u32[]{:S(2)}) collective-permute-start(f32[8,2,128]{2,1,0:T(2,128)S(1)} %get-tuple-element.47), channel_id=1, source_target_pairs={{0,15},{1,12},{2,13},{3,14},{4,3},{5,0},{6,1},{7,2},{8,7},{9,4},{1... | collective-permute-start | bytes 24584 | tf_op jit(solution)/shard_map/ppermute | solution.py:633
  22.9 1.3 %shard_map.83 = (f32[17,8,8,128]{3,2,1,0:T(8,128)S(1)}, f32[16,4,8,128]{3,2,1,0:T(8,128)S(1)}) custom-call(f32[18,4,8,128]{3,2,1,0:T(8,128)S(1)} %get-tuple-element.39.xs, f32[18,4,8,128]{3,2,1,0:T(8,128)S(1)} %get-tuple-element.40.kx), custom_call_target="tpu_custom_call" | custom-call | tf_op jit(solution)/shard_map/pallas_call | solution.py:618
  24.2 0.0 collective-permute-done.4.x3
  24.2 0.4 %shard_map.84 = (f32[17,8,8,128]{3,2,1,0:T(8,128)S(1)}, f32[16,4,8,128]{3,2,1,0:T(8,128)S(1)}) custom-call(f32[17,8,8,128]{3,2,1,0:T(8,128)S(1)} %get-tuple-element.41.sown, f32[16,4,8,128]{3,2,1,0:T(8,128)S(1)} %get-tuple-element.42.pre, f32[180,128]{1,0:T(8,128)S(1)} %collective-permute-done.4.x3, f32[32,8,128]{2,1,0:T(8,128)S(1)} %broadcast_in_dim.8.tables), custom_call_target="tpu_custom_call" | custom-call | tf_op jit(solution)/shard_map/pallas_call | solution.py:618
  24.7 0.4 %collective-permute-done.6.d3 = f32[8,2,128]{2,1,0:T(2,128)S(1)} collective-permute-done((f32[8,2,128]{2,1,0:T(2,128)S(1)}, f32[8,2,128]{2,1,0:T(2,128)S(1)}, u32[]{:S(2)}, u32[]{:S(2)}) %collective-permute-start.6) | collective-permute-done | bytes 8224 | tf_op jit(solution)/shard_map/ppermute | solution.py:633
  25.1 0.0 collective-permute-done.5.y3
  25.1 1.7 %shard_map.85 = (f32[16,4,8,128]{3,2,1,0:T(8,128)}, f32[8,4,8,128]{3,2,1,0:T(8,128)}) custom-call(f32[17,8,8,128]{3,2,1,0:T(8,128)S(1)} %get-tuple-element.44.sown, f32[16,4,8,128]{3,2,1,0:T(8,128)S(1)} %get-tuple-element.45.pre, f32[8,8,128]{2,1,0:T(8,128)S(1)} %collective-permute-done.5.y3, f32[8,2,128]{2,1,0:T(2,128)S(1)} %collective-permute-done.6.d3, ...), custom_call_target="tpu_custom_call" | custom-call | tf_op jit(solution)/shard_map/pallas_call | solution.py:618
Async XLA Ops:
  0.6 8.5 %copy-start = (f32[2,8,4,4]{1,3,2,0:T(4,128)S(1)}, f32[2,8,4,4]{1,3,2,0:T(4,128)}, u32[]{:S(2)}) copy-start(f32[2,8,4,4]{1,3,2,0:T(4,128)} %param.11) | copy-start | bytes 3076
  2.1 9.6 %collective-permute-start = (f32[15,16,128]{2,1,0:T(8,128)S(1)}, f32[15,16,128]{2,1,0:T(8,128)S(1)}, u32[]{:S(2)}, u32[]{:S(2)}) collective-permute-start(f32[15,16,128]{2,1,0:T(8,128)S(1)} %shard_map.79), channel_id=1, source_target_pairs={{0,4},{1,5},{2,6},{3,7},{4,8},{5,9},{6,10},{7,11},{8,12},{9,13},{1... | collective-permute-start | bytes 368648 | tf_op jit(solution)/shard_map/ppermute | solution.py:633
  5.1 8.8 %collective-permute-start.1 = (f32[10,8,128]{2,1,0:T(8,128)S(1)}, f32[10,8,128]{2,1,0:T(8,128)S(1)}, u32[]{:S(2)}, u32[]{:S(2)}) collective-permute-start(f32[10,8,128]{2,1,0:T(8,128)S(1)} %get-tuple-element.33), channel_id=1, source_target_pairs={{0,1},{1,2},{2,3},{3,0},{4,5},{5,6},{6,7},{7,4},{8,9},{9,10},{10,1... | collective-permute-start | bytes 122888 | tf_op jit(solution)/shard_map/ppermute | solution.py:633
  6.7 7.3 %collective-permute-start.2 = (f32[10,2,128]{2,1,0:T(2,128)S(1)}, f32[10,2,128]{2,1,0:T(2,128)S(1)}, u32[]{:S(2)}, u32[]{:S(2)}) collective-permute-start(f32[10,2,128]{2,1,0:T(2,128)S(1)} %get-tuple-element.34), channel_id=1, source_target_pairs={{0,5},{1,6},{2,7},{3,4},{4,9},{5,10},{6,11},{7,8},{8,13},{9,14},{1... | collective-permute-start | bytes 30728 | tf_op jit(solution)/shard_map/ppermute | solution.py:633
  16.0 1.6 %collective-permute-start.3 = (f32[60,8,128]{2,1,0:T(8,128)S(1)}, f32[60,8,128]{2,1,0:T(8,128)S(1)}, u32[]{:S(2)}, u32[]{:S(2)}) collective-permute-start(f32[60,8,128]{2,1,0:T(8,128)S(1)} %get-tuple-element.37.message), channel_id=1, source_target_pairs={{0,16},{16,0},{1,17},{17,1},{2,18},{18,2},{3,19},{19,3},{4,20},{20... | collective-permute-start | bytes 737288 | tf_op jit(solution)/shard_map/ppermute | solution.py:637
  18.2 6.1 %collective-permute-start.4 = (f32[180,128]{1,0:T(8,128)S(1)}, f32[180,128]{1,0:T(8,128)S(1)}, u32[]{:S(2)}, u32[]{:S(2)}) collective-permute-start(f32[180,128]{1,0:T(8,128)S(1)} %get-tuple-element.43), channel_id=1, source_target_pairs={{0,12},{1,13},{2,14},{3,15},{4,0},{5,1},{6,2},{7,3},{8,4},{9,5},{1... | collective-permute-start | bytes 276488 | tf_op jit(solution)/shard_map/ppermute | solution.py:633
  18.8 6.3 %collective-permute-start.5 = (f32[8,8,128]{2,1,0:T(8,128)S(1)}, f32[8,8,128]{2,1,0:T(8,128)S(1)}, u32[]{:S(2)}, u32[]{:S(2)}) collective-permute-start(f32[8,8,128]{2,1,0:T(8,128)S(1)} %get-tuple-element.46), channel_id=1, source_target_pairs={{0,3},{1,0},{2,1},{3,2},{4,7},{5,4},{6,5},{7,6},{8,11},{9,8},{10,9... | collective-permute-start | bytes 98312 | tf_op jit(solution)/shard_map/ppermute | solution.py:633
  20.5 4.5 %collective-permute-start.6 = (f32[8,2,128]{2,1,0:T(2,128)S(1)}, f32[8,2,128]{2,1,0:T(2,128)S(1)}, u32[]{:S(2)}, u32[]{:S(2)}) collective-permute-start(f32[8,2,128]{2,1,0:T(2,128)S(1)} %get-tuple-element.47), channel_id=1, source_target_pairs={{0,15},{1,12},{2,13},{3,14},{4,3},{5,0},{6,1},{7,2},{8,7},{9,4},{1... | collective-permute-start | bytes 24584 | tf_op jit(solution)/shard_map/ppermute | solution.py:633

commit v5 on v4

--- a/solution.py
+++ b/solution.py
@@ -153,7 +153,7 @@
         for k, value in enumerate(summed_fields(tables, codes[n], field)):
             u[n + 1, k] = value
 
-    steps(0, levels, fill)
+    steps(0, levels, fill, 2)
 
     def shift(n):
         z = level_of(side, n, levels)
@@ -162,7 +162,7 @@
         for k, value in enumerate(fields):
             pre[n, k] = roll_lanes(roll_rows(value, 1), 1)
 
-    steps(0, levels, shift, 2)
+    steps(0, levels, shift, 4)
 
     def gather(n):
         for k in range(SUMMED):
@@ -171,7 +171,7 @@
             b = jnp.where(row >= 1, roll_rows(w, 1), 0.0) + g
             sown[n, k] = jnp.where(lane >= 1, roll_lanes(g, 1), 0.0) + (vl * roll_lanes(b, 2) + vu * b)
 
-    steps(0, levels + 1, gather, 2)
+    steps(0, levels + 1, gather, 4)
 
 
 def invert(m):
@@ -274,7 +274,7 @@
 def sweep_kernel(
     levels, sown, pre, ym, dm, codes, tables,
     gains, rests, message, codes_s,
-    yv, ys, fs, rs, ss, ps, ms, qs,
+    yv, ys, fs, rs, ss, ps, ms, qs, vs, total,
 ):
     first_x = lax.axis_index("lx") == 0
     first_y = lax.axis_index("ly") == 0
@@ -305,19 +305,16 @@
         ss[n] = moved[9]
 
     for c in range(4):
-        fs[0, c] = zero()
-        fs[levels + 1, c] = zero()
+        vs[0, c] = zero()
     for k in range(10):
         ms[0, k] = zero()
 
-    def lateral_sums(n):
-        return [
-            sown[n, k] + jnp.where(lane < 2, roll_lanes(yv[k], -2 * n), 0.0)
-            for k in range(SUMMED)
-        ]
+    def gather(n):
+        for k in range(SUMMED):
+            total[n, k] = sown[n, k] + jnp.where(lane < 2, roll_lanes(yv[k], -2 * n), 0.0)
 
     def assemble(n, last=False):
-        sums = lateral_sums(n)
+        sums = [total[n, k] for k in range(SUMMED)]
         act = activity(codes_s[n])
         half = 0.5 * act
         lateral = lookup(tables, 0, codes_s[n])
@@ -334,16 +331,21 @@
             value = half * (lateral[k] * sums[0] + sums[1 + k]) + (below[k] + above[k])
             block.append(value + ss[n] if i == j else value)
         field = [fs[n + 1, c] for c in range(4)]
-        before = apply_sym(below, [fs[n, c] for c in range(4)])
-        after = apply_sym(above, [fs[n + 2, c] for c in range(4)])
-        diagonal = apply_sym(block, field)
-        flow = apply_sym(lateral, sums[11:15])
+        if last:
+            flux = [zero() for _ in range(4)]
+        else:
+            flux = apply_sym(above, [field[c] - fs[n + 2, c] for c in range(4)])
+        flow = apply_sym(lateral, [sums[0] * field[c] - sums[11 + c] for c in range(4)])
+        flow_back = apply_sym(sums[1:11], field)
+        stored = ss[n]
+        for c in range(4):
+            out = half * (flow[c] + (flow_back[c] - sums[15 + c])) + (flux[c] - vs[n, c])
+            qs[n, c] = act * (rs[n, c] - (stored * field[c] + out))
         for k in range(10):
             ms[n + 1, k] = above[k]
             ps[n, k] = block[k]
         for c in range(4):
-            near = (before[c] + after[c]) + half * (flow[c] + sums[15 + c])
-            qs[n, c] = act * (rs[n, c] - (diagonal[c] - near))
+            vs[n + 1, c] = flux[c]
 
     def eliminate(n, carry):
         coupled, carried = carry
@@ -359,19 +361,23 @@
                 gains[n, 4 * i + j] = gain[i][j]
         return back_product(link, gain), apply_sym(link, rest)
 
-    shift(0)
-    shift(1)
-    shift(2)
+    for n in range(3):
+        shift(n)
+    for n in range(2):
+        gather(n)
     assemble(0)
 
     def advance(n, carry):
         carry = eliminate(n, carry)
         assemble(n + 1)
         shift(n + 3)
+        gather(n + 2)
         return carry
 
     zeros = [zero() for _ in range(10)]
     carry = lax.fori_loop(0, levels - 3, advance, (zeros, zeros[:4]))
+    gather(levels - 1)
+    gather(levels)
     carry = eliminate(levels - 3, carry)
     assemble(levels - 2)
     carry = eliminate(levels - 2, carry)
@@ -384,8 +390,8 @@
         message[10 + c] = qs[end_n, c] + carried[c]
         message[33 + c] = fs[levels, c]
         message[56 + c] = rests[end_n - 1, c]
-    for k, value in enumerate(lateral_sums(levels)):
-        message[14 + k] = value
+    for k in range(SUMMED):
+        message[14 + k] = total[levels, k]
     message[37] = codes_s[end_n].astype(F32)
     message[38] = codes_s[end_n - 1].astype(F32)
     message[39] = codes[end_n].astype(F32)
@@ -574,7 +580,8 @@
             x = jnp.where(lane == 127, roll_lanes(ys[c], 127 - 2 * n), pre[n, c])
             up[z, c] = it[z, c] + x
 
-    steps(0, levels, place, 4)
+    for n in range(levels):
+        place(n)
     send_updated = pltpu.make_async_copy(up, updated, sems.at[0])
     send_updated.start()
 
@@ -596,7 +603,8 @@
 
     for c in range(4):
         sm[0, c] = zero()
-    steps(0, levels, lambda n: smooth(n, codes[n]), 4)
+    for n in range(levels):
+        smooth(n, codes[n])
     smooth(levels, got[39].astype(jnp.int32))
 
     step = 1 - 2 * side
@@ -682,6 +690,7 @@
             vmem(SUMMED, *tile), vmem(10, *tile),
             vmem(planes, 4, *tile), vmem(levels, 4, *tile), vmem(levels, *tile),
             vmem(levels, 10, *tile), vmem(levels + 1, 10, *tile), vmem(levels, 4, *tile),
+            vmem(levels + 1, 4, *tile), vmem(levels + 1, SUMMED, *tile),
         ],
     )
     got = swap(message)

time: 26.9 us -> 25.9 us (0.963)
  Pallas kernels: 10.7 us -> 9.49 us
    pallas_call x9, Pallas kernels: 10.7 us -> 9.49 us  [call(): pl.pallas_call(kernel, out_shape=[jax.ShapeDtypeStruct(s, t) for s, t in...]
  transfers between devices with their start and end apart: 7 -> 7, of which waited for: 3 -> 2; matrix products, arithmetic and copies ran while one was open for 0% -> 0% of each run, Pallas kernels for 18% -> 17%
where the time goes in v5:
time: 25.9 us; the launch traced here: 25.8 us
  starting transfers between devices  11.9 us (46%)
  Pallas kernels  9.49 us (37%)
  waiting for transfers between devices  3.61 us (14%)
  between operations  0.74 us (3%)
    ppermute x6, starting transfers between devices, around(): return lax.ppermute(x, ('lx', 'ly'), pairs)  11.8 us
    pallas_call x9, Pallas kernels, call(): pl.pallas_call(kernel, out_shape=[jax.ShapeDtypeStruct(s, t) for s, t in...  9.49 us
    ppermute x6, waiting for transfers between devices, around(): return lax.ppermute(x, ('lx', 'ly'), pairs)  2.11 us
    ppermute x1, waiting for transfers between devices, swap(): return lax.ppermute(x, 'depth', [(0, 1), (1, 0)])  1.5 us
  transfers between devices with their start and end apart: 7, of which 2 were waited for; matrix products, arithmetic and copies ran while one was open for 0% of the time, Pallas kernels for 17%

profile of v5, /device:TPU:0, one launch (start us, length us, event | category | flops | bytes accessed | tf_op | source)
XLA Modules:
  0.0 25.8 jit_solution(5071788369716461295)
XLA Ops:
  0.6 0.0 copy-start
  0.6 1.4 %shard_map.77 = (f32[16,4,8,128]{3,2,1,0:T(8,128)S(1)}, f32[16,4,8,128]{3,2,1,0:T(8,128)S(1)}, f32[16,8,128]{2,1,0:T(8,128)S(1)}, s32[16,8,128]{2,1,0:T(8,128)S(...) custom-call(f32[16,4,8,128]{3,2,1,0:T(8,128)} %iterate.1, f32[16,4,8,128]{3,2,1,0:T(8,128)} %right.1, ...), custom_call_target="tpu_custom_call" | custom-call | tf_op jit(solution)/shard_map/pallas_call | solution.py:626
  2.0 0.1 shard_map.79
  2.1 3.0 %collective-permute-start = (f32[15,16,128]{2,1,0:T(8,128)S(1)}, f32[15,16,128]{2,1,0:T(8,128)S(1)}, u32[]{:S(2)}, u32[]{:S(2)}) collective-permute-start(f32[15,16,128]{2,1,0:T(8,128)S(1)} %shard_map.79), channel_id=1, source_target_pairs={{0,4},{1,5},{2,6},{3,7},{4,8},{5,9},{6,10},{7,11},{8,12},{9,13},{1... | collective-permute-start | bytes 368648 | tf_op jit(solution)/shard_map/ppermute | solution.py:641
  5.1 1.6 %collective-permute-start.1 = (f32[10,8,128]{2,1,0:T(8,128)S(1)}, f32[10,8,128]{2,1,0:T(8,128)S(1)}, u32[]{:S(2)}, u32[]{:S(2)}) collective-permute-start(f32[10,8,128]{2,1,0:T(8,128)S(1)} %get-tuple-element.33), channel_id=1, source_target_pairs={{0,1},{1,2},{2,3},{3,0},{4,5},{5,6},{6,7},{7,4},{8,9},{9,10},{10,1... | collective-permute-start | bytes 122888 | tf_op jit(solution)/shard_map/ppermute | solution.py:641
  6.7 2.5 %collective-permute-start.2 = (f32[10,2,128]{2,1,0:T(2,128)S(1)}, f32[10,2,128]{2,1,0:T(2,128)S(1)}, u32[]{:S(2)}, u32[]{:S(2)}) collective-permute-start(f32[10,2,128]{2,1,0:T(2,128)S(1)} %get-tuple-element.34), channel_id=1, source_target_pairs={{0,5},{1,6},{2,7},{3,4},{4,9},{5,10},{6,11},{7,8},{8,13},{9,14},{1... | collective-permute-start | bytes 30728 | tf_op jit(solution)/shard_map/ppermute | solution.py:641
  9.2 0.0 copy-done
  9.2 0.1 broadcast_in_dim.8.tables
  9.3 1.7 %shard_map.78 = (f32[17,19,8,128]{3,2,1,0:T(8,128)S(1)}, f32[16,10,8,128]{3,2,1,0:T(8,128)S(1)}) custom-call(f32[16,4,8,128]{3,2,1,0:T(8,128)S(1)} %get-tuple-element.25.it, f32[16,4,8,128]{3,2,1,0:T(8,128)S(1)} %get-tuple-element.26.rt, f32[16,8,128]{2,1,0:T(8,128)S(1)} %get-tuple-element.27.st, s32[16,8,128]{2,1,0:T(8,128)S(1)} %get-tuple-element.28.codes, ...), custom_call_target="tpu_custom_call" | custom-call | tf_op jit(solution)/shard_map/pallas_call | solution.py:626
  11.0 0.0 collective-permute-done.xm
  11.0 0.8 %shard_map.80 = (f32[17,19,8,128]{3,2,1,0:T(8,128)S(1)}, f32[16,10,8,128]{3,2,1,0:T(8,128)S(1)}) custom-call(f32[17,19,8,128]{3,2,1,0:T(8,128)S(1)} %get-tuple-element.29.sown, f32[16,10,8,128]{3,2,1,0:T(8,128)S(1)} %get-tuple-element.30.pre, f32[15,16,128]{2,1,0:T(8,128)S(1)} %collective-permute-done.xm, f32[32,8,128]{2,1,0:T(8,128)S(1)} %broadcast_in_dim.8.tables), custom_call_target="tpu_custom_call" | custom-call | tf_op jit(solution)/shard_map/pallas_call | solution.py:626
  11.8 2.1 %collective-permute-done.2.dm = f32[10,2,128]{2,1,0:T(2,128)S(1)} collective-permute-done((f32[10,2,128]{2,1,0:T(2,128)S(1)}, f32[10,2,128]{2,1,0:T(2,128)S(1)}, u32[]{:S(2)}, u32[]{:S(2)}) %collective-permute-start.2) | collective-permute-done | bytes 10272 | tf_op jit(solution)/shard_map/ppermute | solution.py:641
  13.9 0.0 collective-permute-done.1.ym
  13.9 1.9 %shard_map.81 = (f32[15,16,8,128]{3,2,1,0:T(8,128)S(1)}, f32[15,4,8,128]{3,2,1,0:T(8,128)S(1)}, f32[60,8,128]{2,1,0:T(8,128)S(1)}, s32[16,8,128]{2,1,0:T(8,128)S(1)}) custom-call(f32[17,19,8,128]{3,2,1,0:T(8,128)S(1)} %get-tuple-element.31.sown, f32[16,10,8,128]{3,2,1,0:T(8,128)S(1)} %get-tuple-element.32.pre, f32[10,8,128]{2,1,0:T(8,128)S(1)} %collective-permute-done.1.ym, ...), custom_call_target="tpu_custom_call" | custom-call | tf_op jit(solution)/shard_map/pallas_call | solution.py:626
  15.9 0.1 collective-permute-start.3
  15.9 1.5 %collective-permute-done.3.got = f32[60,8,128]{2,1,0:T(8,128)S(1)} collective-permute-done((f32[60,8,128]{2,1,0:T(8,128)S(1)}, f32[60,8,128]{2,1,0:T(8,128)S(1)}, u32[]{:S(2)}, u32[]{:S(2)}) %collective-permute-start.3) | collective-permute-done | bytes 245792 | tf_op jit(solution)/shard_map/ppermute | solution.py:645
  17.4 0.6 %shard_map.82 = (f32[18,4,8,128]{3,2,1,0:T(8,128)S(1)}, f32[18,4,8,128]{3,2,1,0:T(8,128)S(1)}, f32[180,128]{1,0:T(8,128)S(1)}, f32[8,8,128]{2,1,0:T(8,128)S(1)}, f32[8,2,128]{2,1,0:T(2,128)S(1)}) custom-call(f32[15,16,8,128]{3,2,1,0:T(8,128)S(1)} %get-tuple-element.35.gains, f32[15,4,8,128]{3,2,1,0:T(8,128)S(1)} %get-tuple-element.36.rests, ...), custom_call_target="tpu_custom_call" | custom-call | tf_op jit(solution)/shard_map/pallas_call | solution.py:626
  18.0 0.6 %collective-permute-start.4 = (f32[180,128]{1,0:T(8,128)S(1)}, f32[180,128]{1,0:T(8,128)S(1)}, u32[]{:S(2)}, u32[]{:S(2)}) collective-permute-start(f32[180,128]{1,0:T(8,128)S(1)} %get-tuple-element.43), channel_id=1, source_target_pairs={{0,12},{1,13},{2,14},{3,15},{4,0},{5,1},{6,2},{7,3},{8,4},{9,5},{1... | collective-permute-start | bytes 276488 | tf_op jit(solution)/shard_map/ppermute | solution.py:641
  18.6 1.2 %collective-permute-start.5 = (f32[8,8,128]{2,1,0:T(8,128)S(1)}, f32[8,8,128]{2,1,0:T(8,128)S(1)}, u32[]{:S(2)}, u32[]{:S(2)}) collective-permute-start(f32[8,8,128]{2,1,0:T(8,128)S(1)} %get-tuple-element.46), channel_id=1, source_target_pairs={{0,3},{1,0},{2,1},{3,2},{4,7},{5,4},{6,5},{7,6},{8,11},{9,8},{10,9... | collective-permute-start | bytes 98312 | tf_op jit(solution)/shard_map/ppermute | solution.py:641
  19.8 2.9 %collective-permute-start.6 = (f32[8,2,128]{2,1,0:T(2,128)S(1)}, f32[8,2,128]{2,1,0:T(2,128)S(1)}, u32[]{:S(2)}, u32[]{:S(2)}) collective-permute-start(f32[8,2,128]{2,1,0:T(2,128)S(1)} %get-tuple-element.47), channel_id=1, source_target_pairs={{0,15},{1,12},{2,13},{3,14},{4,3},{5,0},{6,1},{7,2},{8,7},{9,4},{1... | collective-permute-start | bytes 24584 | tf_op jit(solution)/shard_map/ppermute | solution.py:641
  22.8 1.3 %shard_map.83 = (f32[17,8,8,128]{3,2,1,0:T(8,128)S(1)}, f32[16,4,8,128]{3,2,1,0:T(8,128)S(1)}) custom-call(f32[18,4,8,128]{3,2,1,0:T(8,128)S(1)} %get-tuple-element.39.xs, f32[18,4,8,128]{3,2,1,0:T(8,128)S(1)} %get-tuple-element.40.kx), custom_call_target="tpu_custom_call" | custom-call | tf_op jit(solution)/shard_map/pallas_call | solution.py:626
  24.1 0.0 collective-permute-done.4.x3
  24.1 0.4 %shard_map.84 = (f32[17,8,8,128]{3,2,1,0:T(8,128)S(1)}, f32[16,4,8,128]{3,2,1,0:T(8,128)S(1)}) custom-call(f32[17,8,8,128]{3,2,1,0:T(8,128)S(1)} %get-tuple-element.41.sown, f32[16,4,8,128]{3,2,1,0:T(8,128)S(1)} %get-tuple-element.42.pre, f32[180,128]{1,0:T(8,128)S(1)} %collective-permute-done.4.x3, f32[32,8,128]{2,1,0:T(8,128)S(1)} %broadcast_in_dim.8.tables), custom_call_target="tpu_custom_call" | custom-call | tf_op jit(solution)/shard_map/pallas_call | solution.py:626
  24.5 0.0 collective-permute-done.6.d3
  24.5 0.0 collective-permute-done.5.y3
  24.5 1.3 %shard_map.85 = (f32[16,4,8,128]{3,2,1,0:T(8,128)}, f32[8,4,8,128]{3,2,1,0:T(8,128)}) custom-call(f32[17,8,8,128]{3,2,1,0:T(8,128)S(1)} %get-tuple-element.44.sown, f32[16,4,8,128]{3,2,1,0:T(8,128)S(1)} %get-tuple-element.45.pre, f32[8,8,128]{2,1,0:T(8,128)S(1)} %collective-permute-done.5.y3, f32[8,2,128]{2,1,0:T(2,128)S(1)} %collective-permute-done.6.d3, ...), custom_call_target="tpu_custom_call" | custom-call | tf_op jit(solution)/shard_map/pallas_call | solution.py:626
Async XLA Ops:
  0.6 8.5 %copy-start = (f32[2,8,4,4]{1,3,2,0:T(4,128)S(1)}, f32[2,8,4,4]{1,3,2,0:T(4,128)}, u32[]{:S(2)}) copy-start(f32[2,8,4,4]{1,3,2,0:T(4,128)} %param.11) | copy-start | bytes 3076
  2.1 8.9 %collective-permute-start = (f32[15,16,128]{2,1,0:T(8,128)S(1)}, f32[15,16,128]{2,1,0:T(8,128)S(1)}, u32[]{:S(2)}, u32[]{:S(2)}) collective-permute-start(f32[15,16,128]{2,1,0:T(8,128)S(1)} %shard_map.79), channel_id=1, source_target_pairs={{0,4},{1,5},{2,6},{3,7},{4,8},{5,9},{6,10},{7,11},{8,12},{9,13},{1... | collective-permute-start | bytes 368648 | tf_op jit(solution)/shard_map/ppermute | solution.py:641
  5.1 8.8 %collective-permute-start.1 = (f32[10,8,128]{2,1,0:T(8,128)S(1)}, f32[10,8,128]{2,1,0:T(8,128)S(1)}, u32[]{:S(2)}, u32[]{:S(2)}) collective-permute-start(f32[10,8,128]{2,1,0:T(8,128)S(1)} %get-tuple-element.33), channel_id=1, source_target_pairs={{0,1},{1,2},{2,3},{3,0},{4,5},{5,6},{6,7},{7,4},{8,9},{9,10},{10,1... | collective-permute-start | bytes 122888 | tf_op jit(solution)/shard_map/ppermute | solution.py:641
  6.7 7.3 %collective-permute-start.2 = (f32[10,2,128]{2,1,0:T(2,128)S(1)}, f32[10,2,128]{2,1,0:T(2,128)S(1)}, u32[]{:S(2)}, u32[]{:S(2)}) collective-permute-start(f32[10,2,128]{2,1,0:T(2,128)S(1)} %get-tuple-element.34), channel_id=1, source_target_pairs={{0,5},{1,6},{2,7},{3,4},{4,9},{5,10},{6,11},{7,8},{8,13},{9,14},{1... | collective-permute-start | bytes 30728 | tf_op jit(solution)/shard_map/ppermute | solution.py:641
  15.9 1.6 %collective-permute-start.3 = (f32[60,8,128]{2,1,0:T(8,128)S(1)}, f32[60,8,128]{2,1,0:T(8,128)S(1)}, u32[]{:S(2)}, u32[]{:S(2)}) collective-permute-start(f32[60,8,128]{2,1,0:T(8,128)S(1)} %get-tuple-element.37.message), channel_id=1, source_target_pairs={{0,16},{16,0},{1,17},{17,1},{2,18},{18,2},{3,19},{19,3},{4,20},{20... | collective-permute-start | bytes 737288 | tf_op jit(solution)/shard_map/ppermute | solution.py:645
  18.0 6.1 %collective-permute-start.4 = (f32[180,128]{1,0:T(8,128)S(1)}, f32[180,128]{1,0:T(8,128)S(1)}, u32[]{:S(2)}, u32[]{:S(2)}) collective-permute-start(f32[180,128]{1,0:T(8,128)S(1)} %get-tuple-element.43), channel_id=1, source_target_pairs={{0,12},{1,13},{2,14},{3,15},{4,0},{5,1},{6,2},{7,3},{8,4},{9,5},{1... | collective-permute-start | bytes 276488 | tf_op jit(solution)/shard_map/ppermute | solution.py:641
  18.6 5.9 %collective-permute-start.5 = (f32[8,8,128]{2,1,0:T(8,128)S(1)}, f32[8,8,128]{2,1,0:T(8,128)S(1)}, u32[]{:S(2)}, u32[]{:S(2)}) collective-permute-start(f32[8,8,128]{2,1,0:T(8,128)S(1)} %get-tuple-element.46), channel_id=1, source_target_pairs={{0,3},{1,0},{2,1},{3,2},{4,7},{5,4},{6,5},{7,6},{8,11},{9,8},{10,9... | collective-permute-start | bytes 98312 | tf_op jit(solution)/shard_map/ppermute | solution.py:641
  19.8 4.7 %collective-permute-start.6 = (f32[8,2,128]{2,1,0:T(2,128)S(1)}, f32[8,2,128]{2,1,0:T(2,128)S(1)}, u32[]{:S(2)}, u32[]{:S(2)}) collective-permute-start(f32[8,2,128]{2,1,0:T(2,128)S(1)} %get-tuple-element.47), channel_id=1, source_target_pairs={{0,15},{1,12},{2,13},{3,14},{4,3},{5,0},{6,1},{7,2},{8,7},{9,4},{1... | collective-permute-start | bytes 24584 | tf_op jit(solution)/shard_map/ppermute | solution.py:641

commit v6 on v5

--- a/solution.py
+++ b/solution.py
@@ -90,12 +90,11 @@
     return jnp.zeros((ROWS, LANES), F32)
 
 
-def pack_kernel(
+def rows_kernel(
     levels, iterate, right, storage, zones, counts,
-    it, rt, st, codes_out, ym, dm, zones_v, counts_v, sems,
+    it, rt, st, codes_out, xm, zones_v, counts_v, sems,
 ):
     side = lax.axis_index("depth")
-    lane = lane_index()
     copies = [
         pltpu.make_async_copy(source, target, sems.at[k])
         for k, (source, target) in enumerate(
@@ -107,7 +106,6 @@
     for copy in copies:
         copy.wait()
     limit = counts_v[...] - side * levels
-    acc = [zero() for _ in range(10)]
     for n in range(levels):
         z = level_of(side, n, levels)
         code = jnp.where(z < limit, zones_v[z] + 1, 0)
@@ -115,22 +113,24 @@
         fields = [code.astype(F32)] + [it[z, c] for c in range(4)]
         fields += [rt[z, c] for c in range(4)] + [st[z]]
         for k, value in enumerate(fields):
-            acc[k] = jnp.where(lane // 2 == n, roll_lanes(value, 2 * n + 2), acc[k])
-    for k in range(10):
-        ym[k] = acc[k]
-        dm[k] = acc[k][6:8]
-
-
-def pack_rows_kernel(levels, it, rt, st, codes, xm):
+            xm[k, n : n + 1, :] = value[7:8]
+            if k < 5:
+                xm[10 + k, n : n + 1, :] = value[6:7]
+
+
+def columns_kernel(levels, it, rt, st, codes, ym, dm):
     side = lax.axis_index("depth")
+    lane = lane_index()
+    acc = [zero() for _ in range(10)]
     for n in range(levels):
         z = level_of(side, n, levels)
         fields = [codes[n].astype(F32)] + [it[z, c] for c in range(4)]
         fields += [rt[z, c] for c in range(4)] + [st[z]]
         for k, value in enumerate(fields):
-            xm[k, n : n + 1, :] = value[7:8]
-            if k < 5:
-                xm[10 + k, n : n + 1, :] = value[6:7]
+            acc[k] = jnp.where(lane // 2 == n, roll_lanes(value, 2 * n + 2), acc[k])
+    for k in range(10):
+        ym[k] = acc[k]
+        dm[k] = acc[k][6:8]
 
 
 def own_kernel(levels, it, rt, st, codes, tables, sown, pre, u):
@@ -294,7 +294,9 @@
         two = jnp.where(row < 2, corner_u[k], roll_rows(side_u[k], 2))
         g = wl * two + wu * side_u[k]
         b = one + g
-        yv[k] = lane_sum(jnp.where(even, roll_lanes(g, -1) + 0.5 * b, vl1 * b))
+        summed = lane_sum(b)
+        across = roll_lanes(g, -1) + 0.5 * (roll_lanes(g, 1) + roll_lanes(g, -3))
+        yv[k] = jnp.where(even, across + 0.5 * summed, vl1 * summed)
 
     def shift(n):
         moved = [jnp.where(lane < 1, roll_lanes(ys[k], -2 * n - 1), pre[n, k]) for k in range(10)]
@@ -590,7 +592,9 @@
         one = roll_rows(jnp.where(row < 1, corner[k], y3[k]), -1)
         g = wl * y3[k] + wu * two
         b = one + g
-        yv[k] = lane_sum(jnp.where(even, 0.5 * b, roll_lanes(g, 1) + vu127 * b))
+        summed = lane_sum(b)
+        across = roll_lanes(g, 1) + 0.5 * (roll_lanes(g, -1) + roll_lanes(g, 3))
+        yv[k] = jnp.where(even, 0.5 * summed, across + vu127 * summed)
 
     def smooth(n, code):
         sums = [
@@ -653,11 +657,11 @@
     tables = jnp.broadcast_to(
         materials.transpose(0, 2, 3, 1).reshape(32, ROWS, 1), (32, ROWS, LANES)
     )
-    it, rt, st, codes, ym, dm = call(
-        functools.partial(pack_kernel, levels),
+    it, rt, st, codes, xm = call(
+        functools.partial(rows_kernel, levels),
         [((levels, 4) + tile, F32), ((levels, 4) + tile, F32), ((levels,) + tile, F32),
          ((levels,) + tile, jnp.int32),
-         ((10,) + tile, F32), ((10, 2, LANES), F32)],
+         ((15, levels, LANES), F32)],
         iterate, right_side, storage, zones, counts,
         scratch=[
             pltpu.VMEM((levels,) + tile, jnp.int32), pltpu.VMEM(tile, jnp.int32),
@@ -665,8 +669,10 @@
         ],
         far_in=True,
     )
-    xm, = call(
-        functools.partial(pack_rows_kernel, levels), [((15, levels, LANES), F32)], it, rt, st, codes
+    ym, dm = call(
+        functools.partial(columns_kernel, levels),
+        [((10,) + tile, F32), ((10, 2, LANES), F32)],
+        it, rt, st, codes,
     )
     xm_in, ym_in, dm_in = around(xm, 1, 0), around(ym, 0, 1), around(dm, 1, 1)
     sown, pre = call(

time: 25.9 us -> 25.8 us (level)
  transfers between devices with their start and end apart: 7 -> 7, of which waited for: 2 -> 2; matrix products, arithmetic and copies ran while one was open for 0% -> 0% of each run, Pallas kernels for 17% -> 18%
where the time goes in v6:
time: 25.8 us; the launch traced here: 25.7 us
  starting transfers between devices  11.9 us (46%)
  Pallas kernels  9.32 us (36%)
  waiting for transfers between devices  3.61 us (14%)
  between operations  0.74 us (3%)
    ppermute x6, starting transfers between devices, around(): return lax.ppermute(x, ('lx', 'ly'), pairs)  11.8 us
    pallas_call x9, Pallas kernels, call(): pl.pallas_call(kernel, out_shape=[jax.ShapeDtypeStruct(s, t) for s, t in...  9.32 us
    ppermute x6, waiting for transfers between devices, around(): return lax.ppermute(x, ('lx', 'ly'), pairs)  2.11 us
    ppermute x1, waiting for transfers between devices, swap(): return lax.ppermute(x, 'depth', [(0, 1), (1, 0)])  1.5 us
  transfers between devices with their start and end apart: 7, of which 2 were waited for; matrix products, arithmetic and copies ran while one was open for 0% of the time, Pallas kernels for 18%

profile of v6, /device:TPU:0, one launch (start us, length us, event | category | flops | bytes accessed | tf_op | source)
XLA Modules:
  0.0 25.7 jit_solution(13699525039545547960)
XLA Ops:
  0.6 0.0 copy-start
  0.6 1.2 %shard_map.77 = (f32[16,4,8,128]{3,2,1,0:T(8,128)S(1)}, f32[16,4,8,128]{3,2,1,0:T(8,128)S(1)}, f32[16,8,128]{2,1,0:T(8,128)S(1)}, s32[16,8,128]{2,1,0:T(8,128)S(1)}, f32[15,16,128]{2,1,0:T(8,128)S(1)}) custom-call(f32[16,4,8,128]{3,2,1,0:T(8,128)} %iterate.1, f32[16,4,8,128]{3,2,1,0:T(8,128)} %right.1, f32[16,8,128]{2,1,0:T(8,128)} %storage.1, ...), custom_call_target="tpu_custom_call" | custom-call | tf_op jit(solution)/shard_map/pallas_call | solution.py:630
  1.9 3.0 %collective-permute-start = (f32[15,16,128]{2,1,0:T(8,128)S(1)}, f32[15,16,128]{2,1,0:T(8,128)S(1)}, u32[]{:S(2)}, u32[]{:S(2)}) collective-permute-start(f32[15,16,128]{2,1,0:T(8,128)S(1)} %get-tuple-element.32), channel_id=1, source_target_pairs={{0,4},{1,5},{2,6},{3,7},{4,8},{5,9},{6,10},{7,11},{8,12},{9,13},{1... | collective-permute-start | bytes 368648 | tf_op jit(solution)/shard_map/ppermute | solution.py:645
  4.8 0.2 shard_map.80
  5.1 1.6 %collective-permute-start.1 = (f32[10,8,128]{2,1,0:T(8,128)S(1)}, f32[10,8,128]{2,1,0:T(8,128)S(1)}, u32[]{:S(2)}, u32[]{:S(2)}) collective-permute-start(f32[10,8,128]{2,1,0:T(8,128)S(1)} %get-tuple-element.35), channel_id=1, source_target_pairs={{0,1},{1,2},{2,3},{3,0},{4,5},{5,6},{6,7},{7,4},{8,9},{9,10},{10,1... | collective-permute-start | bytes 122888 | tf_op jit(solution)/shard_map/ppermute | solution.py:645
  6.7 2.5 %collective-permute-start.2 = (f32[10,2,128]{2,1,0:T(2,128)S(1)}, f32[10,2,128]{2,1,0:T(2,128)S(1)}, u32[]{:S(2)}, u32[]{:S(2)}) collective-permute-start(f32[10,2,128]{2,1,0:T(2,128)S(1)} %get-tuple-element.36), channel_id=1, source_target_pairs={{0,5},{1,6},{2,7},{3,4},{4,9},{5,10},{6,11},{7,8},{8,13},{9,14},{1... | collective-permute-start | bytes 30728 | tf_op jit(solution)/shard_map/ppermute | solution.py:645
  9.2 0.0 copy-done
  9.2 0.1 broadcast_in_dim.8.tables
  9.3 1.7 %shard_map.78 = (f32[17,19,8,128]{3,2,1,0:T(8,128)S(1)}, f32[16,10,8,128]{3,2,1,0:T(8,128)S(1)}) custom-call(f32[16,4,8,128]{3,2,1,0:T(8,128)S(1)} %get-tuple-element.26.it, f32[16,4,8,128]{3,2,1,0:T(8,128)S(1)} %get-tuple-element.27.rt, f32[16,8,128]{2,1,0:T(8,128)S(1)} %get-tuple-element.28.st, s32[16,8,128]{2,1,0:T(8,128)S(1)} %get-tuple-element.29.codes, ...), custom_call_target="tpu_custom_call" | custom-call | tf_op jit(solution)/shard_map/pallas_call | solution.py:630
  11.0 0.0 collective-permute-done.xm
  11.1 0.8 %shard_map.79 = (f32[17,19,8,128]{3,2,1,0:T(8,128)S(1)}, f32[16,10,8,128]{3,2,1,0:T(8,128)S(1)}) custom-call(f32[17,19,8,128]{3,2,1,0:T(8,128)S(1)} %get-tuple-element.30.sown, f32[16,10,8,128]{3,2,1,0:T(8,128)S(1)} %get-tuple-element.31.pre, f32[15,16,128]{2,1,0:T(8,128)S(1)} %collective-permute-done.xm, f32[32,8,128]{2,1,0:T(8,128)S(1)} %broadcast_in_dim.8.tables), custom_call_target="tpu_custom_call" | custom-call | tf_op jit(solution)/shard_map/pallas_call | solution.py:630
  11.9 2.1 %collective-permute-done.2.dm = f32[10,2,128]{2,1,0:T(2,128)S(1)} collective-permute-done((f32[10,2,128]{2,1,0:T(2,128)S(1)}, f32[10,2,128]{2,1,0:T(2,128)S(1)}, u32[]{:S(2)}, u32[]{:S(2)}) %collective-permute-start.2) | collective-permute-done | bytes 10272 | tf_op jit(solution)/shard_map/ppermute | solution.py:645
  14.0 0.0 collective-permute-done.1.ym
  14.0 1.9 %shard_map.81 = (f32[15,16,8,128]{3,2,1,0:T(8,128)S(1)}, f32[15,4,8,128]{3,2,1,0:T(8,128)S(1)}, f32[60,8,128]{2,1,0:T(8,128)S(1)}, s32[16,8,128]{2,1,0:T(8,128)S(1)}) custom-call(f32[17,19,8,128]{3,2,1,0:T(8,128)S(1)} %get-tuple-element.33.sown, f32[16,10,8,128]{3,2,1,0:T(8,128)S(1)} %get-tuple-element.34.pre, f32[10,8,128]{2,1,0:T(8,128)S(1)} %collective-permute-done.1.ym, ...), custom_call_target="tpu_custom_call" | custom-call | tf_op jit(solution)/shard_map/pallas_call | solution.py:630
  15.9 0.1 collective-permute-start.3
  16.0 1.5 %collective-permute-done.3.got = f32[60,8,128]{2,1,0:T(8,128)S(1)} collective-permute-done((f32[60,8,128]{2,1,0:T(8,128)S(1)}, f32[60,8,128]{2,1,0:T(8,128)S(1)}, u32[]{:S(2)}, u32[]{:S(2)}) %collective-permute-start.3) | collective-permute-done | bytes 245792 | tf_op jit(solution)/shard_map/ppermute | solution.py:649
  17.5 0.6 %shard_map.82 = (f32[18,4,8,128]{3,2,1,0:T(8,128)S(1)}, f32[18,4,8,128]{3,2,1,0:T(8,128)S(1)}, f32[180,128]{1,0:T(8,128)S(1)}, f32[8,8,128]{2,1,0:T(8,128)S(1)}, f32[8,2,128]{2,1,0:T(2,128)S(1)}) custom-call(f32[15,16,8,128]{3,2,1,0:T(8,128)S(1)} %get-tuple-element.37.gains, f32[15,4,8,128]{3,2,1,0:T(8,128)S(1)} %get-tuple-element.38.rests, ...), custom_call_target="tpu_custom_call" | custom-call | tf_op jit(solution)/shard_map/pallas_call | solution.py:630
  18.1 0.6 %collective-permute-start.4 = (f32[180,128]{1,0:T(8,128)S(1)}, f32[180,128]{1,0:T(8,128)S(1)}, u32[]{:S(2)}, u32[]{:S(2)}) collective-permute-start(f32[180,128]{1,0:T(8,128)S(1)} %get-tuple-element.45), channel_id=1, source_target_pairs={{0,12},{1,13},{2,14},{3,15},{4,0},{5,1},{6,2},{7,3},{8,4},{9,5},{1... | collective-permute-start | bytes 276488 | tf_op jit(solution)/shard_map/ppermute | solution.py:645
  18.7 1.1 %collective-permute-start.5 = (f32[8,8,128]{2,1,0:T(8,128)S(1)}, f32[8,8,128]{2,1,0:T(8,128)S(1)}, u32[]{:S(2)}, u32[]{:S(2)}) collective-permute-start(f32[8,8,128]{2,1,0:T(8,128)S(1)} %get-tuple-element.48), channel_id=1, source_target_pairs={{0,3},{1,0},{2,1},{3,2},{4,7},{5,4},{6,5},{7,6},{8,11},{9,8},{10,9... | collective-permute-start | bytes 98312 | tf_op jit(solution)/shard_map/ppermute | solution.py:645
  19.8 3.1 %collective-permute-start.6 = (f32[8,2,128]{2,1,0:T(2,128)S(1)}, f32[8,2,128]{2,1,0:T(2,128)S(1)}, u32[]{:S(2)}, u32[]{:S(2)}) collective-permute-start(f32[8,2,128]{2,1,0:T(2,128)S(1)} %get-tuple-element.49), channel_id=1, source_target_pairs={{0,15},{1,12},{2,13},{3,14},{4,3},{5,0},{6,1},{7,2},{8,7},{9,4},{1... | collective-permute-start | bytes 24584 | tf_op jit(solution)/shard_map/ppermute | solution.py:645
  22.8 1.3 %shard_map.83 = (f32[17,8,8,128]{3,2,1,0:T(8,128)S(1)}, f32[16,4,8,128]{3,2,1,0:T(8,128)S(1)}) custom-call(f32[18,4,8,128]{3,2,1,0:T(8,128)S(1)} %get-tuple-element.41.xs, f32[18,4,8,128]{3,2,1,0:T(8,128)S(1)} %get-tuple-element.42.kx), custom_call_target="tpu_custom_call" | custom-call | tf_op jit(solution)/shard_map/pallas_call | solution.py:630
  24.1 0.0 collective-permute-done.4.x3
  24.1 0.4 %shard_map.84 = (f32[17,8,8,128]{3,2,1,0:T(8,128)S(1)}, f32[16,4,8,128]{3,2,1,0:T(8,128)S(1)}) custom-call(f32[17,8,8,128]{3,2,1,0:T(8,128)S(1)} %get-tuple-element.43.sown, f32[16,4,8,128]{3,2,1,0:T(8,128)S(1)} %get-tuple-element.44.pre, f32[180,128]{1,0:T(8,128)S(1)} %collective-permute-done.4.x3, f32[32,8,128]{2,1,0:T(8,128)S(1)} %broadcast_in_dim.8.tables), custom_call_target="tpu_custom_call" | custom-call | tf_op jit(solution)/shard_map/pallas_call | solution.py:630
  24.6 0.0 collective-permute-done.6.d3
  24.6 0.0 collective-permute-done.5.y3
  24.6 1.1 %shard_map.85 = (f32[16,4,8,128]{3,2,1,0:T(8,128)}, f32[8,4,8,128]{3,2,1,0:T(8,128)}) custom-call(f32[17,8,8,128]{3,2,1,0:T(8,128)S(1)} %get-tuple-element.46.sown, f32[16,4,8,128]{3,2,1,0:T(8,128)S(1)} %get-tuple-element.47.pre, f32[8,8,128]{2,1,0:T(8,128)S(1)} %collective-permute-done.5.y3, f32[8,2,128]{2,1,0:T(2,128)S(1)} %collective-permute-done.6.d3, ...), custom_call_target="tpu_custom_call" | custom-call | tf_op jit(solution)/shard_map/pallas_call | solution.py:630
Async XLA Ops:
  0.6 8.6 %copy-start = (f32[2,8,4,4]{1,3,2,0:T(4,128)S(1)}, f32[2,8,4,4]{1,3,2,0:T(4,128)}, u32[]{:S(2)}) copy-start(f32[2,8,4,4]{1,3,2,0:T(4,128)} %param.11) | copy-start | bytes 3076
  1.9 9.2 %collective-permute-start = (f32[15,16,128]{2,1,0:T(8,128)S(1)}, f32[15,16,128]{2,1,0:T(8,128)S(1)}, u32[]{:S(2)}, u32[]{:S(2)}) collective-permute-start(f32[15,16,128]{2,1,0:T(8,128)S(1)} %get-tuple-element.32), channel_id=1, source_target_pairs={{0,4},{1,5},{2,6},{3,7},{4,8},{5,9},{6,10},{7,11},{8,12},{9,13},{1... | collective-permute-start | bytes 368648 | tf_op jit(solution)/shard_map/ppermute | solution.py:645
  5.1 8.9 %collective-permute-start.1 = (f32[10,8,128]{2,1,0:T(8,128)S(1)}, f32[10,8,128]{2,1,0:T(8,128)S(1)}, u32[]{:S(2)}, u32[]{:S(2)}) collective-permute-start(f32[10,8,128]{2,1,0:T(8,128)S(1)} %get-tuple-element.35), channel_id=1, source_target_pairs={{0,1},{1,2},{2,3},{3,0},{4,5},{5,6},{6,7},{7,4},{8,9},{9,10},{10,1... | collective-permute-start | bytes 122888 | tf_op jit(solution)/shard_map/ppermute | solution.py:645
  6.7 7.3 %collective-permute-start.2 = (f32[10,2,128]{2,1,0:T(2,128)S(1)}, f32[10,2,128]{2,1,0:T(2,128)S(1)}, u32[]{:S(2)}, u32[]{:S(2)}) collective-permute-start(f32[10,2,128]{2,1,0:T(2,128)S(1)} %get-tuple-element.36), channel_id=1, source_target_pairs={{0,5},{1,6},{2,7},{3,4},{4,9},{5,10},{6,11},{7,8},{8,13},{9,14},{1... | collective-permute-start | bytes 30728 | tf_op jit(solution)/shard_map/ppermute | solution.py:645
  15.9 1.6 %collective-permute-start.3 = (f32[60,8,128]{2,1,0:T(8,128)S(1)}, f32[60,8,128]{2,1,0:T(8,128)S(1)}, u32[]{:S(2)}, u32[]{:S(2)}) collective-permute-start(f32[60,8,128]{2,1,0:T(8,128)S(1)} %get-tuple-element.39.message), channel_id=1, source_target_pairs={{0,16},{16,0},{1,17},{17,1},{2,18},{18,2},{3,19},{19,3},{4,20},{20... | collective-permute-start | bytes 737288 | tf_op jit(solution)/shard_map/ppermute | solution.py:649
  18.1 6.1 %collective-permute-start.4 = (f32[180,128]{1,0:T(8,128)S(1)}, f32[180,128]{1,0:T(8,128)S(1)}, u32[]{:S(2)}, u32[]{:S(2)}) collective-permute-start(f32[180,128]{1,0:T(8,128)S(1)} %get-tuple-element.45), channel_id=1, source_target_pairs={{0,12},{1,13},{2,14},{3,15},{4,0},{5,1},{6,2},{7,3},{8,4},{9,5},{1... | collective-permute-start | bytes 276488 | tf_op jit(solution)/shard_map/ppermute | solution.py:645
  18.7 5.9 %collective-permute-start.5 = (f32[8,8,128]{2,1,0:T(8,128)S(1)}, f32[8,8,128]{2,1,0:T(8,128)S(1)}, u32[]{:S(2)}, u32[]{:S(2)}) collective-permute-start(f32[8,8,128]{2,1,0:T(8,128)S(1)} %get-tuple-element.48), channel_id=1, source_target_pairs={{0,3},{1,0},{2,1},{3,2},{4,7},{5,4},{6,5},{7,6},{8,11},{9,8},{10,9... | collective-permute-start | bytes 98312 | tf_op jit(solution)/shard_map/ppermute | solution.py:645
  19.8 4.8 %collective-permute-start.6 = (f32[8,2,128]{2,1,0:T(2,128)S(1)}, f32[8,2,128]{2,1,0:T(2,128)S(1)}, u32[]{:S(2)}, u32[]{:S(2)}) collective-permute-start(f32[8,2,128]{2,1,0:T(2,128)S(1)} %get-tuple-element.49), channel_id=1, source_target_pairs={{0,15},{1,12},{2,13},{3,14},{4,3},{5,0},{6,1},{7,2},{8,7},{9,4},{1... | collective-permute-start | bytes 24584 | tf_op jit(solution)/shard_map/ppermute | solution.py:645

commit v7 on v6

--- a/solution.py
+++ b/solution.py
@@ -174,52 +174,57 @@
     steps(0, levels + 1, gather, 4)
 
 
-def invert(m):
-    d = lambda i, j: m[AT[i, j]]
-
-    def small(a, b, c):
-        ia = 1.0 / a
-        l = b * ia
-        ic = 1.0 / (c - l * b)
-        lc = l * ic
-        return ia + l * lc, -lc, ic
-
-    a00, a01, a11 = small(d(0, 0), d(0, 1), d(1, 1))
-    t00 = d(2, 0) * a00 + d(2, 1) * a01
-    t01 = d(2, 0) * a01 + d(2, 1) * a11
-    t10 = d(3, 0) * a00 + d(3, 1) * a01
-    t11 = d(3, 0) * a01 + d(3, 1) * a11
-    s00 = d(2, 2) - (t00 * d(2, 0) + t01 * d(2, 1))
-    s01 = d(3, 2) - (t10 * d(2, 0) + t11 * d(2, 1))
-    s11 = d(3, 3) - (t10 * d(3, 0) + t11 * d(3, 1))
-    i22, i32, i33 = small(s00, s01, s11)
-    u00 = i22 * t00 + i32 * t10
-    u01 = i22 * t01 + i32 * t11
-    u10 = i32 * t00 + i33 * t10
-    u11 = i32 * t01 + i33 * t11
-    i00 = a00 + (t00 * u00 + t10 * u10)
-    i01 = a01 + (t00 * u01 + t10 * u11)
-    i11 = a11 + (t01 * u01 + t11 * u11)
-    return [i00, i01, -u00, -u10, i11, -u01, -u11, i22, i32, i33]
-
-
-def sym_product(left, right):
-    return [
-        [
-            (left[AT[i, 0]] * right[AT[0, j]] + left[AT[i, 1]] * right[AT[1, j]])
-            + (left[AT[i, 2]] * right[AT[2, j]] + left[AT[i, 3]] * right[AT[3, j]])
-            for j in range(4)
-        ]
-        for i in range(4)
-    ]
-
-
-def back_product(link, gain):
-    return [
-        (link[AT[i, 0]] * gain[0][j] + link[AT[i, 1]] * gain[1][j])
-        + (link[AT[i, 2]] * gain[2][j] + link[AT[i, 3]] * gain[3][j])
-        for i, j in PAIRS
-    ]
+def factor(m):
+    rows = {(i, j): m[AT[i, j]] for i in range(4) for j in range(i + 1)}
+    lower, inverse = {}, []
+    for p in range(4):
+        inverse.append(1.0 / rows[p, p])
+        for i in range(p + 1, 4):
+            lower[i, p] = rows[i, p] * inverse[p]
+        for i in range(p + 1, 4):
+            for j in range(p + 1, i + 1):
+                rows[i, j] = rows[i, j] - lower[i, p] * rows[j, p]
+    return lower, inverse
+
+
+def forward(lower, column):
+    out = []
+    for i in range(4):
+        value = column[i]
+        for p in range(i):
+            value = value - lower[i, p] * out[p]
+        out.append(value)
+    return out
+
+
+def backward(lower, column):
+    out = list(column)
+    for i in (2, 1, 0):
+        for p in range(3, i, -1):
+            out[i] = out[i] - lower[p, i] * out[p]
+    return out
+
+
+def dot(a, b):
+    return (a[0] * b[0] + a[1] * b[1]) + (a[2] * b[2] + a[3] * b[3])
+
+
+def reduce_block(block, value, link):
+    lower, inverse = factor(block)
+    columns = [forward(lower, [link[AT[i, j]] for i in range(4)]) for j in range(4)]
+    scaled = [[columns[j][i] * inverse[i] for i in range(4)] for j in range(4)]
+    first = forward(lower, value)
+    coupled = [dot(columns[i], scaled[j]) for i, j in PAIRS]
+    carried = [dot(scaled[i], first) for i in range(4)]
+    gain = [backward(lower, scaled[j]) for j in range(4)]
+    rest = backward(lower, [first[i] * inverse[i] for i in range(4)])
+    return [[gain[j][i] for j in range(4)] for i in range(4)], rest, coupled, carried
+
+
+def solve_block(block, value):
+    lower, inverse = factor(block)
+    first = forward(lower, value)
+    return backward(lower, [first[i] * inverse[i] for i in range(4)])
 
 
 def line_sum(values):
@@ -354,14 +359,14 @@
         block = [ps[n, k] for k in range(10)]
         link = [ms[n + 1, k] for k in range(10)]
         value = [qs[n, c] + carried[c] for c in range(4)]
-        inverse = invert([block[k] - coupled[k] for k in range(10)])
-        gain = sym_product(inverse, link)
-        rest = apply_sym(inverse, value)
+        gain, rest, coupled, carried = reduce_block(
+            [block[k] - coupled[k] for k in range(10)], value, link
+        )
         for i in range(4):
             rests[n, i] = rest[i]
             for j in range(4):
                 gains[n, 4 * i + j] = gain[i][j]
-        return back_product(link, gain), apply_sym(link, rest)
+        return coupled, carried
 
     for n in range(3):
         shift(n)
@@ -377,7 +382,10 @@
         return carry
 
     zeros = [zero() for _ in range(10)]
-    carry = lax.fori_loop(0, levels - 3, advance, (zeros, zeros[:4]))
+    carry = lax.fori_loop(
+        0, (levels - 3) // 2, lambda i, c: advance(2 * i + 1, advance(2 * i, c)), (zeros, zeros[:4])
+    )
+    carry = advance(levels - 4, carry)
     gather(levels - 1)
     gather(levels)
     carry = eliminate(levels - 3, carry)
@@ -443,13 +451,9 @@
 
     block, value = complete(here, there)
     block_there, value_there = complete(there, here)
-    inverse = invert(block_there)
-    gain = sym_product(inverse, link)
-    rest = apply_sym(inverse, value_there)
-    coupled, carried = back_product(link, gain), apply_sym(link, rest)
-    x = apply_sym(
-        invert([block[k] - coupled[k] for k in range(10)]),
-        [value[c] + carried[c] for c in range(4)],
+    gain, rest, coupled, carried = reduce_block(block_there, value_there, link)
+    x = solve_block(
+        [block[k] - coupled[k] for k in range(10)], [value[c] + carried[c] for c in range(4)]
     )
     x_met = carry_on([gain[i][j] for i in range(4) for j in range(4)], rest, x)
     x_far = carry_on([got[40 + k] for k in range(16)], [got[56 + c] for c in range(4)], x_met)

time: 25.8 us -> 25.6 us (level)
  no operation moved by 1% of the time
where the time goes in v7:
time: 25.6 us; the launch traced here: 25.5 us
  starting transfers between devices  11.9 us (46%)
  Pallas kernels  9.12 us (36%)
  waiting for transfers between devices  3.61 us (14%)
  between operations  0.74 us (3%)
    ppermute x6, starting transfers between devices, around(): return lax.ppermute(x, ('lx', 'ly'), pairs)  11.8 us
    pallas_call x9, Pallas kernels, call(): pl.pallas_call(kernel, out_shape=[jax.ShapeDtypeStruct(s, t) for s, t in...  9.12 us
    ppermute x6, waiting for transfers between devices, around(): return lax.ppermute(x, ('lx', 'ly'), pairs)  2.11 us
    ppermute x1, waiting for transfers between devices, swap(): return lax.ppermute(x, 'depth', [(0, 1), (1, 0)])  1.5 us
  transfers between devices with their start and end apart: 7, of which 2 were waited for; matrix products, arithmetic and copies ran while one was open for 0% of the time, Pallas kernels for 18%

profile of v7, /device:TPU:0, one launch (start us, length us, event | category | flops | bytes accessed | tf_op | source)
XLA Modules:
  0.0 25.5 jit_solution(4122238711535985694)
XLA Ops:
  0.6 0.0 copy-start
  0.6 1.2 %shard_map.77 = (f32[16,4,8,128]{3,2,1,0:T(8,128)S(1)}, f32[16,4,8,128]{3,2,1,0:T(8,128)S(1)}, f32[16,8,128]{2,1,0:T(8,128)S(1)}, s32[16,8,128]{2,1,0:T(8,128)S(1)}, f32[15,16,128]{2,1,0:T(8,128)S(1)}) custom-call(f32[16,4,8,128]{3,2,1,0:T(8,128)} %iterate.1, f32[16,4,8,128]{3,2,1,0:T(8,128)} %right.1, f32[16,8,128]{2,1,0:T(8,128)} %storage.1, ...), custom_call_target="tpu_custom_call" | custom-call | tf_op jit(solution)/shard_map/pallas_call | solution.py:634
  1.9 3.0 %collective-permute-start = (f32[15,16,128]{2,1,0:T(8,128)S(1)}, f32[15,16,128]{2,1,0:T(8,128)S(1)}, u32[]{:S(2)}, u32[]{:S(2)}) collective-permute-start(f32[15,16,128]{2,1,0:T(8,128)S(1)} %get-tuple-element.32), channel_id=1, source_target_pairs={{0,4},{1,5},{2,6},{3,7},{4,8},{5,9},{6,10},{7,11},{8,12},{9,13},{1... | collective-permute-start | bytes 368648 | tf_op jit(solution)/shard_map/ppermute | solution.py:649
  4.8 0.2 shard_map.80
  5.1 1.6 %collective-permute-start.1 = (f32[10,8,128]{2,1,0:T(8,128)S(1)}, f32[10,8,128]{2,1,0:T(8,128)S(1)}, u32[]{:S(2)}, u32[]{:S(2)}) collective-permute-start(f32[10,8,128]{2,1,0:T(8,128)S(1)} %get-tuple-element.35), channel_id=1, source_target_pairs={{0,1},{1,2},{2,3},{3,0},{4,5},{5,6},{6,7},{7,4},{8,9},{9,10},{10,1... | collective-permute-start | bytes 122888 | tf_op jit(solution)/shard_map/ppermute | solution.py:649
  6.7 2.5 %collective-permute-start.2 = (f32[10,2,128]{2,1,0:T(2,128)S(1)}, f32[10,2,128]{2,1,0:T(2,128)S(1)}, u32[]{:S(2)}, u32[]{:S(2)}) collective-permute-start(f32[10,2,128]{2,1,0:T(2,128)S(1)} %get-tuple-element.36), channel_id=1, source_target_pairs={{0,5},{1,6},{2,7},{3,4},{4,9},{5,10},{6,11},{7,8},{8,13},{9,14},{1... | collective-permute-start | bytes 30728 | tf_op jit(solution)/shard_map/ppermute | solution.py:649
  9.2 0.0 copy-done
  9.2 0.1 broadcast_in_dim.8.tables
  9.3 1.7 %shard_map.78 = (f32[17,19,8,128]{3,2,1,0:T(8,128)S(1)}, f32[16,10,8,128]{3,2,1,0:T(8,128)S(1)}) custom-call(f32[16,4,8,128]{3,2,1,0:T(8,128)S(1)} %get-tuple-element.26.it, f32[16,4,8,128]{3,2,1,0:T(8,128)S(1)} %get-tuple-element.27.rt, f32[16,8,128]{2,1,0:T(8,128)S(1)} %get-tuple-element.28.st, s32[16,8,128]{2,1,0:T(8,128)S(1)} %get-tuple-element.29.codes, ...), custom_call_target="tpu_custom_call" | custom-call | tf_op jit(solution)/shard_map/pallas_call | solution.py:634
  11.0 0.0 collective-permute-done.xm
  11.1 0.8 %shard_map.79 = (f32[17,19,8,128]{3,2,1,0:T(8,128)S(1)}, f32[16,10,8,128]{3,2,1,0:T(8,128)S(1)}) custom-call(f32[17,19,8,128]{3,2,1,0:T(8,128)S(1)} %get-tuple-element.30.sown, f32[16,10,8,128]{3,2,1,0:T(8,128)S(1)} %get-tuple-element.31.pre, f32[15,16,128]{2,1,0:T(8,128)S(1)} %collective-permute-done.xm, f32[32,8,128]{2,1,0:T(8,128)S(1)} %broadcast_in_dim.8.tables), custom_call_target="tpu_custom_call" | custom-call | tf_op jit(solution)/shard_map/pallas_call | solution.py:634
  11.9 2.1 %collective-permute-done.2.dm = f32[10,2,128]{2,1,0:T(2,128)S(1)} collective-permute-done((f32[10,2,128]{2,1,0:T(2,128)S(1)}, f32[10,2,128]{2,1,0:T(2,128)S(1)}, u32[]{:S(2)}, u32[]{:S(2)}) %collective-permute-start.2) | collective-permute-done | bytes 10272 | tf_op jit(solution)/shard_map/ppermute | solution.py:649
  14.0 0.0 collective-permute-done.1.ym
  14.0 1.8 %shard_map.81 = (f32[15,16,8,128]{3,2,1,0:T(8,128)S(1)}, f32[15,4,8,128]{3,2,1,0:T(8,128)S(1)}, f32[60,8,128]{2,1,0:T(8,128)S(1)}, s32[16,8,128]{2,1,0:T(8,128)S(1)}) custom-call(f32[17,19,8,128]{3,2,1,0:T(8,128)S(1)} %get-tuple-element.33.sown, f32[16,10,8,128]{3,2,1,0:T(8,128)S(1)} %get-tuple-element.34.pre, f32[10,8,128]{2,1,0:T(8,128)S(1)} %collective-permute-done.1.ym, ...), custom_call_target="tpu_custom_call" | custom-call | tf_op jit(solution)/shard_map/pallas_call | solution.py:634
  15.8 0.1 collective-permute-start.3
  15.9 1.5 %collective-permute-done.3.got = f32[60,8,128]{2,1,0:T(8,128)S(1)} collective-permute-done((f32[60,8,128]{2,1,0:T(8,128)S(1)}, f32[60,8,128]{2,1,0:T(8,128)S(1)}, u32[]{:S(2)}, u32[]{:S(2)}) %collective-permute-start.3) | collective-permute-done | bytes 245792 | tf_op jit(solution)/shard_map/ppermute | solution.py:653
  17.3 0.5 %shard_map.82 = (f32[18,4,8,128]{3,2,1,0:T(8,128)S(1)}, f32[18,4,8,128]{3,2,1,0:T(8,128)S(1)}, f32[180,128]{1,0:T(8,128)S(1)}, f32[8,8,128]{2,1,0:T(8,128)S(1)}, f32[8,2,128]{2,1,0:T(2,128)S(1)}) custom-call(f32[15,16,8,128]{3,2,1,0:T(8,128)S(1)} %get-tuple-element.37.gains, f32[15,4,8,128]{3,2,1,0:T(8,128)S(1)} %get-tuple-element.38.rests, ...), custom_call_target="tpu_custom_call" | custom-call | tf_op jit(solution)/shard_map/pallas_call | solution.py:634
  17.9 0.6 %collective-permute-start.4 = (f32[180,128]{1,0:T(8,128)S(1)}, f32[180,128]{1,0:T(8,128)S(1)}, u32[]{:S(2)}, u32[]{:S(2)}) collective-permute-start(f32[180,128]{1,0:T(8,128)S(1)} %get-tuple-element.45), channel_id=1, source_target_pairs={{0,12},{1,13},{2,14},{3,15},{4,0},{5,1},{6,2},{7,3},{8,4},{9,5},{1... | collective-permute-start | bytes 276488 | tf_op jit(solution)/shard_map/ppermute | solution.py:649
  18.5 1.1 %collective-permute-start.5 = (f32[8,8,128]{2,1,0:T(8,128)S(1)}, f32[8,8,128]{2,1,0:T(8,128)S(1)}, u32[]{:S(2)}, u32[]{:S(2)}) collective-permute-start(f32[8,8,128]{2,1,0:T(8,128)S(1)} %get-tuple-element.48), channel_id=1, source_target_pairs={{0,3},{1,0},{2,1},{3,2},{4,7},{5,4},{6,5},{7,6},{8,11},{9,8},{10,9... | collective-permute-start | bytes 98312 | tf_op jit(solution)/shard_map/ppermute | solution.py:649
  19.5 3.1 %collective-permute-start.6 = (f32[8,2,128]{2,1,0:T(2,128)S(1)}, f32[8,2,128]{2,1,0:T(2,128)S(1)}, u32[]{:S(2)}, u32[]{:S(2)}) collective-permute-start(f32[8,2,128]{2,1,0:T(2,128)S(1)} %get-tuple-element.49), channel_id=1, source_target_pairs={{0,15},{1,12},{2,13},{3,14},{4,3},{5,0},{6,1},{7,2},{8,7},{9,4},{1... | collective-permute-start | bytes 24584 | tf_op jit(solution)/shard_map/ppermute | solution.py:649
  22.6 1.3 %shard_map.83 = (f32[17,8,8,128]{3,2,1,0:T(8,128)S(1)}, f32[16,4,8,128]{3,2,1,0:T(8,128)S(1)}) custom-call(f32[18,4,8,128]{3,2,1,0:T(8,128)S(1)} %get-tuple-element.41.xs, f32[18,4,8,128]{3,2,1,0:T(8,128)S(1)} %get-tuple-element.42.kx), custom_call_target="tpu_custom_call" | custom-call | tf_op jit(solution)/shard_map/pallas_call | solution.py:634
  23.9 0.0 collective-permute-done.4.x3
  23.9 0.4 %shard_map.84 = (f32[17,8,8,128]{3,2,1,0:T(8,128)S(1)}, f32[16,4,8,128]{3,2,1,0:T(8,128)S(1)}) custom-call(f32[17,8,8,128]{3,2,1,0:T(8,128)S(1)} %get-tuple-element.43.sown, f32[16,4,8,128]{3,2,1,0:T(8,128)S(1)} %get-tuple-element.44.pre, f32[180,128]{1,0:T(8,128)S(1)} %collective-permute-done.4.x3, f32[32,8,128]{2,1,0:T(8,128)S(1)} %broadcast_in_dim.8.tables), custom_call_target="tpu_custom_call" | custom-call | tf_op jit(solution)/shard_map/pallas_call | solution.py:634
  24.4 0.0 collective-permute-done.6.d3
  24.4 0.0 collective-permute-done.5.y3
  24.4 1.1 %shard_map.85 = (f32[16,4,8,128]{3,2,1,0:T(8,128)}, f32[8,4,8,128]{3,2,1,0:T(8,128)}) custom-call(f32[17,8,8,128]{3,2,1,0:T(8,128)S(1)} %get-tuple-element.46.sown, f32[16,4,8,128]{3,2,1,0:T(8,128)S(1)} %get-tuple-element.47.pre, f32[8,8,128]{2,1,0:T(8,128)S(1)} %collective-permute-done.5.y3, f32[8,2,128]{2,1,0:T(2,128)S(1)} %collective-permute-done.6.d3, ...), custom_call_target="tpu_custom_call" | custom-call | tf_op jit(solution)/shard_map/pallas_call | solution.py:634
Async XLA Ops:
  0.6 8.6 %copy-start = (f32[2,8,4,4]{1,3,2,0:T(4,128)S(1)}, f32[2,8,4,4]{1,3,2,0:T(4,128)}, u32[]{:S(2)}) copy-start(f32[2,8,4,4]{1,3,2,0:T(4,128)} %param.11) | copy-start | bytes 3076
  1.9 9.2 %collective-permute-start = (f32[15,16,128]{2,1,0:T(8,128)S(1)}, f32[15,16,128]{2,1,0:T(8,128)S(1)}, u32[]{:S(2)}, u32[]{:S(2)}) collective-permute-start(f32[15,16,128]{2,1,0:T(8,128)S(1)} %get-tuple-element.32), channel_id=1, source_target_pairs={{0,4},{1,5},{2,6},{3,7},{4,8},{5,9},{6,10},{7,11},{8,12},{9,13},{1... | collective-permute-start | bytes 368648 | tf_op jit(solution)/shard_map/ppermute | solution.py:649
  5.1 8.9 %collective-permute-start.1 = (f32[10,8,128]{2,1,0:T(8,128)S(1)}, f32[10,8,128]{2,1,0:T(8,128)S(1)}, u32[]{:S(2)}, u32[]{:S(2)}) collective-permute-start(f32[10,8,128]{2,1,0:T(8,128)S(1)} %get-tuple-element.35), channel_id=1, source_target_pairs={{0,1},{1,2},{2,3},{3,0},{4,5},{5,6},{6,7},{7,4},{8,9},{9,10},{10,1... | collective-permute-start | bytes 122888 | tf_op jit(solution)/shard_map/ppermute | solution.py:649
  6.7 7.3 %collective-permute-start.2 = (f32[10,2,128]{2,1,0:T(2,128)S(1)}, f32[10,2,128]{2,1,0:T(2,128)S(1)}, u32[]{:S(2)}, u32[]{:S(2)}) collective-permute-start(f32[10,2,128]{2,1,0:T(2,128)S(1)} %get-tuple-element.36), channel_id=1, source_target_pairs={{0,5},{1,6},{2,7},{3,4},{4,9},{5,10},{6,11},{7,8},{8,13},{9,14},{1... | collective-permute-start | bytes 30728 | tf_op jit(solution)/shard_map/ppermute | solution.py:649
  15.8 1.6 %collective-permute-start.3 = (f32[60,8,128]{2,1,0:T(8,128)S(1)}, f32[60,8,128]{2,1,0:T(8,128)S(1)}, u32[]{:S(2)}, u32[]{:S(2)}) collective-permute-start(f32[60,8,128]{2,1,0:T(8,128)S(1)} %get-tuple-element.39.message), channel_id=1, source_target_pairs={{0,16},{16,0},{1,17},{17,1},{2,18},{18,2},{3,19},{19,3},{4,20},{20... | collective-permute-start | bytes 737288 | tf_op jit(solution)/shard_map/ppermute | solution.py:653
  17.9 6.1 %collective-permute-start.4 = (f32[180,128]{1,0:T(8,128)S(1)}, f32[180,128]{1,0:T(8,128)S(1)}, u32[]{:S(2)}, u32[]{:S(2)}) collective-permute-start(f32[180,128]{1,0:T(8,128)S(1)} %get-tuple-element.45), channel_id=1, source_target_pairs={{0,12},{1,13},{2,14},{3,15},{4,0},{5,1},{6,2},{7,3},{8,4},{9,5},{1... | collective-permute-start | bytes 276488 | tf_op jit(solution)/shard_map/ppermute | solution.py:649
  18.5 5.9 %collective-permute-start.5 = (f32[8,8,128]{2,1,0:T(8,128)S(1)}, f32[8,8,128]{2,1,0:T(8,128)S(1)}, u32[]{:S(2)}, u32[]{:S(2)}) collective-permute-start(f32[8,8,128]{2,1,0:T(8,128)S(1)} %get-tuple-element.48), channel_id=1, source_target_pairs={{0,3},{1,0},{2,1},{3,2},{4,7},{5,4},{6,5},{7,6},{8,11},{9,8},{10,9... | collective-permute-start | bytes 98312 | tf_op jit(solution)/shard_map/ppermute | solution.py:649
  19.5 4.8 %collective-permute-start.6 = (f32[8,2,128]{2,1,0:T(2,128)S(1)}, f32[8,2,128]{2,1,0:T(2,128)S(1)}, u32[]{:S(2)}, u32[]{:S(2)}) collective-permute-start(f32[8,2,128]{2,1,0:T(2,128)S(1)} %get-tuple-element.49), channel_id=1, source_target_pairs={{0,15},{1,12},{2,13},{3,14},{4,3},{5,0},{6,1},{7,2},{8,7},{9,4},{1... | collective-permute-start | bytes 24584 | tf_op jit(solution)/shard_map/ppermute | solution.py:649

commit v8 on v7

--- a/solution.py
+++ b/solution.py
@@ -162,7 +162,7 @@
         for k, value in enumerate(fields):
             pre[n, k] = roll_lanes(roll_rows(value, 1), 1)
 
-    steps(0, levels, shift, 4)
+    steps(0, levels, shift, 8)
 
     def gather(n):
         for k in range(SUMMED):
@@ -272,8 +272,8 @@
         for k in range(10):
             moved[n, k] = jnp.where(row < 1, xl[k, pl.ds(n, 1), :], pre[n, k])
 
-    steps(0, levels + 1, add, 2)
-    steps(0, levels, fill, 2)
+    steps(0, levels + 1, add, 4)
+    steps(0, levels, fill, 8)
 
 
 def sweep_kernel(
@@ -509,7 +509,7 @@
             sown[n, k] = jnp.where(lane < 127, roll_lanes(g, -1), 0.0) + (vu * roll_lanes(b, -2) + vl * b)
 
     gather(0, True)
-    steps(1, levels + 1, gather, 2)
+    steps(1, levels + 1, gather, 4)
 
     def shift(n):
         for c in range(4):

time: 25.6 us -> 25.3 us (0.988)
  Pallas kernels: 9.12 us -> 8.62 us
    pallas_call x9, Pallas kernels: 9.12 us -> 8.62 us  [call(): pl.pallas_call(kernel, out_shape=[jax.ShapeDtypeStruct(s, t) for s, t in...]
  transfers between devices with their start and end apart: 7 -> 7, of which waited for: 2 -> 2; matrix products, arithmetic and copies ran while one was open for 0% -> 0% of each run, Pallas kernels for 18% -> 16%
where the time goes in v8:
time: 25.3 us; the launch traced here: 25.1 us
  starting transfers between devices  11.9 us (47%)
  Pallas kernels  8.62 us (34%)
  waiting for transfers between devices  3.78 us (15%)
  between operations  0.74 us (3%)
    ppermute x6, starting transfers between devices, around(): return lax.ppermute(x, ('lx', 'ly'), pairs)  11.8 us
    pallas_call x9, Pallas kernels, call(): pl.pallas_call(kernel, out_shape=[jax.ShapeDtypeStruct(s, t) for s, t in...  8.62 us
    ppermute x6, waiting for transfers between devices, around(): return lax.ppermute(x, ('lx', 'ly'), pairs)  2.28 us
    ppermute x1, waiting for transfers between devices, swap(): return lax.ppermute(x, 'depth', [(0, 1), (1, 0)])  1.5 us
  transfers between devices with their start and end apart: 7, of which 2 were waited for; matrix products, arithmetic and copies ran while one was open for 0% of the time, Pallas kernels for 16%

profile of v8, /device:TPU:0, one launch (start us, length us, event | category | flops | bytes accessed | tf_op | source)
XLA Modules:
  0.0 25.1 jit_solution(4514686623089381273)
XLA Ops:
  0.6 0.0 copy-start
  0.6 1.2 %shard_map.77 = (f32[16,4,8,128]{3,2,1,0:T(8,128)S(1)}, f32[16,4,8,128]{3,2,1,0:T(8,128)S(1)}, f32[16,8,128]{2,1,0:T(8,128)S(1)}, s32[16,8,128]{2,1,0:T(8,128)S(1)}, f32[15,16,128]{2,1,0:T(8,128)S(1)}) custom-call(f32[16,4,8,128]{3,2,1,0:T(8,128)} %iterate.1, f32[16,4,8,128]{3,2,1,0:T(8,128)} %right.1, f32[16,8,128]{2,1,0:T(8,128)} %storage.1, ...), custom_call_target="tpu_custom_call" | custom-call | tf_op jit(solution)/shard_map/pallas_call | solution.py:634
  1.9 3.0 %collective-permute-start = (f32[15,16,128]{2,1,0:T(8,128)S(1)}, f32[15,16,128]{2,1,0:T(8,128)S(1)}, u32[]{:S(2)}, u32[]{:S(2)}) collective-permute-start(f32[15,16,128]{2,1,0:T(8,128)S(1)} %get-tuple-element.32), channel_id=1, source_target_pairs={{0,4},{1,5},{2,6},{3,7},{4,8},{5,9},{6,10},{7,11},{8,12},{9,13},{1... | collective-permute-start | bytes 368648 | tf_op jit(solution)/shard_map/ppermute | solution.py:649
  4.8 0.2 shard_map.80
  5.1 1.6 %collective-permute-start.1 = (f32[10,8,128]{2,1,0:T(8,128)S(1)}, f32[10,8,128]{2,1,0:T(8,128)S(1)}, u32[]{:S(2)}, u32[]{:S(2)}) collective-permute-start(f32[10,8,128]{2,1,0:T(8,128)S(1)} %get-tuple-element.35), channel_id=1, source_target_pairs={{0,1},{1,2},{2,3},{3,0},{4,5},{5,6},{6,7},{7,4},{8,9},{9,10},{10,1... | collective-permute-start | bytes 122888 | tf_op jit(solution)/shard_map/ppermute | solution.py:649
  6.7 2.5 %collective-permute-start.2 = (f32[10,2,128]{2,1,0:T(2,128)S(1)}, f32[10,2,128]{2,1,0:T(2,128)S(1)}, u32[]{:S(2)}, u32[]{:S(2)}) collective-permute-start(f32[10,2,128]{2,1,0:T(2,128)S(1)} %get-tuple-element.36), channel_id=1, source_target_pairs={{0,5},{1,6},{2,7},{3,4},{4,9},{5,10},{6,11},{7,8},{8,13},{9,14},{1... | collective-permute-start | bytes 30728 | tf_op jit(solution)/shard_map/ppermute | solution.py:649
  9.2 0.0 copy-done
  9.2 0.1 broadcast_in_dim.8.tables
  9.3 1.6 %shard_map.78 = (f32[17,19,8,128]{3,2,1,0:T(8,128)S(1)}, f32[16,10,8,128]{3,2,1,0:T(8,128)S(1)}) custom-call(f32[16,4,8,128]{3,2,1,0:T(8,128)S(1)} %get-tuple-element.26.it, f32[16,4,8,128]{3,2,1,0:T(8,128)S(1)} %get-tuple-element.27.rt, f32[16,8,128]{2,1,0:T(8,128)S(1)} %get-tuple-element.28.st, s32[16,8,128]{2,1,0:T(8,128)S(1)} %get-tuple-element.29.codes, ...), custom_call_target="tpu_custom_call" | custom-call | tf_op jit(solution)/shard_map/pallas_call | solution.py:634
  10.9 0.0 collective-permute-done.xm
  10.9 0.8 %shard_map.79 = (f32[17,19,8,128]{3,2,1,0:T(8,128)S(1)}, f32[16,10,8,128]{3,2,1,0:T(8,128)S(1)}) custom-call(f32[17,19,8,128]{3,2,1,0:T(8,128)S(1)} %get-tuple-element.30.sown, f32[16,10,8,128]{3,2,1,0:T(8,128)S(1)} %get-tuple-element.31.pre, f32[15,16,128]{2,1,0:T(8,128)S(1)} %collective-permute-done.xm, f32[32,8,128]{2,1,0:T(8,128)S(1)} %broadcast_in_dim.8.tables), custom_call_target="tpu_custom_call" | custom-call | tf_op jit(solution)/shard_map/pallas_call | solution.py:634
  11.7 2.3 %collective-permute-done.2.dm = f32[10,2,128]{2,1,0:T(2,128)S(1)} collective-permute-done((f32[10,2,128]{2,1,0:T(2,128)S(1)}, f32[10,2,128]{2,1,0:T(2,128)S(1)}, u32[]{:S(2)}, u32[]{:S(2)}) %collective-permute-start.2) | collective-permute-done | bytes 10272 | tf_op jit(solution)/shard_map/ppermute | solution.py:649
  14.0 0.0 collective-permute-done.1.ym
  14.0 1.8 %shard_map.81 = (f32[15,16,8,128]{3,2,1,0:T(8,128)S(1)}, f32[15,4,8,128]{3,2,1,0:T(8,128)S(1)}, f32[60,8,128]{2,1,0:T(8,128)S(1)}, s32[16,8,128]{2,1,0:T(8,128)S(1)}) custom-call(f32[17,19,8,128]{3,2,1,0:T(8,128)S(1)} %get-tuple-element.33.sown, f32[16,10,8,128]{3,2,1,0:T(8,128)S(1)} %get-tuple-element.34.pre, f32[10,8,128]{2,1,0:T(8,128)S(1)} %collective-permute-done.1.ym, ...), custom_call_target="tpu_custom_call" | custom-call | tf_op jit(solution)/shard_map/pallas_call | solution.py:634
  15.8 0.1 collective-permute-start.3
  15.9 1.5 %collective-permute-done.3.got = f32[60,8,128]{2,1,0:T(8,128)S(1)} collective-permute-done((f32[60,8,128]{2,1,0:T(8,128)S(1)}, f32[60,8,128]{2,1,0:T(8,128)S(1)}, u32[]{:S(2)}, u32[]{:S(2)}) %collective-permute-start.3) | collective-permute-done | bytes 245792 | tf_op jit(solution)/shard_map/ppermute | solution.py:653
  17.3 0.5 %shard_map.82 = (f32[18,4,8,128]{3,2,1,0:T(8,128)S(1)}, f32[18,4,8,128]{3,2,1,0:T(8,128)S(1)}, f32[180,128]{1,0:T(8,128)S(1)}, f32[8,8,128]{2,1,0:T(8,128)S(1)}, f32[8,2,128]{2,1,0:T(2,128)S(1)}) custom-call(f32[15,16,8,128]{3,2,1,0:T(8,128)S(1)} %get-tuple-element.37.gains, f32[15,4,8,128]{3,2,1,0:T(8,128)S(1)} %get-tuple-element.38.rests, ...), custom_call_target="tpu_custom_call" | custom-call | tf_op jit(solution)/shard_map/pallas_call | solution.py:634
  17.9 0.6 %collective-permute-start.4 = (f32[180,128]{1,0:T(8,128)S(1)}, f32[180,128]{1,0:T(8,128)S(1)}, u32[]{:S(2)}, u32[]{:S(2)}) collective-permute-start(f32[180,128]{1,0:T(8,128)S(1)} %get-tuple-element.45), channel_id=1, source_target_pairs={{0,12},{1,13},{2,14},{3,15},{4,0},{5,1},{6,2},{7,3},{8,4},{9,5},{1... | collective-permute-start | bytes 276488 | tf_op jit(solution)/shard_map/ppermute | solution.py:649
  18.5 0.9 %collective-permute-start.5 = (f32[8,8,128]{2,1,0:T(8,128)S(1)}, f32[8,8,128]{2,1,0:T(8,128)S(1)}, u32[]{:S(2)}, u32[]{:S(2)}) collective-permute-start(f32[8,8,128]{2,1,0:T(8,128)S(1)} %get-tuple-element.48), channel_id=1, source_target_pairs={{0,3},{1,0},{2,1},{3,2},{4,7},{5,4},{6,5},{7,6},{8,11},{9,8},{10,9... | collective-permute-start | bytes 98312 | tf_op jit(solution)/shard_map/ppermute | solution.py:649
  19.4 3.2 %collective-permute-start.6 = (f32[8,2,128]{2,1,0:T(2,128)S(1)}, f32[8,2,128]{2,1,0:T(2,128)S(1)}, u32[]{:S(2)}, u32[]{:S(2)}) collective-permute-start(f32[8,2,128]{2,1,0:T(2,128)S(1)} %get-tuple-element.49), channel_id=1, source_target_pairs={{0,15},{1,12},{2,13},{3,14},{4,3},{5,0},{6,1},{7,2},{8,7},{9,4},{1... | collective-permute-start | bytes 24584 | tf_op jit(solution)/shard_map/ppermute | solution.py:649
  22.6 1.0 %shard_map.83 = (f32[17,8,8,128]{3,2,1,0:T(8,128)S(1)}, f32[16,4,8,128]{3,2,1,0:T(8,128)S(1)}) custom-call(f32[18,4,8,128]{3,2,1,0:T(8,128)S(1)} %get-tuple-element.41.xs, f32[18,4,8,128]{3,2,1,0:T(8,128)S(1)} %get-tuple-element.42.kx), custom_call_target="tpu_custom_call" | custom-call | tf_op jit(solution)/shard_map/pallas_call | solution.py:634
  23.6 0.0 collective-permute-done.4.x3
  23.6 0.4 %shard_map.84 = (f32[17,8,8,128]{3,2,1,0:T(8,128)S(1)}, f32[16,4,8,128]{3,2,1,0:T(8,128)S(1)}) custom-call(f32[17,8,8,128]{3,2,1,0:T(8,128)S(1)} %get-tuple-element.43.sown, f32[16,4,8,128]{3,2,1,0:T(8,128)S(1)} %get-tuple-element.44.pre, f32[180,128]{1,0:T(8,128)S(1)} %collective-permute-done.4.x3, f32[32,8,128]{2,1,0:T(8,128)S(1)} %broadcast_in_dim.8.tables), custom_call_target="tpu_custom_call" | custom-call | tf_op jit(solution)/shard_map/pallas_call | solution.py:634
  24.0 0.0 collective-permute-done.6.d3
  24.0 0.0 collective-permute-done.5.y3
  24.0 1.1 %shard_map.85 = (f32[16,4,8,128]{3,2,1,0:T(8,128)}, f32[8,4,8,128]{3,2,1,0:T(8,128)}) custom-call(f32[17,8,8,128]{3,2,1,0:T(8,128)S(1)} %get-tuple-element.46.sown, f32[16,4,8,128]{3,2,1,0:T(8,128)S(1)} %get-tuple-element.47.pre, f32[8,8,128]{2,1,0:T(8,128)S(1)} %collective-permute-done.5.y3, f32[8,2,128]{2,1,0:T(2,128)S(1)} %collective-permute-done.6.d3, ...), custom_call_target="tpu_custom_call" | custom-call | tf_op jit(solution)/shard_map/pallas_call | solution.py:634
Async XLA Ops:
  0.6 8.6 %copy-start = (f32[2,8,4,4]{1,3,2,0:T(4,128)S(1)}, f32[2,8,4,4]{1,3,2,0:T(4,128)}, u32[]{:S(2)}) copy-start(f32[2,8,4,4]{1,3,2,0:T(4,128)} %param.11) | copy-start | bytes 3076
  1.9 9.1 %collective-permute-start = (f32[15,16,128]{2,1,0:T(8,128)S(1)}, f32[15,16,128]{2,1,0:T(8,128)S(1)}, u32[]{:S(2)}, u32[]{:S(2)}) collective-permute-start(f32[15,16,128]{2,1,0:T(8,128)S(1)} %get-tuple-element.32), channel_id=1, source_target_pairs={{0,4},{1,5},{2,6},{3,7},{4,8},{5,9},{6,10},{7,11},{8,12},{9,13},{1... | collective-permute-start | bytes 368648 | tf_op jit(solution)/shard_map/ppermute | solution.py:649
  5.1 8.9 %collective-permute-start.1 = (f32[10,8,128]{2,1,0:T(8,128)S(1)}, f32[10,8,128]{2,1,0:T(8,128)S(1)}, u32[]{:S(2)}, u32[]{:S(2)}) collective-permute-start(f32[10,8,128]{2,1,0:T(8,128)S(1)} %get-tuple-element.35), channel_id=1, source_target_pairs={{0,1},{1,2},{2,3},{3,0},{4,5},{5,6},{6,7},{7,4},{8,9},{9,10},{10,1... | collective-permute-start | bytes 122888 | tf_op jit(solution)/shard_map/ppermute | solution.py:649
  6.7 7.3 %collective-permute-start.2 = (f32[10,2,128]{2,1,0:T(2,128)S(1)}, f32[10,2,128]{2,1,0:T(2,128)S(1)}, u32[]{:S(2)}, u32[]{:S(2)}) collective-permute-start(f32[10,2,128]{2,1,0:T(2,128)S(1)} %get-tuple-element.36), channel_id=1, source_target_pairs={{0,5},{1,6},{2,7},{3,4},{4,9},{5,10},{6,11},{7,8},{8,13},{9,14},{1... | collective-permute-start | bytes 30728 | tf_op jit(solution)/shard_map/ppermute | solution.py:649
  15.8 1.6 %collective-permute-start.3 = (f32[60,8,128]{2,1,0:T(8,128)S(1)}, f32[60,8,128]{2,1,0:T(8,128)S(1)}, u32[]{:S(2)}, u32[]{:S(2)}) collective-permute-start(f32[60,8,128]{2,1,0:T(8,128)S(1)} %get-tuple-element.39.message), channel_id=1, source_target_pairs={{0,16},{16,0},{1,17},{17,1},{2,18},{18,2},{3,19},{19,3},{4,20},{20... | collective-permute-start | bytes 737288 | tf_op jit(solution)/shard_map/ppermute | solution.py:653
  17.9 5.7 %collective-permute-start.4 = (f32[180,128]{1,0:T(8,128)S(1)}, f32[180,128]{1,0:T(8,128)S(1)}, u32[]{:S(2)}, u32[]{:S(2)}) collective-permute-start(f32[180,128]{1,0:T(8,128)S(1)} %get-tuple-element.45), channel_id=1, source_target_pairs={{0,12},{1,13},{2,14},{3,15},{4,0},{5,1},{6,2},{7,3},{8,4},{9,5},{1... | collective-permute-start | bytes 276488 | tf_op jit(solution)/shard_map/ppermute | solution.py:649
  18.5 5.6 %collective-permute-start.5 = (f32[8,8,128]{2,1,0:T(8,128)S(1)}, f32[8,8,128]{2,1,0:T(8,128)S(1)}, u32[]{:S(2)}, u32[]{:S(2)}) collective-permute-start(f32[8,8,128]{2,1,0:T(8,128)S(1)} %get-tuple-element.48), channel_id=1, source_target_pairs={{0,3},{1,0},{2,1},{3,2},{4,7},{5,4},{6,5},{7,6},{8,11},{9,8},{10,9... | collective-permute-start | bytes 98312 | tf_op jit(solution)/shard_map/ppermute | solution.py:649
  19.4 4.7 %collective-permute-start.6 = (f32[8,2,128]{2,1,0:T(2,128)S(1)}, f32[8,2,128]{2,1,0:T(2,128)S(1)}, u32[]{:S(2)}, u32[]{:S(2)}) collective-permute-start(f32[8,2,128]{2,1,0:T(2,128)S(1)} %get-tuple-element.49), channel_id=1, source_target_pairs={{0,15},{1,12},{2,13},{3,14},{4,3},{5,0},{6,1},{7,2},{8,7},{9,4},{1... | collective-permute-start | bytes 24584 | tf_op jit(solution)/shard_map/ppermute | solution.py:649

commit v9 on v8

--- a/solution.py
+++ b/solution.py
@@ -153,7 +153,7 @@
         for k, value in enumerate(summed_fields(tables, codes[n], field)):
             u[n + 1, k] = value
 
-    steps(0, levels, fill, 2)
+    steps(0, levels, fill, 4)
 
     def shift(n):
         z = level_of(side, n, levels)
@@ -515,7 +515,7 @@
         for c in range(4):
             pre[n, c] = roll_lanes(roll_rows(xs[n, c], -1), -1)
 
-    steps(0, levels, shift, 4)
+    steps(0, levels, shift, 8)
 
 
 def line_back_kernel(levels, sown, pre, x3, tables, sums, moved, xw, xl):
@@ -558,8 +558,8 @@
         for c in range(4):
             moved[n, c] = jnp.where(row == 7, xl[c, pl.ds(n, 1), :], pre[n, c])
 
-    steps(0, levels + 1, add, 4)
-    steps(0, levels, fill, 4)
+    steps(0, levels + 1, add, 8)
+    steps(0, levels, fill, 8)
 
 
 def finish_kernel(

time: 25.3 us -> 25.2 us (level)
  transfers between devices with their start and end apart: 7 -> 7, of which waited for: 2 -> 3; matrix products, arithmetic and copies ran while one was open for 0% -> 0% of each run, Pallas kernels for 16% -> 15%
where the time goes in v9:
time: 25.2 us; the launch traced here: 25.1 us
  starting transfers between devices  11.9 us (47%)
  Pallas kernels  8.43 us (33%)
  waiting for transfers between devices  3.91 us (16%)
  between operations  0.74 us (3%)
    ppermute x6, starting transfers between devices, around(): return lax.ppermute(x, ('lx', 'ly'), pairs)  11.8 us
    pallas_call x9, Pallas kernels, call(): pl.pallas_call(kernel, out_shape=[jax.ShapeDtypeStruct(s, t) for s, t in...  8.43 us
    ppermute x6, waiting for transfers between devices, around(): return lax.ppermute(x, ('lx', 'ly'), pairs)  2.41 us
    ppermute x1, waiting for transfers between devices, swap(): return lax.ppermute(x, 'depth', [(0, 1), (1, 0)])  1.5 us
  transfers between devices with their start and end apart: 7, of which 3 were waited for; matrix products, arithmetic and copies ran while one was open for 0% of the time, Pallas kernels for 15%

profile of v9, /device:TPU:0, one launch (start us, length us, event | category | flops | bytes accessed | tf_op | source)
XLA Modules:
  0.0 25.1 jit_solution(8096487517795629946)
XLA Ops:
  0.6 0.0 copy-start
  0.6 1.2 %shard_map.77 = (f32[16,4,8,128]{3,2,1,0:T(8,128)S(1)}, f32[16,4,8,128]{3,2,1,0:T(8,128)S(1)}, f32[16,8,128]{2,1,0:T(8,128)S(1)}, s32[16,8,128]{2,1,0:T(8,128)S(1)}, f32[15,16,128]{2,1,0:T(8,128)S(1)}) custom-call(f32[16,4,8,128]{3,2,1,0:T(8,128)} %iterate.1, f32[16,4,8,128]{3,2,1,0:T(8,128)} %right.1, f32[16,8,128]{2,1,0:T(8,128)} %storage.1, ...), custom_call_target="tpu_custom_call" | custom-call | tf_op jit(solution)/shard_map/pallas_call | solution.py:634
  1.9 3.0 %collective-permute-start = (f32[15,16,128]{2,1,0:T(8,128)S(1)}, f32[15,16,128]{2,1,0:T(8,128)S(1)}, u32[]{:S(2)}, u32[]{:S(2)}) collective-permute-start(f32[15,16,128]{2,1,0:T(8,128)S(1)} %get-tuple-element.32), channel_id=1, source_target_pairs={{0,4},{1,5},{2,6},{3,7},{4,8},{5,9},{6,10},{7,11},{8,12},{9,13},{1... | collective-permute-start | bytes 368648 | tf_op jit(solution)/shard_map/ppermute | solution.py:649
  4.8 0.2 shard_map.80
  5.1 1.6 %collective-permute-start.1 = (f32[10,8,128]{2,1,0:T(8,128)S(1)}, f32[10,8,128]{2,1,0:T(8,128)S(1)}, u32[]{:S(2)}, u32[]{:S(2)}) collective-permute-start(f32[10,8,128]{2,1,0:T(8,128)S(1)} %get-tuple-element.35), channel_id=1, source_target_pairs={{0,1},{1,2},{2,3},{3,0},{4,5},{5,6},{6,7},{7,4},{8,9},{9,10},{10,1... | collective-permute-start | bytes 122888 | tf_op jit(solution)/shard_map/ppermute | solution.py:649
  6.7 2.5 %collective-permute-start.2 = (f32[10,2,128]{2,1,0:T(2,128)S(1)}, f32[10,2,128]{2,1,0:T(2,128)S(1)}, u32[]{:S(2)}, u32[]{:S(2)}) collective-permute-start(f32[10,2,128]{2,1,0:T(2,128)S(1)} %get-tuple-element.36), channel_id=1, source_target_pairs={{0,5},{1,6},{2,7},{3,4},{4,9},{5,10},{6,11},{7,8},{8,13},{9,14},{1... | collective-permute-start | bytes 30728 | tf_op jit(solution)/shard_map/ppermute | solution.py:649
  9.2 0.0 copy-done
  9.2 0.1 broadcast_in_dim.8.tables
  9.3 1.5 %shard_map.78 = (f32[17,19,8,128]{3,2,1,0:T(8,128)S(1)}, f32[16,10,8,128]{3,2,1,0:T(8,128)S(1)}) custom-call(f32[16,4,8,128]{3,2,1,0:T(8,128)S(1)} %get-tuple-element.26.it, f32[16,4,8,128]{3,2,1,0:T(8,128)S(1)} %get-tuple-element.27.rt, f32[16,8,128]{2,1,0:T(8,128)S(1)} %get-tuple-element.28.st, s32[16,8,128]{2,1,0:T(8,128)S(1)} %get-tuple-element.29.codes, ...), custom_call_target="tpu_custom_call" | custom-call | tf_op jit(solution)/shard_map/pallas_call | solution.py:634
  10.9 0.0 collective-permute-done.xm
  10.9 0.8 %shard_map.79 = (f32[17,19,8,128]{3,2,1,0:T(8,128)S(1)}, f32[16,10,8,128]{3,2,1,0:T(8,128)S(1)}) custom-call(f32[17,19,8,128]{3,2,1,0:T(8,128)S(1)} %get-tuple-element.30.sown, f32[16,10,8,128]{3,2,1,0:T(8,128)S(1)} %get-tuple-element.31.pre, f32[15,16,128]{2,1,0:T(8,128)S(1)} %collective-permute-done.xm, f32[32,8,128]{2,1,0:T(8,128)S(1)} %broadcast_in_dim.8.tables), custom_call_target="tpu_custom_call" | custom-call | tf_op jit(solution)/shard_map/pallas_call | solution.py:634
  11.7 2.3 %collective-permute-done.2.dm = f32[10,2,128]{2,1,0:T(2,128)S(1)} collective-permute-done((f32[10,2,128]{2,1,0:T(2,128)S(1)}, f32[10,2,128]{2,1,0:T(2,128)S(1)}, u32[]{:S(2)}, u32[]{:S(2)}) %collective-permute-start.2) | collective-permute-done | bytes 10272 | tf_op jit(solution)/shard_map/ppermute | solution.py:649
  14.0 0.0 collective-permute-done.1.ym
  14.0 1.8 %shard_map.81 = (f32[15,16,8,128]{3,2,1,0:T(8,128)S(1)}, f32[15,4,8,128]{3,2,1,0:T(8,128)S(1)}, f32[60,8,128]{2,1,0:T(8,128)S(1)}, s32[16,8,128]{2,1,0:T(8,128)S(1)}) custom-call(f32[17,19,8,128]{3,2,1,0:T(8,128)S(1)} %get-tuple-element.33.sown, f32[16,10,8,128]{3,2,1,0:T(8,128)S(1)} %get-tuple-element.34.pre, f32[10,8,128]{2,1,0:T(8,128)S(1)} %collective-permute-done.1.ym, ...), custom_call_target="tpu_custom_call" | custom-call | tf_op jit(solution)/shard_map/pallas_call | solution.py:634
  15.8 0.1 collective-permute-start.3
  15.9 1.5 %collective-permute-done.3.got = f32[60,8,128]{2,1,0:T(8,128)S(1)} collective-permute-done((f32[60,8,128]{2,1,0:T(8,128)S(1)}, f32[60,8,128]{2,1,0:T(8,128)S(1)}, u32[]{:S(2)}, u32[]{:S(2)}) %collective-permute-start.3) | collective-permute-done | bytes 245792 | tf_op jit(solution)/shard_map/ppermute | solution.py:653
  17.3 0.5 %shard_map.82 = (f32[18,4,8,128]{3,2,1,0:T(8,128)S(1)}, f32[18,4,8,128]{3,2,1,0:T(8,128)S(1)}, f32[180,128]{1,0:T(8,128)S(1)}, f32[8,8,128]{2,1,0:T(8,128)S(1)}, f32[8,2,128]{2,1,0:T(2,128)S(1)}) custom-call(f32[15,16,8,128]{3,2,1,0:T(8,128)S(1)} %get-tuple-element.37.gains, f32[15,4,8,128]{3,2,1,0:T(8,128)S(1)} %get-tuple-element.38.rests, ...), custom_call_target="tpu_custom_call" | custom-call | tf_op jit(solution)/shard_map/pallas_call | solution.py:634
  17.9 0.6 %collective-permute-start.4 = (f32[180,128]{1,0:T(8,128)S(1)}, f32[180,128]{1,0:T(8,128)S(1)}, u32[]{:S(2)}, u32[]{:S(2)}) collective-permute-start(f32[180,128]{1,0:T(8,128)S(1)} %get-tuple-element.45), channel_id=1, source_target_pairs={{0,12},{1,13},{2,14},{3,15},{4,0},{5,1},{6,2},{7,3},{8,4},{9,5},{1... | collective-permute-start | bytes 276488 | tf_op jit(solution)/shard_map/ppermute | solution.py:649
  18.5 0.9 %collective-permute-start.5 = (f32[8,8,128]{2,1,0:T(8,128)S(1)}, f32[8,8,128]{2,1,0:T(8,128)S(1)}, u32[]{:S(2)}, u32[]{:S(2)}) collective-permute-start(f32[8,8,128]{2,1,0:T(8,128)S(1)} %get-tuple-element.48), channel_id=1, source_target_pairs={{0,3},{1,0},{2,1},{3,2},{4,7},{5,4},{6,5},{7,6},{8,11},{9,8},{10,9... | collective-permute-start | bytes 98312 | tf_op jit(solution)/shard_map/ppermute | solution.py:649
  19.4 3.3 %collective-permute-start.6 = (f32[8,2,128]{2,1,0:T(2,128)S(1)}, f32[8,2,128]{2,1,0:T(2,128)S(1)}, u32[]{:S(2)}, u32[]{:S(2)}) collective-permute-start(f32[8,2,128]{2,1,0:T(2,128)S(1)} %get-tuple-element.49), channel_id=1, source_target_pairs={{0,15},{1,12},{2,13},{3,14},{4,3},{5,0},{6,1},{7,2},{8,7},{9,4},{1... | collective-permute-start | bytes 24584 | tf_op jit(solution)/shard_map/ppermute | solution.py:649
  22.6 0.9 %shard_map.83 = (f32[17,8,8,128]{3,2,1,0:T(8,128)S(1)}, f32[16,4,8,128]{3,2,1,0:T(8,128)S(1)}) custom-call(f32[18,4,8,128]{3,2,1,0:T(8,128)S(1)} %get-tuple-element.41.xs, f32[18,4,8,128]{3,2,1,0:T(8,128)S(1)} %get-tuple-element.42.kx), custom_call_target="tpu_custom_call" | custom-call | tf_op jit(solution)/shard_map/pallas_call | solution.py:634
  23.5 0.0 collective-permute-done.4.x3
  23.5 0.4 %shard_map.84 = (f32[17,8,8,128]{3,2,1,0:T(8,128)S(1)}, f32[16,4,8,128]{3,2,1,0:T(8,128)S(1)}) custom-call(f32[17,8,8,128]{3,2,1,0:T(8,128)S(1)} %get-tuple-element.43.sown, f32[16,4,8,128]{3,2,1,0:T(8,128)S(1)} %get-tuple-element.44.pre, f32[180,128]{1,0:T(8,128)S(1)} %collective-permute-done.4.x3, f32[32,8,128]{2,1,0:T(8,128)S(1)} %broadcast_in_dim.8.tables), custom_call_target="tpu_custom_call" | custom-call | tf_op jit(solution)/shard_map/pallas_call | solution.py:634
  23.9 0.1 collective-permute-done.6.d3
  24.0 0.0 collective-permute-done.5.y3
  24.0 1.1 %shard_map.85 = (f32[16,4,8,128]{3,2,1,0:T(8,128)}, f32[8,4,8,128]{3,2,1,0:T(8,128)}) custom-call(f32[17,8,8,128]{3,2,1,0:T(8,128)S(1)} %get-tuple-element.46.sown, f32[16,4,8,128]{3,2,1,0:T(8,128)S(1)} %get-tuple-element.47.pre, f32[8,8,128]{2,1,0:T(8,128)S(1)} %collective-permute-done.5.y3, f32[8,2,128]{2,1,0:T(2,128)S(1)} %collective-permute-done.6.d3, ...), custom_call_target="tpu_custom_call" | custom-call | tf_op jit(solution)/shard_map/pallas_call | solution.py:634
Async XLA Ops:
  0.6 8.6 %copy-start = (f32[2,8,4,4]{1,3,2,0:T(4,128)S(1)}, f32[2,8,4,4]{1,3,2,0:T(4,128)}, u32[]{:S(2)}) copy-start(f32[2,8,4,4]{1,3,2,0:T(4,128)} %param.11) | copy-start | bytes 3076
  1.9 9.0 %collective-permute-start = (f32[15,16,128]{2,1,0:T(8,128)S(1)}, f32[15,16,128]{2,1,0:T(8,128)S(1)}, u32[]{:S(2)}, u32[]{:S(2)}) collective-permute-start(f32[15,16,128]{2,1,0:T(8,128)S(1)} %get-tuple-element.32), channel_id=1, source_target_pairs={{0,4},{1,5},{2,6},{3,7},{4,8},{5,9},{6,10},{7,11},{8,12},{9,13},{1... | collective-permute-start | bytes 368648 | tf_op jit(solution)/shard_map/ppermute | solution.py:649
  5.1 8.9 %collective-permute-start.1 = (f32[10,8,128]{2,1,0:T(8,128)S(1)}, f32[10,8,128]{2,1,0:T(8,128)S(1)}, u32[]{:S(2)}, u32[]{:S(2)}) collective-permute-start(f32[10,8,128]{2,1,0:T(8,128)S(1)} %get-tuple-element.35), channel_id=1, source_target_pairs={{0,1},{1,2},{2,3},{3,0},{4,5},{5,6},{6,7},{7,4},{8,9},{9,10},{10,1... | collective-permute-start | bytes 122888 | tf_op jit(solution)/shard_map/ppermute | solution.py:649
  6.7 7.3 %collective-permute-start.2 = (f32[10,2,128]{2,1,0:T(2,128)S(1)}, f32[10,2,128]{2,1,0:T(2,128)S(1)}, u32[]{:S(2)}, u32[]{:S(2)}) collective-permute-start(f32[10,2,128]{2,1,0:T(2,128)S(1)} %get-tuple-element.36), channel_id=1, source_target_pairs={{0,5},{1,6},{2,7},{3,4},{4,9},{5,10},{6,11},{7,8},{8,13},{9,14},{1... | collective-permute-start | bytes 30728 | tf_op jit(solution)/shard_map/ppermute | solution.py:649
  15.8 1.6 %collective-permute-start.3 = (f32[60,8,128]{2,1,0:T(8,128)S(1)}, f32[60,8,128]{2,1,0:T(8,128)S(1)}, u32[]{:S(2)}, u32[]{:S(2)}) collective-permute-start(f32[60,8,128]{2,1,0:T(8,128)S(1)} %get-tuple-element.39.message), channel_id=1, source_target_pairs={{0,16},{16,0},{1,17},{17,1},{2,18},{18,2},{3,19},{19,3},{4,20},{20... | collective-permute-start | bytes 737288 | tf_op jit(solution)/shard_map/ppermute | solution.py:653
  17.9 5.6 %collective-permute-start.4 = (f32[180,128]{1,0:T(8,128)S(1)}, f32[180,128]{1,0:T(8,128)S(1)}, u32[]{:S(2)}, u32[]{:S(2)}) collective-permute-start(f32[180,128]{1,0:T(8,128)S(1)} %get-tuple-element.45), channel_id=1, source_target_pairs={{0,12},{1,13},{2,14},{3,15},{4,0},{5,1},{6,2},{7,3},{8,4},{9,5},{1... | collective-permute-start | bytes 276488 | tf_op jit(solution)/shard_map/ppermute | solution.py:649
  18.5 5.5 %collective-permute-start.5 = (f32[8,8,128]{2,1,0:T(8,128)S(1)}, f32[8,8,128]{2,1,0:T(8,128)S(1)}, u32[]{:S(2)}, u32[]{:S(2)}) collective-permute-start(f32[8,8,128]{2,1,0:T(8,128)S(1)} %get-tuple-element.48), channel_id=1, source_target_pairs={{0,3},{1,0},{2,1},{3,2},{4,7},{5,4},{6,5},{7,6},{8,11},{9,8},{10,9... | collective-permute-start | bytes 98312 | tf_op jit(solution)/shard_map/ppermute | solution.py:649
  19.4 4.6 %collective-permute-start.6 = (f32[8,2,128]{2,1,0:T(2,128)S(1)}, f32[8,2,128]{2,1,0:T(2,128)S(1)}, u32[]{:S(2)}, u32[]{:S(2)}) collective-permute-start(f32[8,2,128]{2,1,0:T(2,128)S(1)} %get-tuple-element.49), channel_id=1, source_target_pairs={{0,15},{1,12},{2,13},{3,14},{4,3},{5,0},{6,1},{7,2},{8,7},{9,4},{1... | collective-permute-start | bytes 24584 | tf_op jit(solution)/shard_map/ppermute | solution.py:649
